TPU v7x, 128 devices: a whole 4x4x4 slice. The times are simulated.
128 devices in a mesh: dp: 8 (over z_hi, y), seq: 16 (over z_lo, x, core).
Axes of the slice: x: 4, y: 4, z: 4 (z_hi: 2, z_lo: 2; z = z_hi * 2 + z_lo), core: 2. Of those that a mesh axis runs over, the one named last changes fastest.
Arguments:
- qkv_txt: bfloat16 [8, 512, 6144], P('dp', 'seq'), may hold values from -6 to 6
- qkv_img: bfloat16 [8, 2048, 6144], P('dp', 'seq'), may hold values from -8 to 8
- attn_img: bfloat16 [8, 2048, 2048], P('dp', 'seq'), may hold values from -6 to 6
- cot_txt: bfloat16 [8, 512, 2048], P('dp', 'seq'), may hold values from -320 to 320
- cot_img: bfloat16 [8, 2048, 3072], P('dp', 'seq'), may hold values from -320 to 320
- gate: float32 [8, 3072], P('dp'), may hold values from 0.1 to 1.9
- advantage: float32 [8], P('dp'), may hold values from -3 to 3
- proj_weight: bfloat16 [2048, 3072], replicated, may hold values from -0.125 to 0.125
Outputs:
- dqkv_txt: bfloat16 [8, 512, 6144], P('dp', 'seq')
- dqkv_img: bfloat16 [8, 2048, 6144], P('dp', 'seq')
- grad_proj: float32 [2048, 3072], P(('dp', 'seq'))
All inputs are finite; a program needn't handle non-finite values.
Results may differ from a plain program's by a relative error of at most 0.0077.
Values may be sent and summed in bfloat16 or wider, within the bound.
No kernel may reach another device: no remote copies, remote signals or barrier semaphores. Data moves between devices by JAX's collectives and lax.ppermute only.
A program may use at most 192 MiB of HBM per device.

v0:
```python
import jax
import jax.numpy as jnp
from jax import lax
from jax.sharding import PartitionSpec as P

HEAD_SIZE = 128


def sample_grads(query_rows, key_rows, value_rows, grad_rows):
    length = query_rows.shape[0]
    block = 512
    scale = HEAD_SIZE ** (-0.5)
    tail = query_rows.shape[1:]
    query_blocks = query_rows.reshape((length // block, block) + tail)
    grad_blocks = grad_rows.reshape((length // block, block) + tail)

    def block_step(running, pieces):
        key_total, value_total = running
        query_block, grad_block = pieces
        scores = (
            jnp.einsum("qhe,khe->hqk", query_block, key_rows, preferred_element_type=jnp.float32)
            * scale
        )
        shifted = jnp.exp(scores - jnp.max(scores, axis=-1, keepdims=True))
        probs = shifted / jnp.sum(shifted, axis=-1, keepdims=True)
        probs_low = probs.astype(jnp.bfloat16)
        value_total = value_total + jnp.einsum(
            "hqk,qhe->khe", probs_low, grad_block, preferred_element_type=jnp.float32
        )
        prob_grad = jnp.einsum(
            "qhe,khe->hqk", grad_block, value_rows, preferred_element_type=jnp.float32
        )
        centre = jnp.sum(probs * prob_grad, axis=-1, keepdims=True)
        score_grad = (probs * (prob_grad - centre) * scale).astype(jnp.bfloat16)
        query_grad = jnp.einsum(
            "hqk,khe->qhe", score_grad, key_rows, preferred_element_type=jnp.float32
        )
        key_total = key_total + jnp.einsum(
            "hqk,qhe->khe", score_grad, query_block, preferred_element_type=jnp.float32
        )
        return ((key_total, value_total), query_grad)

    empty = jnp.zeros(key_rows.shape, jnp.float32)
    finals, query_parts = lax.scan(block_step, (empty, empty), (query_blocks, grad_blocks))
    return (query_parts.reshape(query_rows.shape), finals[0], finals[1])


def head_grads(txt_heads, img_heads, dtxt_heads, dimg_heads):
    joint = jnp.concatenate([txt_heads, img_heads], axis=1)
    d_joint = jnp.concatenate([dtxt_heads, dimg_heads], axis=1)
    samples, length, _, local_width = joint.shape
    heads_here = local_width // HEAD_SIZE
    shape_heads = (samples, length, heads_here, HEAD_SIZE)
    query_rows = joint[:, :, 0].reshape(shape_heads)
    key_rows = joint[:, :, 1].reshape(shape_heads)
    value_rows = joint[:, :, 2].reshape(shape_heads)
    grad_rows = d_joint[:, :, 0].reshape(shape_heads)
    query_grad, key_grad, value_grad = jax.vmap(sample_grads)(
        query_rows, key_rows, value_rows, grad_rows
    )
    stacked = jnp.stack([query_grad, key_grad, value_grad], axis=2)
    stacked = stacked.reshape(samples, length, 3, local_width).astype(jnp.bfloat16)
    text_length = txt_heads.shape[1]
    return (stacked[:, :text_length], stacked[:, text_length:])


def per_device(qkv_txt, qkv_img, attn_img, cot_txt, cot_img, gate, advantage, proj_weight):
    samples = qkv_img.shape[0]
    img_local = qkv_img.shape[1]
    txt_local = qkv_txt.shape[1]
    width = attn_img.shape[2]
    model_width = cot_img.shape[2]
    weighted = advantage[:, None, None] * gate[:, None, :]
    d_image = (weighted * cot_img.astype(jnp.float32)).astype(jnp.bfloat16)
    d_out_img = jnp.einsum(
        "btd,hd->bth", d_image, proj_weight, preferred_element_type=jnp.float32
    ).astype(jnp.bfloat16)
    d_out_txt = (advantage[:, None, None] * cot_txt.astype(jnp.float32)).astype(jnp.bfloat16)
    txt_four = qkv_txt.reshape(samples, txt_local, 3, width)
    img_four = qkv_img.reshape(samples, img_local, 3, width)
    dtxt_four = d_out_txt.reshape(samples, txt_local, 1, width)
    dimg_four = d_out_img.reshape(samples, img_local, 1, width)
    txt_heads = lax.all_to_all(txt_four, "seq", split_axis=3, concat_axis=1, tiled=True)
    img_heads = lax.all_to_all(img_four, "seq", split_axis=3, concat_axis=1, tiled=True)
    dtxt_heads = lax.all_to_all(dtxt_four, "seq", split_axis=3, concat_axis=1, tiled=True)
    dimg_heads = lax.all_to_all(dimg_four, "seq", split_axis=3, concat_axis=1, tiled=True)
    grad_text, grad_image = head_grads(txt_heads, img_heads, dtxt_heads, dimg_heads)
    back_text = lax.all_to_all(grad_text, "seq", split_axis=1, concat_axis=3, tiled=True)
    back_image = lax.all_to_all(grad_image, "seq", split_axis=1, concat_axis=3, tiled=True)
    dqkv_txt = back_text.reshape(samples, txt_local, 3 * width)
    dqkv_img = back_image.reshape(samples, img_local, 3 * width)
    data_count = lax.axis_size("dp")
    seq_count = lax.axis_size("seq")
    total_tokens = samples * data_count * img_local * seq_count
    flat_attn = attn_img.reshape(samples * img_local, width)
    flat_grad = d_image.reshape(samples * img_local, model_width)
    product = lax.dot_general(
        flat_attn, flat_grad, (((0,), (0,)), ((), ())), preferred_element_type=jnp.float32
    )
    grad_proj = lax.psum_scatter(
        product / total_tokens, ("dp", "seq"), scatter_dimension=0, tiled=True
    )
    return (dqkv_txt, dqkv_img, grad_proj)


def solution(mesh):
    return jax.shard_map(
        per_device,
        mesh=mesh,
        in_specs=(
            P("dp", "seq", None),
            P("dp", "seq", None),
            P("dp", "seq", None),
            P("dp", "seq", None),
            P("dp", "seq", None),
            P("dp", None),
            P("dp"),
            P(),
        ),
        out_specs=(P("dp", "seq", None), P("dp", "seq", None), P(("dp", "seq"), None)),
        check_vma=False,
    )
```

profile of v0, /device:TPU:0, one launch (start us, length us, event | category | flops | bytes accessed | tf_op | source)
XLA Modules:
  0.0 755.8 jit_solution(1814636862926251376)
XLA Ops:
  8.7 11.3 %multiply_bitcast_fusion = f32[2048,3072]{0,1:T(8,128)} fusion(bf16[1,128,3072]{2,1,0:T(8,128)(2,1)} %param.14, f32[3072]{0:T(1024)S(1)} %bitcast.173, bf16[1,128,2048]{2,1,0:T(8,128)(2,1)S(1)} %copy-done), kind=kOutput, calls=%fused_computation.29 | convolution fusion | flops 1618083840 | bytes 26488832 | tf_op jit(solution)/shard_map/dot_general | solution.py:97
  20.0 24.7 %copy.126 = f32[2048,3072]{1,0:T(8,128)} copy(f32[2048,3072]{0,1:T(8,128)} %multiply_bitcast_fusion) | data formatting | bytes 50331648
  44.7 0.9 copy-done.12
  46.9 11.5 %reduce.7 = bf16[2048,32]{1,0:T(8,128)(2,1)S(1)} reduce(bf16[2048,1,1,32]{3,2,1,0:T(2,128)(2,1)S(1)} %bitcast.160, bf16[]{:T(256)} %broadcast.46), dimensions={1,2}, to_apply=%bitcast.112.reduce_sub_computation | reduce | bytes 262146
  58.5 1.2 reshape.139
  59.6 5.8 all-to-all-start.2
  66.1 1.5 copy.101
  67.6 2.4 reshape.135
  70.0 2.4 all-to-all-done.2
  72.5 3.7 all-to-all-start
  76.2 8.9 %fusion.23 = bf16[1,128,1,2048]{3,1,2,0:T(8,128)(2,1)S(1)} fusion(bf16[2048,3072]{1,0:T(8,128)(2,1)} %param.17, bf16[1,128,3072]{2,1,0:T(8,128)(2,1)S(1)} %copy-done.2, f32[3072]{0:T(1024)S(1)} %bitcast.174), kind=kOutput, calls=%fused_computation.33 | convolution fusion | flops 1612054528 | bytes 13905920 | tf_op jit(solution)/shard_map/btd,hd->bth/dot_general | solution.py:75
  85.9 11.5 %reduce.6 = bf16[2048,128]{1,0:T(8,128)(2,1)S(1)} reduce(bf16[2048,1,1,128]{3,2,1,0:T(2,128)(2,1)S(1)} %bitcast.161, bf16[]{:T(256)} %broadcast.46), dimensions={1,2}, to_apply=%bitcast.110.reduce_sub_computation | reduce | bytes 1048578
  97.4 0.9 reshape.137
  99.1 5.8 all-to-all-start.3
  104.8 1.9 copy.104
  106.8 10.7 %copy.105 = bf16[1,128,3,2048]{1,2,0,3:T(4,128)(2,1)} copy(bf16[1,128,3,2048]{1,3,2,0:T(8,128)(2,1)S(1)} %bitcast.155) | data formatting | bytes 3145728 | tf_op jit(solution)/shard_map/reshape | solution.py:80
  117.5 6.0 all-to-all-start.1
  124.9 2.6 reshape.136
  127.5 3.8 copy.125
  132.2 1.0 pad_maximum_fusion.1
  133.2 21.7 %all-to-all-done.1 = bf16[1,128,3,2048]{1,2,0,3:T(4,128)(2,1)} async-done(((bf16[1,128,3,2048]{1,2,0,3:T(4,128)(2,1)}), bf16[1,128,3,2048]{1,2,0,3:T(4,128)(2,1)}, u32[]{:S(2)}, u32[]{:S(2)}) %all-to-all-start.1) | async-done | bytes 1572896 | tf_op jit(solution)/shard_map/all_to_all | solution.py:84
  154.9 1.8 copy.106
  156.7 1.6 copy.107
  158.3 2.3 pad_maximum_fusion
  160.6 53.0 %while.15 = (s32[]{:T(128)}, f32[1,2560,1,128]{1,3,2,0:T(8,128)S(1)}, f32[1,2560,1,128]{1,3,2,0:T(8,128)}, bf16[5,1,512,1,128]{4,2,3,1,0:T(8,128)(2,1)}, bf16[5,...) while((s32[]{:T(128)}, ...), condition=%wide.region_4.5_spmd.clone, body=%wide.region_0.4_spmd.clone.sunk | while | flops 1701313024 | bytes 70932752 | solution.py:44
  160.6 0.9 fusion.52
  161.6 0.8 fusion.53
  162.9 2.3 fusion.55
  165.2 2.5 multiply_reduce_fusion.2
  167.7 1.7 multiply_convert_fusion.4
  169.4 0.9 fusion.56
  171.2 0.9 fusion.52
  172.1 0.8 fusion.53
  173.5 2.3 fusion.55
  175.8 2.5 multiply_reduce_fusion.2
  178.3 1.7 multiply_convert_fusion.4
  180.0 0.9 fusion.56
  181.8 0.9 fusion.52
  184.1 2.3 fusion.55
  186.4 2.5 multiply_reduce_fusion.2
  188.9 1.7 multiply_convert_fusion.4
  190.6 0.9 fusion.56
  192.4 0.9 fusion.52
  194.7 2.3 fusion.55
  197.0 2.5 multiply_reduce_fusion.2
  199.5 1.7 multiply_convert_fusion.4
  201.2 0.9 fusion.56
  203.0 0.9 fusion.52
  203.9 0.8 fusion.53
  205.3 2.3 fusion.55
  207.6 2.5 multiply_reduce_fusion.2
  210.1 1.7 multiply_convert_fusion.4
  211.8 0.9 fusion.56
  213.9 2.4 copy.117
  216.3 1.5 maximum_bitcast_fusion
  217.9 1.1 copy.118
  219.0 5.0 all-to-all-start.4
  224.1 10.7 %copy.121 = bf16[1,2048,3,128]{3,2,0,1:T(4,128)(2,1)} copy(bf16[1,2048,3,128]{3,1,2,0:T(8,128)(2,1)S(1)} %slice.25) | data formatting | bytes 3145728 | tf_op jit(solution)/shard_map/slice | solution.py:64
  235.3 5.3 all-to-all-start.5
  240.9 0.9 reshape.126
  241.8 30.8 %all-to-all-done.5 = bf16[1,2048,3,128]{3,2,0,1:T(4,128)(2,1)S(1)} async-done(((bf16[1,2048,3,128]{3,2,0,1:T(4,128)(2,1)}), bf16[1,2048,3,128]{3,2,0,1:T(4,128)(2,1)S(1)}, u32[]{:S(2)}, u32[]{:S(2)}) %all-to-all-start.5) | async-done | bytes 1572896 | tf_op jit(solution)/shard_map/all_to_all | solution.py:89
  272.6 3.0 copy.122
  275.6 3.6 reshape.127
  279.2 469.3 %reduce-scatter.4.cloned.1.call-done = f32[16,3072]{1,0:T(8,128)} async-done(((f32[2048,3072]{1,0:T(8,128)}), f32[16,3072]{1,0:T(8,128)}) %reduce-scatter.4.cloned.1.call-update) | async-done | bytes 196624
  (98 shorter events, 16.0 us)
Async XLA Ops:
  7.2 1.5 copy-start
  7.2 741.3 %reduce-scatter.4.cloned.1.call-start = ((), (), s32[]{:S(2)}) async-start(), calls=%async_computation.7 | async-start | bytes 25362432
  44.7 0.9 copy-start.12
  44.7 20.8 %copy-start.11 = (bf16[1,32,6144]{2,1,0:T(8,128)(2,1)S(1)}, bf16[1,32,6144]{2,1,0:T(8,128)(2,1)}, u32[]{:S(2)}) copy-start(bf16[1,32,6144]{2,1,0:T(8,128)(2,1)} %param.10) | copy-start | bytes 1179652
  59.6 12.8 %all-to-all-start.2 = ((bf16[16,2,2048]{2,1,0:T(2,128)(2,1)}), bf16[16,2,2048]{2,1,0:T(2,128)(2,1)S(1)}, u32[]{:S(2)}, u32[]{:S(2)}) async-start(bf16[16,2,2048]{2,1,0:T(2,128)(2,1)} %reshape.139), calls=%async_computation.2 | async-start | bytes 262144 | tf_op jit(solution)/shard_map/all_to_all | solution.py:85
  67.6 8.6 %copy-start.2 = (bf16[1,128,3072]{2,1,0:T(8,128)(2,1)S(1)}, bf16[1,128,3072]{2,1,0:T(8,128)(2,1)}, u32[]{:S(2)}) copy-start(bf16[1,128,3072]{2,1,0:T(8,128)(2,1)} %param.14) | copy-start | bytes 2359300
  72.5 25.9 %all-to-all-start = ((bf16[16,2,6144]{2,1,0:T(2,128)(2,1)}), bf16[16,2,6144]{2,1,0:T(2,128)(2,1)S(1)}, u32[]{:S(2)}, u32[]{:S(2)}) async-start(bf16[16,2,6144]{2,1,0:T(2,128)(2,1)} %reshape.135), calls=%async_computation | async-start | bytes 786432 | tf_op jit(solution)/shard_map/all_to_all | solution.py:83
  98.3 0.7 copy-start.3
  99.1 18.4 %all-to-all-start.3 = ((bf16[16,2,8192]{2,1,0:T(2,128)(2,1)}), bf16[16,2,8192]{2,1,0:T(2,128)(2,1)S(1)}, u32[]{:S(2)}, u32[]{:S(2)}) async-start(bf16[16,2,8192]{2,1,0:T(2,128)(2,1)} %reshape.137), calls=%async_computation.3 | async-start | bytes 1048576 | tf_op jit(solution)/shard_map/all_to_all | solution.py:86
  117.5 37.4 %all-to-all-start.1 = ((bf16[1,128,3,2048]{1,2,0,3:T(4,128)(2,1)}), bf16[1,128,3,2048]{1,2,0,3:T(4,128)(2,1)}, u32[]{:S(2)}, u32[]{:S(2)}) async-start(bf16[1,128,3,2048]{1,2,0,3:T(4,128)(2,1)} %copy.105), calls=%async_computation.1 | async-start | bytes 4194304 | tf_op jit(solution)/shard_map/all_to_all | solution.py:84
  123.5 1.4 copy-start.4
  156.7 1.6 copy-start.5
  161.5 1.3 copy-start.6
  162.9 2.3 copy-start.8
  165.2 2.5 copy-start.7
  167.7 1.7 copy-start.9
  170.3 0.9 copy-start.10
  172.1 1.3 copy-start.6
  173.5 2.3 copy-start.8
  175.8 2.5 copy-start.7
  178.3 1.7 copy-start.9
  180.9 0.9 copy-start.10
  182.7 1.3 copy-start.6
  184.1 2.3 copy-start.8
  186.4 2.5 copy-start.7
  188.9 1.7 copy-start.9
  191.5 0.9 copy-start.10
  193.3 1.3 copy-start.6
  194.7 2.3 copy-start.8
  197.0 2.5 copy-start.7
  199.5 1.7 copy-start.9
  202.1 0.9 copy-start.10
  203.9 1.3 copy-start.6
  205.3 2.3 copy-start.8
  207.6 2.5 copy-start.7
  210.1 1.7 copy-start.9
  212.7 0.9 copy-start.10
  219.0 16.3 %all-to-all-start.4 = ((bf16[1,512,3,128]{3,2,0,1:T(4,128)(2,1)}), bf16[1,512,3,128]{3,2,0,1:T(4,128)(2,1)S(1)}, u32[]{:S(2)}, u32[]{:S(2)}) async-start(bf16[1,512,3,128]{3,2,0,1:T(4,128)(2,1)} %copy.118), calls=%async_computation.4 | async-start | bytes 1048576 | tf_op jit(solution)/shard_map/all_to_all | solution.py:88
  235.3 37.3 %all-to-all-start.5 = ((bf16[1,2048,3,128]{3,2,0,1:T(4,128)(2,1)}), bf16[1,2048,3,128]{3,2,0,1:T(4,128)(2,1)S(1)}, u32[]{:S(2)}, u32[]{:S(2)}) async-start(bf16[1,2048,3,128]{3,2,0,1:T(4,128)(2,1)} %copy.121), calls=%async_computation.5 | async-start | bytes 4194304 | tf_op jit(solution)/shard_map/all_to_all | solution.py:89
  272.6 475.9 %copy-start.1 = (bf16[1,128,2048]{2,1,0:T(8,128)(2,1)S(1)}, bf16[1,128,2048]{2,1,0:T(8,128)(2,1)}, u32[]{:S(2)}) copy-start(bf16[1,128,2048]{2,1,0:T(8,128)(2,1)} %param.12) | copy-start | bytes 1572868
Sparse Core Ops, SparseCore 0:
  44.8 703.6 reduce-scatter.3
where the time goes:
time: 765 us; the launch traced here: 756 us
  waiting for transfers between devices  525 us (69%)
  local copies, waits for them, and re-layouts  85.5 us (11%)
  matrix products  56.6 us (7%)
  other arithmetic  41.4 us (5%)
  starting transfers between devices  31.7 us (4%)
  between operations  15.5 us (2%)
    unnamed x2, waiting for transfers between devices  469 us
    unnamed x27, local copies, waits for them, and re-layouts  37.3 us
    all_to_all x1, waiting for transfers between devices, per_device(): lax.all_to_all(grad_image, 'seq', split_axis=1, concat_axis=3, tiled=True)  30.8 us
    unnamed x4, other arithmetic  23 us
    all_to_all x1, waiting for transfers between devices, per_device(): lax.all_to_all(img_four, 'seq', split_axis=3, concat_axis=1, tiled=True)  21.7 us
  transfers between devices with their start and end apart: 7, of which 5 were waited for; matrix products, arithmetic and copies ran while one was open for 19% of the time, Pallas kernels for 0%

commit v1 on v0

v1 whole, which is shorter than its diff:
```python
import functools

import jax
import jax.numpy as jnp
from jax import lax
from jax.experimental import pallas as pl
from jax.experimental.pallas import tpu as pltpu
from jax.sharding import Mesh, PartitionSpec as P

HEAD_SIZE = 128
SCALE = HEAD_SIZE ** (-0.5)
LOG2E = 1.4426950408889634
BLOCK = 256
SEQ = ("zl", "x", "c")
PLANE = ("zh", "zl", "x")
COLUMN = ("y", "c")
BF16 = jnp.bfloat16
F32 = jnp.float32


def exchange(array, axes):
    return lax.all_to_all(array, axes, split_axis=0, concat_axis=0, tiled=True)


def params(mib):
    return pltpu.CompilerParams(vmem_limit_bytes=mib << 20)


def cost(flops, nbytes, exps=0):
    return pl.CostEstimate(flops=flops, bytes_accessed=nbytes, transcendentals=exps)


def pack_kernel(slots, *refs):
    out = refs[-1]
    txt, img = refs[:slots], refs[slots : 2 * slots]
    heads = out.shape[0]
    t = txt[0].shape[0]
    for j in range(slots):
        lanes = slice(j * HEAD_SIZE, (j + 1) * HEAD_SIZE)
        for h in range(heads):
            cols = slice(h * HEAD_SIZE, (h + 1) * HEAD_SIZE)
            out[h, :t, lanes] = txt[j][:, cols]
            out[h, t:, lanes] = img[j][:, cols]


def pack_heads(txt, img, first, slots, heads, step=4):
    t, i = txt.shape[0], img.shape[0]
    per = heads // step

    def spec(rows, j):
        return pl.BlockSpec((rows, step * HEAD_SIZE), lambda g: (0, (first + j) * per + g))

    nbytes = 2 * (t + i) * slots * heads * HEAD_SIZE * 2
    return pl.pallas_call(
        functools.partial(pack_kernel, slots),
        grid=(per,),
        in_specs=[spec(t, j) for j in range(slots)] + [spec(i, j) for j in range(slots)],
        out_specs=pl.BlockSpec((step, t + i, slots * HEAD_SIZE), lambda g: (g, 0, 0)),
        out_shape=jax.ShapeDtypeStruct((heads, t + i, slots * HEAD_SIZE), BF16),
        compiler_params=params(32),
        cost_estimate=cost(0, nbytes),
    )(*([txt] * slots), *([img] * slots))


def d_image_kernel(cot, gate, adv, out):
    weighted = adv[0, 0] * gate[...]
    value = (weighted * cot[...].astype(F32)).astype(BF16)
    groups, _, width = out.shape
    for g in range(groups):
        out[g] = value[:, g * width : (g + 1) * width]


def d_image_call(cot, gate, adv, groups):
    rows, width = cot.shape
    return pl.pallas_call(
        d_image_kernel,
        in_specs=[
            pl.BlockSpec(memory_space=pltpu.VMEM),
            pl.BlockSpec(memory_space=pltpu.VMEM),
            pl.BlockSpec(memory_space=pltpu.SMEM),
        ],
        out_specs=pl.BlockSpec(memory_space=pltpu.VMEM),
        out_shape=jax.ShapeDtypeStruct((groups, rows, width // groups), BF16),
        compiler_params=params(32),
        cost_estimate=cost(2 * rows * width, 4 * rows * width),
    )(cot, gate, adv)


def d_out_kernel(dimg, weight, cot_txt, adv, vt, vi, out):
    groups, rows, part = dimg.shape
    heads = out.shape[0]
    t = cot_txt.shape[0]
    total = jnp.zeros((rows, heads * HEAD_SIZE), F32)
    for g in range(groups):
        total += lax.dot_general(
            dimg[g],
            weight[:, g * part : (g + 1) * part],
            (((1,), (1,)), ((), ())),
            preferred_element_type=F32,
        )
    total = total.astype(BF16)
    text = (adv[0, 0] * cot_txt[...].astype(F32)).astype(BF16)
    for h in range(heads):
        cols = slice(h * HEAD_SIZE, (h + 1) * HEAD_SIZE)
        out[h, :t, :HEAD_SIZE] = vt[:, cols]
        out[h, t:, :HEAD_SIZE] = vi[:, cols]
        out[h, :t, HEAD_SIZE:] = text[:, cols]
        out[h, t:, HEAD_SIZE:] = total[:, cols]


def d_out_call(dimg, weight, cot_txt, adv, txt, img, heads, step=4):
    groups, rows, part = dimg.shape
    t = cot_txt.shape[0]
    width = step * HEAD_SIZE
    per = heads // step
    return pl.pallas_call(
        d_out_kernel,
        grid=(per,),
        in_specs=[
            pl.BlockSpec((groups, rows, part), lambda g: (0, 0, 0)),
            pl.BlockSpec((width, groups * part), lambda g: (g, 0)),
            pl.BlockSpec((t, width), lambda g: (0, g)),
            pl.BlockSpec(memory_space=pltpu.SMEM),
            pl.BlockSpec((t, width), lambda g: (0, 2 * per + g)),
            pl.BlockSpec((rows, width), lambda g: (0, 2 * per + g)),
        ],
        out_specs=pl.BlockSpec((step, t + rows, 2 * HEAD_SIZE), lambda g: (g, 0, 0)),
        out_shape=jax.ShapeDtypeStruct((heads, t + rows, 2 * HEAD_SIZE), BF16),
        compiler_params=params(40),
        cost_estimate=cost(
            2 * rows * weight.size, 2 * (weight.size + dimg.size + 3 * (t + rows) * heads * HEAD_SIZE)
        ),
    )(dimg, weight, cot_txt, adv, txt, img)


def exps_kernel(q, k, e_out, inv_out):
    scores = lax.dot_general(k[...], q[...], (((1,), (1,)), ((), ())), preferred_element_type=F32)
    top = jnp.max(scores, axis=0, keepdims=True)
    low = jnp.exp2((scores - top) * (SCALE * LOG2E)).astype(BF16)
    e_out[...] = low
    inverse = 1.0 / jnp.sum(low.astype(F32), axis=0, keepdims=True)
    inv_out[...] = jnp.transpose(jnp.broadcast_to(inverse, (HEAD_SIZE, inverse.shape[1])))


def exps_call(qk):
    n = qk.shape[0]
    return pl.pallas_call(
        exps_kernel,
        grid=(n // BLOCK,),
        in_specs=[
            pl.BlockSpec((BLOCK, HEAD_SIZE), lambda i: (i, 0)),
            pl.BlockSpec((n, HEAD_SIZE), lambda i: (0, 1)),
        ],
        out_specs=[
            pl.BlockSpec((n, BLOCK), lambda i: (0, i)),
            pl.BlockSpec((BLOCK, HEAD_SIZE), lambda i: (i, 0)),
        ],
        out_shape=[
            jax.ShapeDtypeStruct((n, n), BF16),
            jax.ShapeDtypeStruct((n, HEAD_SIZE), F32),
        ],
        compiler_params=params(56),
        cost_estimate=cost(2 * n * n * HEAD_SIZE * 2, 2 * n * n, n * n),
    )(qk, qk)


def grads_kernel(e, inv, q, k, v, d, out, dk, dv):
    step = pl.program_id(0)

    @pl.when(step == 0)
    def _():
        dk[...] = jnp.zeros_like(dk)
        dv[...] = jnp.zeros_like(dv)

    inverse = inv[...]
    d_low = (d[...].astype(F32) * inverse).astype(BF16)
    probs = e[...]
    prob_grad = lax.dot_general(v[...], d_low, (((1,), (1,)), ((), ())), preferred_element_type=F32)
    wide = probs.astype(F32)
    row = jnp.transpose(inverse)[:1]
    centre = jnp.sum(wide * prob_grad, axis=0, keepdims=True) * row
    score_grad = (wide * (prob_grad - centre)).astype(BF16)
    dv[...] += jnp.dot(probs, d_low, preferred_element_type=F32)
    dk[...] += jnp.dot(score_grad, q[...], preferred_element_type=F32)
    dq = lax.dot_general(score_grad, k[...], (((0,), (0,)), ((), ())), preferred_element_type=F32)
    rows = pl.ds(pl.multiple_of(step * BLOCK, BLOCK), BLOCK)
    out[rows, :HEAD_SIZE] = (dq * SCALE).astype(BF16)

    @pl.when(step == pl.num_programs(0) - 1)
    def _():
        out[:, HEAD_SIZE : 2 * HEAD_SIZE] = (dk[...] * SCALE).astype(BF16)
        out[:, 2 * HEAD_SIZE :] = dv[...].astype(BF16)


def grads_call(exps, inverse, qk, vd):
    n = qk.shape[0]
    block = lambda col: pl.BlockSpec((BLOCK, HEAD_SIZE), lambda i: (i, col))
    whole = lambda col: pl.BlockSpec((n, HEAD_SIZE), lambda i: (0, col))
    return pl.pallas_call(
        grads_kernel,
        grid=(n // BLOCK,),
        in_specs=[pl.BlockSpec((n, BLOCK), lambda i: (0, i)), block(0), block(0), whole(1), whole(0), block(1)],
        out_specs=pl.BlockSpec((n, 3 * HEAD_SIZE), lambda i: (0, 0)),
        out_shape=jax.ShapeDtypeStruct((n, 3 * HEAD_SIZE), BF16),
        scratch_shapes=[pltpu.VMEM((n, HEAD_SIZE), F32), pltpu.VMEM((n, HEAD_SIZE), F32)],
        compiler_params=params(56),
        cost_estimate=cost(2 * n * n * HEAD_SIZE * 8, 2 * n * n),
    )(exps, inverse, qk, qk, vd, vd)


def unpack_kernel(back, txt, img):
    t = txt.shape[0]
    for h in range(back.shape[0]):
        cols = slice(h * HEAD_SIZE, (h + 1) * HEAD_SIZE)
        txt[:, cols] = back[h, :t]
        img[:, cols] = back[h, t:]


def unpack_call(back, t):
    heads, tokens, _ = back.shape
    width = heads * HEAD_SIZE
    i = tokens - t
    return pl.pallas_call(
        unpack_kernel,
        grid=(3,),
        in_specs=[pl.BlockSpec((heads, tokens, HEAD_SIZE), lambda j: (0, 0, j))],
        out_specs=[
            pl.BlockSpec((t, width), lambda j: (0, j)),
            pl.BlockSpec((i, width), lambda j: (0, j)),
        ],
        out_shape=[
            jax.ShapeDtypeStruct((t, 3 * width), BF16),
            jax.ShapeDtypeStruct((i, 3 * width), BF16),
        ],
        compiler_params=params(32),
        cost_estimate=cost(0, 12 * tokens * width),
    )(back)


def per_device(qkv_txt, qkv_img, attn_img, cot_txt, cot_img, gate, advantage, proj_weight):
    txt, img = qkv_txt[0], qkv_img[0]
    tokens = txt.shape[0] + img.shape[0]
    width = attn_img.shape[2]
    heads = width // HEAD_SIZE
    model = cot_img.shape[2]
    adv = advantage[:, None]
    column = 1
    for name in COLUMN:
        column *= lax.axis_size(name)
    plane = 1
    for name in PLANE:
        plane *= lax.axis_size(name)

    attn = lax.all_gather(attn_img[0], COLUMN, axis=0, tiled=True)
    qk = exchange(pack_heads(txt, img, 0, 2, heads), SEQ)
    d_image = d_image_call(cot_img[0], gate, adv, column)
    vd = exchange(d_out_call(d_image, proj_weight, cot_txt[0], adv, txt, img, heads), SEQ)
    d_columns = exchange(d_image, COLUMN)

    n = heads * tokens
    qk = qk.reshape(n, 2 * HEAD_SIZE)
    vd = vd.reshape(n, 2 * HEAD_SIZE)
    exps, inverse = exps_call(qk)

    d_columns = d_columns.reshape(-1, model // column)
    product = lax.dot_general(attn, d_columns, (((0,), (0,)), ((), ())), preferred_element_type=F32)
    sizes = [lax.axis_size(name) for name in ("zh", "y", "zl", "x", "c")]
    rows = width // (column * plane)
    product = product.astype(BF16).reshape(*sizes, rows, model // column)
    product = jnp.transpose(product, (0, 2, 3, 1, 4, 5, 6)).reshape(plane, column * rows, model // column)
    product = exchange(product, PLANE)
    total = jnp.sum(product.astype(F32), axis=0) * (1.0 / (img.shape[0] * column * plane))
    total = exchange(total.reshape(column, rows, model // column), COLUMN)
    grad_proj = jnp.transpose(total, (1, 0, 2)).reshape(rows, model)

    grads = grads_call(exps, inverse, qk, vd).reshape(heads, tokens, 3 * HEAD_SIZE)
    dqkv_txt, dqkv_img = unpack_call(exchange(grads, SEQ), txt.shape[0])
    return (dqkv_txt[None], dqkv_img[None], grad_proj)


def solution(mesh):
    fine = Mesh(mesh.devices.reshape(2, 4, 2, 4, 2), ("zh", "y", "zl", "x", "c"))
    dp = ("zh", "y")
    tokens = P(dp, SEQ, None)
    return jax.shard_map(
        per_device,
        mesh=fine,
        in_specs=(tokens, tokens, tokens, tokens, tokens, P(dp, None), P(dp), P()),
        out_specs=(tokens, tokens, P(dp + SEQ, None)),
        check_vma=False,
    )
```

time: 765 us -> 181 us (0.24)
  the two profiles are of different devices: /device:TPU:0 before, /device:TPU:2 now
where the time goes in v1:
time: 181 us; the launch traced here: 180 us
  waiting for transfers between devices  65.1 us (36%)
  Pallas kernels  54.9 us (30%)
  starting transfers between devices  34.9 us (19%)
  between operations  14.8 us (8%)
  local copies, waits for them, and re-layouts  5.69 us (3%)
  matrix products  4.01 us (2%)
    all_to_all x6, waiting for transfers between devices, exchange(): return lax.all_to_all(array, axes, split_axis=0, concat_axis=0, tiled=True)  64.4 us
    all_to_all x6, starting transfers between devices, exchange(): return lax.all_to_all(array, axes, split_axis=0, concat_axis=0, tiled=True)  34.8 us
    pallas_call x1, Pallas kernels, grads_call(): pl.pallas_call(grads_kernel, grid=(n // BLOCK,), in_specs=[pl.BlockSpec((...  23.3 us
    pallas_call x1, Pallas kernels, exps_call(): pl.pallas_call(exps_kernel, grid=(n // BLOCK,), in_specs=[pl.BlockSpec((B...  17.9 us
    pallas_call x1, Pallas kernels, d_out_call(): pl.pallas_call(d_out_kernel, grid=(per,), in_specs=[pl.BlockSpec((groups,...  8.67 us
    dot_general x1, matrix products, per_device(): lax.dot_general(attn, d_columns, (((0,), (0,)), ((), ())), preferred_elem...  4.01 us
  transfers between devices with their start and end apart: 7, of which 5 were waited for; matrix products, arithmetic and copies ran while one was open for 4% of the time, Pallas kernels for 30%

profile of v1, /device:TPU:2, one launch (start us, length us, event | category | flops | bytes accessed | tf_op | source)
XLA Modules:
  0.0 180.2 jit_solution(9363693492729845188)
XLA Ops:
  7.2 0.0 all-gather.3.cloned.1.call-start
  7.2 0.7 all-gather.3.cloned.1.call-update
  8.5 0.0 copy-start.2
  8.6 1.1 copy-done.2
  9.7 0.0 copy-start.4
  9.7 0.7 copy-done.4
  10.4 0.0 copy-start
  10.4 0.0 copy-start.1
  10.4 0.0 copy-start.3
  10.4 1.0 shard_map.105.dimg
  11.4 4.5 %all-to-all-start.3 = ((bf16[8,128,384]{2,1,0:T(8,128)(2,1)}), bf16[8,128,384]{2,1,0:T(8,128)(2,1)S(1)}, u32[]{:S(2)}, u32[]{:S(2)}) async-start(bf16[8,128,384]{2,1,0:T(8,128)(2,1)} %shard_map.105.dimg), calls=%async_computation.3 | async-start | bytes 1572864 | tf_op jit(solution)/shard_map/all_to_all | solution.py:22
  15.9 0.0 copy-done
  15.9 0.0 copy-done.1
  15.9 0.0 copy-done.3
  15.9 8.7 %shard_map.106 = bf16[16,160,256]{2,1,0:T(8,128)(2,1)} custom-call(bf16[8,128,384]{2,1,0:T(8,128)(2,1)} %shard_map.105.dimg, bf16[2048,3072]{1,0:T(8,128)(2,1)} %weight.1, bf16[32,2048]{1,0:T(8,128)(2,1)S(1)} %bitcast.38, f32[1,1]{1,0:T(1,128)} %bitcast.30.adv, bf16[32,6144]{1,0:T(8,128)(2,1)S(1)} %bitcast.34, bf16[128,6144]{1,0:T(8,128)(2,1)S(1)} %bitcast.31), custom_call_target="tpu_custom_call" | custom-call | flops 1610612736 | bytes 15335424 | tf_op jit(solution)/shard_map/pallas_call | solution.py:116
  24.6 7.9 %all-to-all-done.3 = bf16[8,128,384]{2,1,0:T(8,128)(2,1)S(1)} async-done(((bf16[8,128,384]{2,1,0:T(8,128)(2,1)}), bf16[8,128,384]{2,1,0:T(8,128)(2,1)S(1)}, u32[]{:S(2)}, u32[]{:S(2)}) %all-to-all-start.3) | async-done | bytes 786464 | tf_op jit(solution)/shard_map/all_to_all | solution.py:22
  32.4 0.0 copy-start.6
  32.4 0.9 copy-done.6
  33.3 6.6 %all-to-all-start.1 = ((bf16[16,160,256]{2,1,0:T(8,128)(2,1)}), bf16[16,160,256]{2,1,0:T(8,128)(2,1)S(1)}, u32[]{:S(2)}, u32[]{:S(2)}) async-start(bf16[16,160,256]{2,1,0:T(8,128)(2,1)} %shard_map.106), calls=%async_computation.1 | async-start | bytes 2621440 | tf_op jit(solution)/shard_map/all_to_all | solution.py:22
  39.9 1.8 %shard_map.103 = bf16[16,160,256]{2,1,0:T(8,128)(2,1)} custom-call(bf16[32,6144]{1,0:T(8,128)(2,1)S(1)} %bitcast.35, bf16[32,6144]{1,0:T(8,128)(2,1)S(1)} %bitcast.36, bf16[128,6144]{1,0:T(8,128)(2,1)S(1)} %bitcast.32, bf16[128,6144]{1,0:T(8,128)(2,1)S(1)} %bitcast.33), custom_call_target="tpu_custom_call" | custom-call | bytes 2621440 | tf_op jit(solution)/shard_map/pallas_call | solution.py:54
  41.7 0.0 copy-start.7
  41.7 15.3 %all-to-all-done.1 = bf16[16,160,256]{2,1,0:T(8,128)(2,1)S(1)} async-done(((bf16[16,160,256]{2,1,0:T(8,128)(2,1)}), bf16[16,160,256]{2,1,0:T(8,128)(2,1)S(1)}, u32[]{:S(2)}, u32[]{:S(2)}) %all-to-all-start.1) | async-done | bytes 1310752 | tf_op jit(solution)/shard_map/all_to_all | solution.py:22
  57.1 0.0 copy-start.5
  57.1 6.4 %all-to-all-start = ((bf16[16,160,256]{2,1,0:T(8,128)(2,1)}), bf16[16,160,256]{2,1,0:T(8,128)(2,1)}, u32[]{:S(2)}, u32[]{:S(2)}) async-start(bf16[16,160,256]{2,1,0:T(8,128)(2,1)} %shard_map.103), calls=%async_computation | async-start | bytes 2621440 | tf_op jit(solution)/shard_map/all_to_all | solution.py:22
  63.4 0.0 all-gather.3.cloned.1.call-done
  63.4 0.0 copy-done.5
  63.5 0.0 copy-done.7
  63.5 4.0 %fusion.5 = bf16[2048,384]{0,1:T(8,128)(2,1)S(1)} fusion(bf16[1024,384]{1,0:T(8,128)(2,1)S(1)} %bitcast.43, bf16[1,1024,2048]{2,1,0:T(8,128)(2,1)} %all-gather.3.cloned.1.call-done), kind=kOutput, calls=%fused_computation.4 | convolution fusion | flops 1611399168 | bytes 6553600 | tf_op jit(solution)/shard_map/dot_general | solution.py:266
  67.5 0.9 copy.13
  68.4 1.4 copy.14
  69.8 10.7 %all-to-all-done = bf16[16,160,256]{2,1,0:T(8,128)(2,1)} async-done(((bf16[16,160,256]{2,1,0:T(8,128)(2,1)}), bf16[16,160,256]{2,1,0:T(8,128)(2,1)}, u32[]{:S(2)}, u32[]{:S(2)}) %all-to-all-start) | async-done | bytes 1310752 | tf_op jit(solution)/shard_map/all_to_all | solution.py:22
  80.4 8.3 %all-to-all-start.4 = ((bf16[16,128,384]{2,1,0:T(8,128)(2,1)}), bf16[16,128,384]{2,1,0:T(8,128)(2,1)S(1)}, u32[]{:S(2)}, u32[]{:S(2)}) async-start(bf16[16,128,384]{2,1,0:T(8,128)(2,1)} %bitcast.15), calls=%async_computation.4 | async-start | bytes 3145728 | tf_op jit(solution)/shard_map/all_to_all | solution.py:22
  88.7 17.9 %shard_map.104 = (bf16[2560,2560]{1,0:T(8,128)(2,1)}, f32[2560,128]{1,0:T(8,128)}) custom-call(bf16[2560,256]{1,0:T(8,128)(2,1)} %bitcast.2.q.k, bf16[2560,256]{1,0:T(8,128)(2,1)} %bitcast.2.q.k), custom_call_target="tpu_custom_call" | custom-call | flops 3355443200 | bytes 13107200 | tf_op jit(solution)/shard_map/pallas_call | solution.py:147
  106.6 23.3 %shard_map.107 = bf16[2560,384]{1,0:T(8,128)(2,1)} custom-call(bf16[2560,2560]{1,0:T(8,128)(2,1)} %get-tuple-element.7.e, f32[2560,128]{1,0:T(8,128)} %get-tuple-element.8.inv, bf16[2560,256]{1,0:T(8,128)(2,1)} %bitcast.2.q.k, bf16[2560,256]{1,0:T(8,128)(2,1)} %bitcast.2.q.k, bf16[2560,256]{1,0:T(8,128)(2,1)} %bitcast.41, bf16[2560,256]{1,0:T(8,128)(2,1)} %bitcast.42), custom_call_target="tpu_custom_call" | custom-call | flops 13421772800 | bytes 13107200 | tf_op jit(solution)/shard_map/pallas_call | solution.py:199
  129.9 0.0 all-to-all-done.4
  129.9 5.7 %all-to-all-start.2 = ((bf16[16,160,384]{2,1,0:T(8,128)(2,1)}), bf16[16,160,384]{2,1,0:T(8,128)(2,1)S(1)}, u32[]{:S(2)}, u32[]{:S(2)}) async-start(bf16[16,160,384]{2,1,0:T(8,128)(2,1)} %bitcast.40), calls=%async_computation.2 | async-start | bytes 3932160 | tf_op jit(solution)/shard_map/all_to_all | solution.py:22
  135.6 0.2 convert_reduce_fusion
  135.8 0.7 broadcast_multiply_fusion
  136.5 26.1 %all-to-all-done.2.back = bf16[16,160,384]{2,1,0:T(8,128)(2,1)S(1)} async-done(((bf16[16,160,384]{2,1,0:T(8,128)(2,1)}), bf16[16,160,384]{2,1,0:T(8,128)(2,1)S(1)}, u32[]{:S(2)}, u32[]{:S(2)}) %all-to-all-start.2) | async-done | bytes 1966112 | tf_op jit(solution)/shard_map/all_to_all | solution.py:22
  162.5 3.4 %all-to-all-start.5 = ((f32[8,16,384]{2,1,0:T(8,128)}), f32[8,16,384]{2,1,0:T(8,128)S(1)}, u32[]{:S(2)}, u32[]{:S(2)}) async-start(f32[8,16,384]{2,1,0:T(8,128)} %bitcast.16), calls=%async_computation.5 | async-start | bytes 393216 | tf_op jit(solution)/shard_map/all_to_all | solution.py:22
  165.9 2.3 %shard_map.108 = (bf16[32,6144]{1,0:T(8,128)(2,1)}, bf16[128,6144]{1,0:T(8,128)(2,1)}) custom-call(bf16[16,160,384]{2,1,0:T(8,128)(2,1)S(1)} %all-to-all-done.2.back), custom_call_target="tpu_custom_call" | custom-call | bytes 3932160 | tf_op jit(solution)/shard_map/pallas_call | solution.py:223
  168.2 4.5 %all-to-all-done.5 = f32[8,16,384]{2,1,0:T(8,128)S(1)} async-done(((f32[8,16,384]{2,1,0:T(8,128)}), f32[8,16,384]{2,1,0:T(8,128)S(1)}, u32[]{:S(2)}, u32[]{:S(2)}) %all-to-all-start.5) | async-done | bytes 196640 | tf_op jit(solution)/shard_map/all_to_all | solution.py:22
  172.7 0.7 copy.16
Async XLA Ops:
  7.2 56.3 %all-gather.3.cloned.1.call-start = ((), (), s32[]{:S(2)}) async-start(), calls=%async_computation.6 | async-start | bytes 4718592 | tf_op jit(solution)/shard_map/all_gather | solution.py:254
  8.5 1.1 copy-start.2
  9.7 0.7 copy-start.4
  10.4 5.5 %copy-start = (bf16[1,128,6144]{2,1,0:T(8,128)(2,1)S(1)}, bf16[1,128,6144]{2,1,0:T(8,128)(2,1)}, u32[]{:S(2)}) copy-start(bf16[1,128,6144]{2,1,0:T(8,128)(2,1)} %param.9) | copy-start | bytes 4718596
  10.4 5.5 %copy-start.1 = (bf16[1,32,6144]{2,1,0:T(8,128)(2,1)S(1)}, bf16[1,32,6144]{2,1,0:T(8,128)(2,1)}, u32[]{:S(2)}) copy-start(bf16[1,32,6144]{2,1,0:T(8,128)(2,1)} %param.8) | copy-start | bytes 1179652
  10.4 5.5 %copy-start.3 = (bf16[1,32,2048]{2,1,0:T(8,128)(2,1)S(1)}, bf16[1,32,2048]{2,1,0:T(8,128)(2,1)}, u32[]{:S(2)}) copy-start(bf16[1,32,2048]{2,1,0:T(8,128)(2,1)} %param.11) | copy-start | bytes 393220
  11.4 21.0 %all-to-all-start.3 = ((bf16[8,128,384]{2,1,0:T(8,128)(2,1)}), bf16[8,128,384]{2,1,0:T(8,128)(2,1)S(1)}, u32[]{:S(2)}, u32[]{:S(2)}) async-start(bf16[8,128,384]{2,1,0:T(8,128)(2,1)} %shard_map.105.dimg), calls=%async_computation.3 | async-start | bytes 1572864 | tf_op jit(solution)/shard_map/all_to_all | solution.py:22
  32.4 0.9 copy-start.6
  33.3 23.7 %all-to-all-start.1 = ((bf16[16,160,256]{2,1,0:T(8,128)(2,1)}), bf16[16,160,256]{2,1,0:T(8,128)(2,1)S(1)}, u32[]{:S(2)}, u32[]{:S(2)}) async-start(bf16[16,160,256]{2,1,0:T(8,128)(2,1)} %shard_map.106), calls=%async_computation.1 | async-start | bytes 2621440 | tf_op jit(solution)/shard_map/all_to_all | solution.py:22
  41.7 21.7 %copy-start.7 = (bf16[8,128,384]{2,1,0:T(8,128)(2,1)S(1)}, bf16[8,128,384]{2,1,0:T(8,128)(2,1)}, u32[]{:S(2)}) copy-start(bf16[8,128,384]{2,1,0:T(8,128)(2,1)} %copy-done.6) | copy-start | bytes 2359300
  57.1 6.4 %copy-start.5 = (bf16[16,160,256]{2,1,0:T(8,128)(2,1)}, bf16[16,160,256]{2,1,0:T(8,128)(2,1)S(1)}, u32[]{:S(2)}) copy-start(bf16[16,160,256]{2,1,0:T(8,128)(2,1)S(1)} %all-to-all-done.1) | copy-start | bytes 3932164
  57.1 23.4 %all-to-all-start = ((bf16[16,160,256]{2,1,0:T(8,128)(2,1)}), bf16[16,160,256]{2,1,0:T(8,128)(2,1)}, u32[]{:S(2)}, u32[]{:S(2)}) async-start(bf16[16,160,256]{2,1,0:T(8,128)(2,1)} %shard_map.103), calls=%async_computation | async-start | bytes 2621440 | tf_op jit(solution)/shard_map/all_to_all | solution.py:22
  80.4 49.4 %all-to-all-start.4 = ((bf16[16,128,384]{2,1,0:T(8,128)(2,1)}), bf16[16,128,384]{2,1,0:T(8,128)(2,1)S(1)}, u32[]{:S(2)}, u32[]{:S(2)}) async-start(bf16[16,128,384]{2,1,0:T(8,128)(2,1)} %bitcast.15), calls=%async_computation.4 | async-start | bytes 3145728 | tf_op jit(solution)/shard_map/all_to_all | solution.py:22
  129.9 32.7 %all-to-all-start.2 = ((bf16[16,160,384]{2,1,0:T(8,128)(2,1)}), bf16[16,160,384]{2,1,0:T(8,128)(2,1)S(1)}, u32[]{:S(2)}, u32[]{:S(2)}) async-start(bf16[16,160,384]{2,1,0:T(8,128)(2,1)} %bitcast.40), calls=%async_computation.2 | async-start | bytes 3932160 | tf_op jit(solution)/shard_map/all_to_all | solution.py:22
  162.5 10.2 %all-to-all-start.5 = ((f32[8,16,384]{2,1,0:T(8,128)}), f32[8,16,384]{2,1,0:T(8,128)S(1)}, u32[]{:S(2)}, u32[]{:S(2)}) async-start(f32[8,16,384]{2,1,0:T(8,128)} %bitcast.16), calls=%async_computation.5 | async-start | bytes 393216 | tf_op jit(solution)/shard_map/all_to_all | solution.py:22
Sparse Core Ops, SparseCore 0:
  9.7 37.5 all-gather.2

commit v2 on v1

v2 whole, which is shorter than its diff:
```python
import functools

import jax
import jax.numpy as jnp
from jax import lax
from jax.experimental import pallas as pl
from jax.experimental.pallas import tpu as pltpu
from jax.sharding import Mesh, PartitionSpec as P

HEAD_SIZE = 128
SCALE = HEAD_SIZE ** (-0.5)
LOG2E = 1.4426950408889634
BLOCK = 512
CHUNK = 256
SEQ = ("zl", "x", "c")
PLANE = ("zh", "zl", "x")
ALL = ("zh", "y", "zl", "x", "c")
BF16 = jnp.bfloat16
F32 = jnp.float32


def exchange(array, axes):
    return lax.all_to_all(array, axes, split_axis=0, concat_axis=0, tiled=True)


def params(mib):
    return pltpu.CompilerParams(vmem_limit_bytes=mib << 20)


def cost(flops, nbytes, exps=0):
    return pl.CostEstimate(flops=flops // 1000, bytes_accessed=nbytes // 1000, transcendentals=exps // 1000)


def pack_kernel(slots, *refs):
    out = refs[-1]
    txt, img = refs[:slots], refs[slots : 2 * slots]
    heads = out.shape[0]
    t = txt[0].shape[0]
    for j in range(slots):
        lanes = slice(j * HEAD_SIZE, (j + 1) * HEAD_SIZE)
        for h in range(heads):
            cols = slice(h * HEAD_SIZE, (h + 1) * HEAD_SIZE)
            out[h, :t, lanes] = txt[j][:, cols]
            out[h, t:, lanes] = img[j][:, cols]


def pack_heads(txt, img, first, slots, heads, step=4):
    t, i = txt.shape[0], img.shape[0]
    per = heads // step

    def spec(rows, j):
        return pl.BlockSpec((rows, step * HEAD_SIZE), lambda g: (0, (first + j) * per + g))

    nbytes = 2 * (t + i) * slots * heads * HEAD_SIZE * 2
    return pl.pallas_call(
        functools.partial(pack_kernel, slots),
        grid=(per,),
        in_specs=[spec(t, j) for j in range(slots)] + [spec(i, j) for j in range(slots)],
        out_specs=pl.BlockSpec((step, t + i, slots * HEAD_SIZE), lambda g: (g, 0, 0)),
        out_shape=jax.ShapeDtypeStruct((heads, t + i, slots * HEAD_SIZE), BF16),
        compiler_params=params(56),
        cost_estimate=cost(0, nbytes),
    )(*([txt] * slots), *([img] * slots))


def d_image_kernel(cot, gate, adv, y, attn, out, here, ahead, behind, across):
    weighted = adv[0, 0] * gate[...]
    out[...] = (weighted * cot[...].astype(F32)).astype(BF16)
    width = here.shape[1]
    count = out.shape[1] // width
    for hop, ref in ((0, here), (1, ahead), (count - 1, behind), (2, across)):
        start = lax.rem(y[0, 0] + hop, count) * width
        ref[:, ref.shape[1] - width :] = out[:, pl.ds(pl.multiple_of(start, width), width)]
    across[:, : attn.shape[1]] = attn[...]


def d_image_call(cot, gate, adv, y, attn, count):
    rows, width = cot.shape
    vmem = pl.BlockSpec(memory_space=pltpu.VMEM)
    smem = pl.BlockSpec(memory_space=pltpu.SMEM)
    part = jax.ShapeDtypeStruct((rows, width // count), BF16)
    return pl.pallas_call(
        d_image_kernel,
        in_specs=[vmem, vmem, smem, smem, vmem],
        out_specs=[vmem] * 5,
        out_shape=[
            jax.ShapeDtypeStruct((rows, width), BF16),
            part,
            part,
            part,
            jax.ShapeDtypeStruct((rows, width // count + attn.shape[1]), BF16),
        ],
        compiler_params=params(56),
        cost_estimate=cost(2 * rows * width, 6 * rows * width),
    )(cot, gate, adv, y, attn)


def partial_kernel(c, a0, a1, a2, d0, d1, d2, merged, keep, low, high):
    block, half = keep.shape
    at = pl.program_id(0) * block
    rows = merged.shape[1] - 2 * half
    lhs = [a0[...], a1[...], a2[...], merged[:, pl.ds(pl.multiple_of(at, block), block)]]
    rhs = [d0[...], d1[...], d2[...], merged[:, rows:]]
    value = lax.dot_general(
        jnp.concatenate(lhs, axis=0),
        jnp.concatenate(rhs, axis=0),
        (((0,), (0,)), ((), ())),
        preferred_element_type=F32,
    )
    left, right = value[:, :half], value[:, half:]
    first = c[0, 0] == 0
    keep[...] = jnp.where(first, left, right).astype(BF16)
    send = jnp.where(first, right, left).astype(BF16)
    early = pl.program_id(0) < pl.num_programs(0) // 2

    @pl.when(early)
    def _():
        low[...] = send

    @pl.when(jnp.logical_not(early))
    def _():
        high[...] = send


def partial_call(c, attns, parts, merged):
    tokens, rows = attns[0].shape
    cols = parts[0].shape[1]
    block = 512
    a_spec = pl.BlockSpec((tokens, block), lambda i: (0, i))
    d_spec = pl.BlockSpec((tokens, cols), lambda i: (0, 0))
    m_spec = pl.BlockSpec((tokens, rows + cols), lambda i: (0, 0))
    half = rows // block // 2
    out = pl.BlockSpec((block, cols // 2), lambda i: (i, 0))
    return pl.pallas_call(
        partial_kernel,
        grid=(rows // block,),
        in_specs=[pl.BlockSpec(memory_space=pltpu.SMEM)] + [a_spec] * 3 + [d_spec] * 3 + [m_spec],
        out_specs=[
            out,
            pl.BlockSpec((block, cols // 2), lambda i: (jnp.minimum(i, half - 1), 0)),
            pl.BlockSpec((block, cols // 2), lambda i: (jnp.maximum(i - half, 0), 0)),
        ],
        out_shape=[
            jax.ShapeDtypeStruct((rows, cols // 2), BF16),
            jax.ShapeDtypeStruct((rows // 2, cols // 2), BF16),
            jax.ShapeDtypeStruct((rows // 2, cols // 2), BF16),
        ],
        compiler_params=params(40),
        cost_estimate=cost(8 * tokens * rows * cols, 8 * tokens * (rows + cols) + 2 * rows * cols),
    )(c, *attns, *parts, merged)


def place_kernel(ring, keep, low, high, out):
    places, rows, _ = out.shape
    got = jnp.where(pl.program_id(0) == 0, low[...], high[...])
    value = (keep[...].astype(F32) + got.astype(F32)).astype(BF16)
    rows //= ring
    for y in range(ring):
        for place in range(places):
            at = (y * places + place) * rows
            out[place, y * rows : (y + 1) * rows] = value[at : at + rows]


def place_call(keep, got, ring, places, rows):
    cols = keep.shape[1]
    block = pl.BlockSpec((ring * places * rows, cols), lambda h: (h, 0))
    return pl.pallas_call(
        functools.partial(place_kernel, ring),
        grid=(len(got),),
        in_specs=[block] + [pl.BlockSpec((ring * places * rows, cols), lambda h: (0, 0))] * len(got),
        out_specs=pl.BlockSpec((places, ring * rows, cols), lambda h: (h, 0, 0)),
        out_shape=jax.ShapeDtypeStruct((len(got) * places, ring * rows, cols), BF16),
        compiler_params=params(24),
        cost_estimate=cost(0, 6 * keep.size),
    )(keep, *got)


def d_out_kernel(dimg, weight, cot_txt, adv, vt, vi, out):
    heads = out.shape[0]
    t = cot_txt.shape[0]
    total = lax.dot_general(dimg[...], weight[...], (((1,), (1,)), ((), ())), preferred_element_type=F32)
    total = total.astype(BF16)
    text = (adv[0, 0] * cot_txt[...].astype(F32)).astype(BF16)
    for h in range(heads):
        cols = slice(h * HEAD_SIZE, (h + 1) * HEAD_SIZE)
        out[h, :t, :HEAD_SIZE] = vt[:, cols]
        out[h, t:, :HEAD_SIZE] = vi[:, cols]
        out[h, :t, HEAD_SIZE:] = text[:, cols]
        out[h, t:, HEAD_SIZE:] = total[:, cols]


def d_out_call(dimg, weight, cot_txt, adv, txt, img, heads, step=4):
    rows, model = dimg.shape
    t = cot_txt.shape[0]
    width = step * HEAD_SIZE
    per = heads // step
    return pl.pallas_call(
        d_out_kernel,
        grid=(per,),
        in_specs=[
            pl.BlockSpec((rows, model), lambda g: (0, 0)),
            pl.BlockSpec((width, model), lambda g: (g, 0)),
            pl.BlockSpec((t, width), lambda g: (0, g)),
            pl.BlockSpec(memory_space=pltpu.SMEM),
            pl.BlockSpec((t, width), lambda g: (0, 2 * per + g)),
            pl.BlockSpec((rows, width), lambda g: (0, 2 * per + g)),
        ],
        out_specs=pl.BlockSpec((step, t + rows, 2 * HEAD_SIZE), lambda g: (g, 0, 0)),
        out_shape=jax.ShapeDtypeStruct((heads, t + rows, 2 * HEAD_SIZE), BF16),
        compiler_params=params(56),
        cost_estimate=cost(
            2 * rows * weight.size, 2 * (weight.size + dimg.size + 3 * (t + rows) * heads * HEAD_SIZE)
        ),
    )(dimg, weight, cot_txt, adv, txt, img)


def fold(array, combine):
    return combine(array.reshape(-1, 8, array.shape[1]), axis=0)


def exps_kernel(q, k, e_out, inv_out, scores):
    chunks = [slice(at, at + CHUNK) for at in range(0, k.shape[0], CHUNK)]
    top = None
    for rows in chunks:
        part = lax.dot_general(k[rows], q[...], (((1,), (1,)), ((), ())), preferred_element_type=F32)
        scores[rows] = part
        part = fold(part, jnp.max)
        top = part if top is None else jnp.maximum(top, part)
    top = jnp.max(top, axis=0, keepdims=True)
    total = jnp.zeros((8, top.shape[1]), F32)
    for rows in chunks:
        low = jnp.exp2((scores[rows] - top) * (SCALE * LOG2E)).astype(BF16)
        e_out[rows] = low
        total += fold(low.astype(F32), jnp.sum)
    inverse = 1.0 / jnp.sum(total, axis=0, keepdims=True)
    inv_out[...] = jnp.transpose(jnp.broadcast_to(inverse, (HEAD_SIZE, inverse.shape[1])))


def exps_call(qk):
    n = qk.shape[0]
    block = BLOCK
    return pl.pallas_call(
        exps_kernel,
        grid=(n // block,),
        in_specs=[
            pl.BlockSpec((block, HEAD_SIZE), lambda i: (i, 0)),
            pl.BlockSpec((n, HEAD_SIZE), lambda i: (0, 1)),
        ],
        out_specs=[
            pl.BlockSpec((n, block), lambda i: (0, i)),
            pl.BlockSpec((block, HEAD_SIZE), lambda i: (i, 0)),
        ],
        out_shape=[
            jax.ShapeDtypeStruct((n, n), BF16),
            jax.ShapeDtypeStruct((n, HEAD_SIZE), F32),
        ],
        scratch_shapes=[pltpu.VMEM((n, block), F32)],
        compiler_params=params(56),
        cost_estimate=cost(2 * n * n * HEAD_SIZE * 2, 2 * n * n, n * n),
    )(qk, qk)


def grads_kernel(e, inv, q, k, v, d, out, dk, dv, prob_grads):
    step = pl.program_id(0)
    chunks = [slice(at, at + CHUNK) for at in range(0, k.shape[0], CHUNK)]

    @pl.when(step == 0)
    def _():
        dk[...] = jnp.zeros_like(dk)
        dv[...] = jnp.zeros_like(dv)

    inverse = inv[...]
    d_low = (d[...].astype(F32) * inverse).astype(BF16)
    centre = jnp.zeros((8, BLOCK), F32)
    for rows in chunks:
        probs = e[rows]
        part = lax.dot_general(v[rows], d_low, (((1,), (1,)), ((), ())), preferred_element_type=F32)
        prob_grads[rows] = part
        centre += fold(probs.astype(F32) * part, jnp.sum)
        dv[rows] += jnp.dot(probs, d_low, preferred_element_type=F32)
    centre = jnp.sum(centre, axis=0, keepdims=True) * jnp.transpose(inverse)[:1]
    dq = jnp.zeros((BLOCK, HEAD_SIZE), F32)
    for rows in chunks:
        score_grad = (e[rows].astype(F32) * (prob_grads[rows] - centre)).astype(BF16)
        dk[rows] += jnp.dot(score_grad, q[...], preferred_element_type=F32)
        dq += lax.dot_general(score_grad, k[rows], (((0,), (0,)), ((), ())), preferred_element_type=F32)
    out[pl.ds(pl.multiple_of(step * BLOCK, BLOCK), BLOCK), :HEAD_SIZE] = (dq * SCALE).astype(BF16)

    @pl.when(step == pl.num_programs(0) - 1)
    def _():
        out[:, HEAD_SIZE : 2 * HEAD_SIZE] = (dk[...] * SCALE).astype(BF16)
        out[:, 2 * HEAD_SIZE :] = dv[...].astype(BF16)


def grads_call(exps, inverse, qk, vd):
    n = qk.shape[0]
    block = lambda col: pl.BlockSpec((BLOCK, HEAD_SIZE), lambda i: (i, col))
    whole = lambda col: pl.BlockSpec((n, HEAD_SIZE), lambda i: (0, col))
    return pl.pallas_call(
        grads_kernel,
        grid=(n // BLOCK,),
        in_specs=[pl.BlockSpec((n, BLOCK), lambda i: (0, i)), block(0), block(0), whole(1), whole(0), block(1)],
        out_specs=pl.BlockSpec((n, 3 * HEAD_SIZE), lambda i: (0, 0)),
        out_shape=jax.ShapeDtypeStruct((n, 3 * HEAD_SIZE), BF16),
        scratch_shapes=[pltpu.VMEM((n, HEAD_SIZE), F32)] * 2 + [pltpu.VMEM((n, BLOCK), F32)],
        compiler_params=params(56),
        cost_estimate=cost(2 * n * n * HEAD_SIZE * 8, 2 * n * n),
    )(exps, inverse, qk, qk, vd, vd)


def unpack_kernel(back, txt, img):
    t = txt.shape[0]
    for h in range(back.shape[0]):
        cols = slice(h * HEAD_SIZE, (h + 1) * HEAD_SIZE)
        txt[:, cols] = back[h, :t]
        img[:, cols] = back[h, t:]


def unpack_call(back, t):
    heads, tokens, _ = back.shape
    width = heads * HEAD_SIZE
    i = tokens - t
    return pl.pallas_call(
        unpack_kernel,
        grid=(3,),
        in_specs=[pl.BlockSpec((heads, tokens, HEAD_SIZE), lambda j: (0, 0, j))],
        out_specs=[
            pl.BlockSpec((t, width), lambda j: (0, j)),
            pl.BlockSpec((i, width), lambda j: (0, j)),
        ],
        out_shape=[
            jax.ShapeDtypeStruct((t, 3 * width), BF16),
            jax.ShapeDtypeStruct((i, 3 * width), BF16),
        ],
        compiler_params=params(24),
        cost_estimate=cost(0, 12 * tokens * width),
    )(back)


def ring_kernel(y, *refs):
    out = refs[-1]
    count = len(refs) - 1
    width = refs[0].shape[1]
    for hop in range(count):
        start = lax.rem(y[0, 0] + count - hop, count) * width
        out[:, pl.ds(pl.multiple_of(start, width), width)] = refs[hop][...]


def ring_call(y, pieces):
    rows, width = pieces[0].shape
    vmem = pl.BlockSpec(memory_space=pltpu.VMEM)
    return pl.pallas_call(
        ring_kernel,
        in_specs=[pl.BlockSpec(memory_space=pltpu.SMEM)] + [vmem] * len(pieces),
        out_specs=vmem,
        out_shape=jax.ShapeDtypeStruct((rows, width * len(pieces)), F32),
        compiler_params=params(16),
        cost_estimate=cost(0, 8 * rows * width * len(pieces)),
    )(y, *pieces)


def per_device(qkv_txt, qkv_img, attn_img, cot_txt, cot_img, gate, advantage, proj_weight):
    txt, img = qkv_txt[0], qkv_img[0]
    tokens = txt.shape[0] + img.shape[0]
    width = attn_img.shape[2]
    heads = width // HEAD_SIZE
    model = cot_img.shape[2]
    adv = advantage[:, None]
    count = lax.axis_size("y")
    y = lax.axis_index("y").astype(jnp.int32)
    c = lax.axis_index("c").astype(jnp.int32)
    hops = (1, count - 1, 2)

    def shift(array, hop):
        return lax.ppermute(array, "y", [(i, (i + hop) % count) for i in range(count)])

    def swap(array):
        return lax.ppermute(array, "c", [(0, 1), (1, 0)])

    attn = attn_img[0]
    packed = pack_heads(txt, img, 0, 2, heads)
    qk = exchange(packed, SEQ)
    cot, attn, packed = lax.optimization_barrier((cot_img[0], attn, packed))
    attns = [shift(attn, hop) for hop in hops[:2]]
    d_image, here, *parts = d_image_call(cot, gate, adv, y.reshape(1, 1), attn, count)
    *parts, merged = [shift(part, hop) for hop, part in zip(hops, parts)]
    vd = d_out_call(d_image, proj_weight, cot_txt[0], adv, txt, img, heads)
    vd, qk = lax.optimization_barrier((vd, qk))
    vd = exchange(vd, SEQ)

    n = heads * tokens
    qk = qk.reshape(n, 2 * HEAD_SIZE)
    exps, inverse = exps_call(qk)
    attn, attns, here, parts, merged, inverse = lax.optimization_barrier(
        (attn, attns, here, parts, merged, inverse)
    )
    keep, *send = partial_call(c.reshape(1, 1), [attn, *attns], [here, *parts], merged)
    got = [swap(part) for part in send]

    devices = lax.axis_size(ALL)
    rows = width // devices
    cols = keep.shape[1]
    product = place_call(keep, got, count, lax.axis_size(PLANE) // 2, 2 * rows)
    product = exchange(product, PLANE)

    vd = vd.reshape(n, 2 * HEAD_SIZE)
    grads = grads_call(exps, inverse, qk, vd).reshape(heads, tokens, 3 * HEAD_SIZE)
    grads, product = lax.optimization_barrier((grads, product))
    back = exchange(grads, SEQ)

    total = jnp.sum(product.astype(F32), axis=0) * (1.0 / (img.shape[0] * devices))
    total = total.reshape(count, 2, rows, cols)
    own = lax.dynamic_index_in_dim(total, c, 1, keepdims=False)
    other = swap(lax.dynamic_index_in_dim(total, 1 - c, 1, keepdims=False))
    wide = jnp.where(c == 0, jnp.concatenate([own, other], -1), jnp.concatenate([other, own], -1))
    pick = lambda hop: lax.dynamic_index_in_dim(wide, (y + hop) % count, 0, keepdims=False)
    placed = [pick(0)] + [shift(pick(hop), hop) for hop in hops]
    order = [placed[0], placed[1], placed[3], placed[2]]
    grad_proj = ring_call(y.reshape(1, 1), order)
    back, grad_proj = lax.optimization_barrier((back, grad_proj))

    dqkv_txt, dqkv_img = unpack_call(back, txt.shape[0])
    return (dqkv_txt[None], dqkv_img[None], grad_proj)


def solution(mesh):
    fine = Mesh(mesh.devices.reshape(2, 4, 2, 4, 2), ALL)
    dp = ("zh", "y")
    tokens = P(dp, SEQ, None)
    return jax.shard_map(
        per_device,
        mesh=fine,
        in_specs=(tokens, tokens, tokens, tokens, tokens, P(dp, None), P(dp), P()),
        out_specs=(tokens, tokens, P(dp + SEQ, None)),
        check_vma=False,
    )
```

time: 181 us -> 126 us (0.70)
  waiting for transfers between devices: 65.1 us -> 25.8 us
  between operations: 14.8 us -> 1.41 us
  starting transfers between devices: 34.9 us -> 41.1 us
  local copies, waits for them, and re-layouts: 5.69 us -> 0.07 us
  matrix products: 4.01 us -> 0 us
  Pallas kernels: 54.9 us -> 57.3 us
    all_to_all x6 -> x4, waiting for transfers between devices: 64.4 us -> 18.6 us  [exchange(): return lax.all_to_all(array, axes, split_axis=0, concat_axis=0, tiled=True)]
    ppermute x0 -> x11, starting transfers between devices: none -> 14.2 us  [the longest x8 13.4 us: shift(): lax.ppermute(array, 'y', [(i, (i + hop) % count) for i in range(count)])]
    all_to_all x6 -> x4, starting transfers between devices: 34.8 us -> 26.9 us  [exchange(): return lax.all_to_all(array, axes, split_axis=0, concat_axis=0, tiled=True)]
    ppermute x0 -> x11, waiting for transfers between devices: none -> 7.17 us  [the longest x3 4.05 us: swap(): return lax.ppermute(array, 'c', [(0, 1), (1, 0)])]
    dot_general x1 -> x0, matrix products: 4.01 us -> none  [per_device(): lax.dot_general(attn, d_columns, (((0,), (0,)), ((), ())), preferred_elem...]
    pallas_call x3 -> x6, Pallas kernels: 27.6 us -> 30.4 us  [the longest x1 13.7 us: exps_call(): pl.pallas_call(exps_kernel, grid=(n // block,), in_specs=[pl.BlockSpec((b...]
    unnamed x16 -> x8, local copies, waits for them, and re-layouts: 2.74 us -> 0.01 us
    pallas_call x1, Pallas kernels: 23.3 us -> 21 us  [grads_call(): pl.pallas_call(grads_kernel, grid=(n // BLOCK,), in_specs=[pl.BlockSpec((...]
  transfers between devices with their start and end apart: 7 -> 15, of which waited for: 5 -> 7; matrix products, arithmetic and copies ran while one was open for 4% -> 0% of each run, Pallas kernels for 30% -> 41%
where the time goes in v2:
time: 126 us
  Pallas kernels  57.3 us (45%)
  starting transfers between devices  41.1 us (33%)
  waiting for transfers between devices  25.8 us (20%)
  between operations  1.41 us (1%)
    all_to_all x4, starting transfers between devices, exchange(): return lax.all_to_all(array, axes, split_axis=0, concat_axis=0, tiled=True)  26.9 us
    pallas_call x1, Pallas kernels, grads_call(): pl.pallas_call(grads_kernel, grid=(n // BLOCK,), in_specs=[pl.BlockSpec((...  21 us
    all_to_all x4, waiting for transfers between devices, exchange(): return lax.all_to_all(array, axes, split_axis=0, concat_axis=0, tiled=True)  18.6 us
    pallas_call x1, Pallas kernels, exps_call(): pl.pallas_call(exps_kernel, grid=(n // block,), in_specs=[pl.BlockSpec((b...  13.7 us
    ppermute x8, starting transfers between devices, shift(): lax.ppermute(array, 'y', [(i, (i + hop) % count) for i in range(count)])  13.4 us
    pallas_call x1, Pallas kernels, d_out_call(): pl.pallas_call(d_out_kernel, grid=(per,), in_specs=[pl.BlockSpec((rows, m...  8.74 us
    ppermute x3, waiting for transfers between devices, swap(): return lax.ppermute(array, 'c', [(0, 1), (1, 0)])  4.05 us
    pallas_call x1, Pallas kernels, pack_heads(): pl.pallas_call(functools.partial(pack_kernel, slots), grid=(per,), in_spe...  3.64 us
  transfers between devices with their start and end apart: 15, of which 7 were waited for; matrix products, arithmetic and copies ran while one was open for 0% of the time, Pallas kernels for 41%

profile of v2, /device:TPU:2, one launch (start us, length us, event | category | flops | bytes accessed | tf_op | source)
XLA Modules:
  0.0 125.9 jit_solution(9411314857344055246)
XLA Ops:
  0.6 3.6 %shard_map.103 = bf16[16,160,256]{2,1,0:T(8,128)(2,1)} custom-call(bf16[32,6144]{1,0:T(8,128)(2,1)} %bitcast.36, bf16[32,6144]{1,0:T(8,128)(2,1)} %bitcast.37, bf16[128,6144]{1,0:T(8,128)(2,1)} %bitcast.32, bf16[128,6144]{1,0:T(8,128)(2,1)} %bitcast.33), custom_call_target="tpu_custom_call" | custom-call | bytes 2621 | tf_op jit(solution)/shard_map/pallas_call | solution.py:55
  4.3 0.0 copy-start
  4.3 6.3 %all-to-all-start = ((bf16[16,160,256]{2,1,0:T(8,128)(2,1)}), bf16[16,160,256]{2,1,0:T(8,128)(2,1)}, u32[]{:S(2)}, u32[]{:S(2)}) async-start(bf16[16,160,256]{2,1,0:T(8,128)(2,1)} %shard_map.103), calls=%async_computation | async-start | bytes 2621440 | tf_op jit(solution)/shard_map/all_to_all | solution.py:23
  11.3 3.0 %shard_map.104 = (bf16[128,3072]{1,0:T(8,128)(2,1)}, bf16[128,768]{1,0:T(8,128)(2,1)}, bf16[128,768]{1,0:T(8,128)(2,1)}, bf16[128,768]{1,0:T(8,128)(2,1)}, bf16[128,2816]{1,0:T(8,128)(2,1)}) custom-call(bf16[128,3072]{1,0:T(8,128)(2,1)} %bitcast.39, f32[1,3072]{1,0:T(1,128)} %gate.1, f32[1,1]{1,0:T(1,128)} %bitcast.26.adv, s32[1,1]{1,0:T(1,128)} %bitcast.5.y, ...), custom_call_target="tpu_custom_call" | custom-call | flops 786 | bytes 2359 | tf_op jit(solution)/shard_map/pallas_call | solution.py:82
  14.3 3.2 %collective-permute-start.4 = (bf16[128,2816]{1,0:T(8,128)(2,1)}, bf16[128,2816]{1,0:T(8,128)(2,1)S(1)}, u32[]{:S(2)}, u32[]{:S(2)}) collective-permute-start(bf16[128,2816]{1,0:T(8,128)(2,1)} %get-tuple-element.39), channel_id=1, source_target_pairs={{0,32},{16,48},{32,0},{48,16},{1,33},{17,49},{33,1},{49,17},{2,34}... | collective-permute-start | bytes 2162696 | tf_op jit(solution)/shard_map/ppermute | solution.py:375
  17.5 0.0 copy-done
  17.5 0.7 collective-permute-start
  18.1 2.6 %collective-permute-start.1 = (bf16[128,2048]{1,0:T(8,128)(2,1)S(1)}, bf16[128,2048]{1,0:T(8,128)(2,1)S(1)}, u32[]{:S(2)}, u32[]{:S(2)}) collective-permute-start(bf16[128,2048]{1,0:T(8,128)(2,1)S(1)} %bitcast.30), channel_id=1, source_target_pairs={{0,48},{16,0},{32,16},{48,32},{1,49},{17,1},{33,17},{49,33},{2,50}... | collective-permute-start | bytes 1572872 | tf_op jit(solution)/shard_map/ppermute | solution.py:375
  20.7 8.7 %shard_map.105 = bf16[16,160,256]{2,1,0:T(8,128)(2,1)} custom-call(bf16[128,3072]{1,0:T(8,128)(2,1)} %get-tuple-element.33.dimg, bf16[2048,3072]{1,0:T(8,128)(2,1)} %weight.1, bf16[32,2048]{1,0:T(8,128)(2,1)} %bitcast.41, f32[1,1]{1,0:T(1,128)} %bitcast.27.adv, bf16[32,6144]{1,0:T(8,128)(2,1)} %bitcast.38, bf16[128,6144]{1,0:T(8,128)(2,1)} %bitcast.34), custom_call_target="tpu_custom_call" | custom-call | flops 1610612 | bytes 15335 | tf_op jit(solution)/shard_map/pallas_call | solution.py:197
  29.4 0.0 copy-start.3
  29.5 0.0 copy-start.2
  29.5 0.0 all-to-all-done
  29.5 5.9 %all-to-all-start.1 = ((bf16[16,160,256]{2,1,0:T(8,128)(2,1)}), bf16[16,160,256]{2,1,0:T(8,128)(2,1)}, u32[]{:S(2)}, u32[]{:S(2)}) async-start(bf16[16,160,256]{2,1,0:T(8,128)(2,1)} %shard_map.105), calls=%async_computation.1 | async-start | bytes 2621440 | tf_op jit(solution)/shard_map/all_to_all | solution.py:23
  35.3 0.0 copy-start.1
  35.3 0.0 copy-done.3
  35.3 0.5 collective-permute-start.2
  35.9 0.0 copy-done.2
  35.9 2.8 %collective-permute-start.3 = (bf16[128,768]{1,0:T(8,128)(2,1)S(1)}, bf16[128,768]{1,0:T(8,128)(2,1)S(1)}, u32[]{:S(2)}, u32[]{:S(2)}) collective-permute-start(bf16[128,768]{1,0:T(8,128)(2,1)S(1)} %copy-done.2), channel_id=1, source_target_pairs={{0,48},{16,0},{32,16},{48,32},{1,49},{17,1},{33,17},{49,33},{2,50}... | collective-permute-start | bytes 589832 | tf_op jit(solution)/shard_map/ppermute | solution.py:375
  38.7 13.7 %shard_map.106 = (bf16[2560,2560]{1,0:T(8,128)(2,1)}, f32[2560,128]{1,0:T(8,128)}) custom-call(bf16[2560,256]{1,0:T(8,128)(2,1)} %bitcast.7.q.k, bf16[2560,256]{1,0:T(8,128)(2,1)} %bitcast.7.q.k), custom_call_target="tpu_custom_call" | custom-call | flops 3355443 | bytes 13107 | tf_op jit(solution)/shard_map/pallas_call | solution.py:242
  52.4 0.0 collective-permute-done.2.d1
  52.4 0.0 collective-permute-done.3.d2
  52.4 0.0 collective-permute-done.a1
  52.4 0.0 collective-permute-done.1.a2
  52.4 0.0 collective-permute-done.4.merged
  52.4 0.0 copy-done.1
  52.4 2.9 %shard_map.108 = (bf16[2048,384]{1,0:T(8,128)(2,1)S(1)}, bf16[1024,384]{1,0:T(8,128)(2,1)S(1)}, bf16[1024,384]{1,0:T(8,128)(2,1)S(1)}) custom-call(s32[1,1]{1,0:T(1,128)} %bitcast.10.c, bf16[128,2048]{1,0:T(8,128)(2,1)S(1)} %bitcast.31, bf16[128,2048]{1,0:T(8,128)(2,1)S(1)} %collective-permute-done.a1, bf16[128,2048]{1,0:T(8,128)(2,1)S(1)} %collective-permute-done.1.a2, ...), custom_call_target="tpu_custom_call" | custom-call | flops 1610612 | bytes 6029 | tf_op jit(solution)/shard_map/pallas_call | solution.py:134
  55.3 0.1 collective-permute-start.5
  55.4 0.5 collective-permute-start.6
  55.9 1.8 %collective-permute-done.5.low = bf16[1024,384]{1,0:T(8,128)(2,1)S(1)} collective-permute-done((bf16[1024,384]{1,0:T(8,128)(2,1)S(1)}, bf16[1024,384]{1,0:T(8,128)(2,1)S(1)}, u32[]{:S(2)}, u32[]{:S(2)}) %collective-permute-start.5) | collective-permute-done | bytes 786464 | tf_op jit(solution)/shard_map/ppermute | solution.py:378
  57.7 1.1 collective-permute-done.6.high
  58.8 1.4 %shard_map.109 = bf16[16,128,384]{2,1,0:T(8,128)(2,1)} custom-call(bf16[2048,384]{1,0:T(8,128)(2,1)S(1)} %get-tuple-element.50.keep, bf16[1024,384]{1,0:T(8,128)(2,1)S(1)} %collective-permute-done.5.low, bf16[1024,384]{1,0:T(8,128)(2,1)S(1)} %collective-permute-done.6.high), custom_call_target="tpu_custom_call" | custom-call | bytes 4718 | tf_op jit(solution)/shard_map/pallas_call | solution.py:167
  60.2 0.0 all-to-all-done.1
  60.2 7.8 %all-to-all-start.2 = ((bf16[16,128,384]{2,1,0:T(8,128)(2,1)}), bf16[16,128,384]{2,1,0:T(8,128)(2,1)S(1)}, u32[]{:S(2)}, u32[]{:S(2)}) async-start(bf16[16,128,384]{2,1,0:T(8,128)(2,1)} %shard_map.109), calls=%async_computation.2 | async-start | bytes 3145728 | tf_op jit(solution)/shard_map/all_to_all | solution.py:23
  68.0 21.0 %shard_map.107 = bf16[2560,384]{1,0:T(8,128)(2,1)} custom-call(bf16[2560,2560]{1,0:T(8,128)(2,1)} %get-tuple-element.35.e, f32[2560,128]{1,0:T(8,128)} %get-tuple-element.41.inv, bf16[2560,256]{1,0:T(8,128)(2,1)} %bitcast.7.q.k, bf16[2560,256]{1,0:T(8,128)(2,1)} %bitcast.7.q.k, bf16[2560,256]{1,0:T(8,128)(2,1)} %bitcast.8.v.d, bf16[2560,256]{1,0:T(8,128)(2,1)} %bitcast.8.v.d), custom_call_target="tpu_custom_call" | custom-call | flops 13421772 | bytes 13107 | tf_op jit(solution)/shard_map/pallas_call | solution.py:299
  89.0 0.8 all-to-all-done.2
  89.8 6.9 %all-to-all-start.3 = ((bf16[16,160,384]{2,1,0:T(8,128)(2,1)}), bf16[16,160,384]{2,1,0:T(8,128)(2,1)S(1)}, u32[]{:S(2)}, u32[]{:S(2)}) async-start(bf16[16,160,384]{2,1,0:T(8,128)(2,1)} %bitcast.35), calls=%async_computation.3 | async-start | bytes 3932160 | tf_op jit(solution)/shard_map/all_to_all | solution.py:23
  96.7 0.2 convert_reduce_fusion
  96.9 0.2 collective-permute-start.7
  97.2 1.2 collective-permute-done.7
  98.4 0.1 collective-permute-start.8
  98.5 2.2 %collective-permute-start.9 = (f32[16,768]{1,0:T(8,128)S(1)}, f32[16,768]{1,0:T(8,128)S(1)}, u32[]{:S(2)}, u32[]{:S(2)}) collective-permute-start(f32[16,768]{1,0:T(8,128)S(1)} %get-tuple-element.60), channel_id=1, source_target_pairs={{0,32},{16,48},{32,0},{48,16},{1,33},{17,49},{33,1},{49,17},{2,34}... | collective-permute-start | bytes 147464 | tf_op jit(solution)/shard_map/ppermute | solution.py:375
  100.7 1.3 %collective-permute-start.10 = (f32[16,768]{1,0:T(8,128)S(1)}, f32[16,768]{1,0:T(8,128)S(1)}, u32[]{:S(2)}, u32[]{:S(2)}) collective-permute-start(f32[16,768]{1,0:T(8,128)S(1)} %get-tuple-element.59), channel_id=1, source_target_pairs={{0,48},{16,0},{32,16},{48,32},{1,49},{17,1},{33,17},{49,33},{2,50}... | collective-permute-start | bytes 147464 | tf_op jit(solution)/shard_map/ppermute | solution.py:375
  102.0 2.5 %collective-permute-done.8.refs_1_ = f32[16,768]{1,0:T(8,128)S(1)} collective-permute-done((f32[16,768]{1,0:T(8,128)S(1)}, f32[16,768]{1,0:T(8,128)S(1)}, u32[]{:S(2)}, u32[]{:S(2)}) %collective-permute-start.8) | collective-permute-done | bytes 49184 | tf_op jit(solution)/shard_map/ppermute | solution.py:375
  104.5 0.0 collective-permute-done.9.refs_2_
  104.5 0.6 collective-permute-done.10.refs_3_
  105.1 0.7 shard_map.110
  105.8 17.8 %all-to-all-done.3.back = bf16[16,160,384]{2,1,0:T(8,128)(2,1)S(1)} async-done(((bf16[16,160,384]{2,1,0:T(8,128)(2,1)}), bf16[16,160,384]{2,1,0:T(8,128)(2,1)S(1)}, u32[]{:S(2)}, u32[]{:S(2)}) %all-to-all-start.3) | async-done | bytes 1966112 | tf_op jit(solution)/shard_map/all_to_all | solution.py:23
  123.6 2.3 %shard_map.111 = (bf16[32,6144]{1,0:T(8,128)(2,1)}, bf16[128,6144]{1,0:T(8,128)(2,1)}) custom-call(bf16[16,160,384]{2,1,0:T(8,128)(2,1)S(1)} %all-to-all-done.3.back), custom_call_target="tpu_custom_call" | custom-call | bytes 3932 | tf_op jit(solution)/shard_map/pallas_call | solution.py:323
  (4 shorter events, 0.1 us)
Async XLA Ops:
  4.3 13.2 %copy-start = (bf16[1,128,2048]{2,1,0:T(8,128)(2,1)S(1)}, bf16[1,128,2048]{2,1,0:T(8,128)(2,1)}, u32[]{:S(2)}) copy-start(bf16[1,128,2048]{2,1,0:T(8,128)(2,1)} %param.10) | copy-start | bytes 1572868
  4.3 25.2 %all-to-all-start = ((bf16[16,160,256]{2,1,0:T(8,128)(2,1)}), bf16[16,160,256]{2,1,0:T(8,128)(2,1)}, u32[]{:S(2)}, u32[]{:S(2)}) async-start(bf16[16,160,256]{2,1,0:T(8,128)(2,1)} %shard_map.103), calls=%async_computation | async-start | bytes 2621440 | tf_op jit(solution)/shard_map/all_to_all | solution.py:23
  14.3 38.2 %collective-permute-start.4 = (bf16[128,2816]{1,0:T(8,128)(2,1)}, bf16[128,2816]{1,0:T(8,128)(2,1)S(1)}, u32[]{:S(2)}, u32[]{:S(2)}) collective-permute-start(bf16[128,2816]{1,0:T(8,128)(2,1)} %get-tuple-element.39), channel_id=1, source_target_pairs={{0,32},{16,48},{32,0},{48,16},{1,33},{17,49},{33,1},{49,17},{2,34}... | collective-permute-start | bytes 2162696 | tf_op jit(solution)/shard_map/ppermute | solution.py:375
  17.5 34.9 %collective-permute-start = (bf16[128,2048]{1,0:T(8,128)(2,1)S(1)}, bf16[128,2048]{1,0:T(8,128)(2,1)S(1)}, u32[]{:S(2)}, u32[]{:S(2)}) collective-permute-start(bf16[128,2048]{1,0:T(8,128)(2,1)S(1)} %bitcast.29), channel_id=1, source_target_pairs={{0,16},{16,32},{32,48},{48,0},{1,17},{17,33},{33,49},{49,1},{2,18}... | collective-permute-start | bytes 1572872 | tf_op jit(solution)/shard_map/ppermute | solution.py:375
  18.1 34.3 %collective-permute-start.1 = (bf16[128,2048]{1,0:T(8,128)(2,1)S(1)}, bf16[128,2048]{1,0:T(8,128)(2,1)S(1)}, u32[]{:S(2)}, u32[]{:S(2)}) collective-permute-start(bf16[128,2048]{1,0:T(8,128)(2,1)S(1)} %bitcast.30), channel_id=1, source_target_pairs={{0,48},{16,0},{32,16},{48,32},{1,49},{17,1},{33,17},{49,33},{2,50}... | collective-permute-start | bytes 1572872 | tf_op jit(solution)/shard_map/ppermute | solution.py:375
  29.4 5.9 %copy-start.3 = (bf16[128,768]{1,0:T(8,128)(2,1)S(1)}, bf16[128,768]{1,0:T(8,128)(2,1)}, u32[]{:S(2)}) copy-start(bf16[128,768]{1,0:T(8,128)(2,1)} %get-tuple-element.37) | copy-start | bytes 589828
  29.5 6.4 %copy-start.2 = (bf16[128,768]{1,0:T(8,128)(2,1)S(1)}, bf16[128,768]{1,0:T(8,128)(2,1)}, u32[]{:S(2)}) copy-start(bf16[128,768]{1,0:T(8,128)(2,1)} %get-tuple-element.38) | copy-start | bytes 589828
  29.5 30.7 %all-to-all-start.1 = ((bf16[16,160,256]{2,1,0:T(8,128)(2,1)}), bf16[16,160,256]{2,1,0:T(8,128)(2,1)}, u32[]{:S(2)}, u32[]{:S(2)}) async-start(bf16[16,160,256]{2,1,0:T(8,128)(2,1)} %shard_map.105), calls=%async_computation.1 | async-start | bytes 2621440 | tf_op jit(solution)/shard_map/all_to_all | solution.py:23
  35.3 17.1 %copy-start.1 = (bf16[128,768]{1,0:T(8,128)(2,1)S(1)}, bf16[128,768]{1,0:T(8,128)(2,1)}, u32[]{:S(2)}) copy-start(bf16[128,768]{1,0:T(8,128)(2,1)} %get-tuple-element.46.d0) | copy-start | bytes 589828
  35.3 17.1 %collective-permute-start.2 = (bf16[128,768]{1,0:T(8,128)(2,1)S(1)}, bf16[128,768]{1,0:T(8,128)(2,1)S(1)}, u32[]{:S(2)}, u32[]{:S(2)}) collective-permute-start(bf16[128,768]{1,0:T(8,128)(2,1)S(1)} %copy-done.3), channel_id=1, source_target_pairs={{0,16},{16,32},{32,48},{48,0},{1,17},{17,33},{33,49},{49,1},{2,18}... | collective-permute-start | bytes 589832 | tf_op jit(solution)/shard_map/ppermute | solution.py:375
  35.9 16.5 %collective-permute-start.3 = (bf16[128,768]{1,0:T(8,128)(2,1)S(1)}, bf16[128,768]{1,0:T(8,128)(2,1)S(1)}, u32[]{:S(2)}, u32[]{:S(2)}) collective-permute-start(bf16[128,768]{1,0:T(8,128)(2,1)S(1)} %copy-done.2), channel_id=1, source_target_pairs={{0,48},{16,0},{32,16},{48,32},{1,49},{17,1},{33,17},{49,33},{2,50}... | collective-permute-start | bytes 589832 | tf_op jit(solution)/shard_map/ppermute | solution.py:375
  55.3 2.4 %collective-permute-start.5 = (bf16[1024,384]{1,0:T(8,128)(2,1)S(1)}, bf16[1024,384]{1,0:T(8,128)(2,1)S(1)}, u32[]{:S(2)}, u32[]{:S(2)}) collective-permute-start(bf16[1024,384]{1,0:T(8,128)(2,1)S(1)} %get-tuple-element.51), channel_id=1, source_target_pairs={{0,1},{1,0},{2,3},{3,2},{4,5},{5,4},{6,7},{7,6},{8,9},{9,8},{10,11... | collective-permute-start | bytes 2359304 | tf_op jit(solution)/shard_map/ppermute | solution.py:378
  55.4 3.4 %collective-permute-start.6 = (bf16[1024,384]{1,0:T(8,128)(2,1)S(1)}, bf16[1024,384]{1,0:T(8,128)(2,1)S(1)}, u32[]{:S(2)}, u32[]{:S(2)}) collective-permute-start(bf16[1024,384]{1,0:T(8,128)(2,1)S(1)} %get-tuple-element.52), channel_id=1, source_target_pairs={{0,1},{1,0},{2,3},{3,2},{4,5},{5,4},{6,7},{7,6},{8,9},{9,8},{10,11... | collective-permute-start | bytes 2359304 | tf_op jit(solution)/shard_map/ppermute | solution.py:378
  60.2 29.7 %all-to-all-start.2 = ((bf16[16,128,384]{2,1,0:T(8,128)(2,1)}), bf16[16,128,384]{2,1,0:T(8,128)(2,1)S(1)}, u32[]{:S(2)}, u32[]{:S(2)}) async-start(bf16[16,128,384]{2,1,0:T(8,128)(2,1)} %shard_map.109), calls=%async_computation.2 | async-start | bytes 3145728 | tf_op jit(solution)/shard_map/all_to_all | solution.py:23
  89.8 33.8 %all-to-all-start.3 = ((bf16[16,160,384]{2,1,0:T(8,128)(2,1)}), bf16[16,160,384]{2,1,0:T(8,128)(2,1)S(1)}, u32[]{:S(2)}, u32[]{:S(2)}) async-start(bf16[16,160,384]{2,1,0:T(8,128)(2,1)} %bitcast.35), calls=%async_computation.3 | async-start | bytes 3932160 | tf_op jit(solution)/shard_map/all_to_all | solution.py:23
  96.9 1.4 %collective-permute-start.7 = (f32[4,16,384]{2,1,0:T(8,128)S(1)}, f32[4,16,384]{2,1,0:T(8,128)S(1)}, u32[]{:S(2)}, u32[]{:S(2)}) collective-permute-start(f32[4,16,384]{2,1,0:T(8,128)S(1)} %get-tuple-element.64), channel_id=1, source_target_pairs={{0,1},{1,0},{2,3},{3,2},{4,5},{5,4},{6,7},{7,6},{8,9},{9,8},{10,11... | collective-permute-start | bytes 294920 | tf_op jit(solution)/shard_map/ppermute | solution.py:378
  98.4 6.1 %collective-permute-start.8 = (f32[16,768]{1,0:T(8,128)S(1)}, f32[16,768]{1,0:T(8,128)S(1)}, u32[]{:S(2)}, u32[]{:S(2)}) collective-permute-start(f32[16,768]{1,0:T(8,128)S(1)} %get-tuple-element.61), channel_id=1, source_target_pairs={{0,16},{16,32},{32,48},{48,0},{1,17},{17,33},{33,49},{49,1},{2,18}... | collective-permute-start | bytes 147464 | tf_op jit(solution)/shard_map/ppermute | solution.py:375
  98.5 6.1 %collective-permute-start.9 = (f32[16,768]{1,0:T(8,128)S(1)}, f32[16,768]{1,0:T(8,128)S(1)}, u32[]{:S(2)}, u32[]{:S(2)}) collective-permute-start(f32[16,768]{1,0:T(8,128)S(1)} %get-tuple-element.60), channel_id=1, source_target_pairs={{0,32},{16,48},{32,0},{48,16},{1,33},{17,49},{33,1},{49,17},{2,34}... | collective-permute-start | bytes 147464 | tf_op jit(solution)/shard_map/ppermute | solution.py:375
  100.7 4.5 %collective-permute-start.10 = (f32[16,768]{1,0:T(8,128)S(1)}, f32[16,768]{1,0:T(8,128)S(1)}, u32[]{:S(2)}, u32[]{:S(2)}) collective-permute-start(f32[16,768]{1,0:T(8,128)S(1)} %get-tuple-element.59), channel_id=1, source_target_pairs={{0,48},{16,0},{32,16},{48,32},{1,49},{17,1},{33,17},{49,33},{2,50}... | collective-permute-start | bytes 147464 | tf_op jit(solution)/shard_map/ppermute | solution.py:375

commit v3 on v2

--- a/solution.py
+++ b/solution.py
@@ -12,9 +12,12 @@
 LOG2E = 1.4426950408889634
 BLOCK = 512
 CHUNK = 256
+SMALL = 1000
 SEQ = ("zl", "x", "c")
+ALL = ("zh", "y", "zl", "x", "c")
 PLANE = ("zh", "zl", "x")
-ALL = ("zh", "y", "zl", "x", "c")
+RING = 4
+HOPS = (1, RING - 1, 2)
 BF16 = jnp.bfloat16
 F32 = jnp.float32
 
@@ -27,8 +30,8 @@
     return pltpu.CompilerParams(vmem_limit_bytes=mib << 20)
 
 
-def cost(flops, nbytes, exps=0):
-    return pl.CostEstimate(flops=flops // 1000, bytes_accessed=nbytes // 1000, transcendentals=exps // 1000)
+def cost(flops, nbytes, part=1):
+    return pl.CostEstimate(flops=flops // part, bytes_accessed=nbytes // part, transcendentals=0)
 
 
 def pack_kernel(slots, *refs):
@@ -44,7 +47,7 @@
             out[h, t:, lanes] = img[j][:, cols]
 
 
-def pack_heads(txt, img, first, slots, heads, step=4):
+def pack_heads(txt, img, first, slots, heads, step=8):
     t, i = txt.shape[0], img.shape[0]
     per = heads // step
 
@@ -67,43 +70,43 @@
     weighted = adv[0, 0] * gate[...]
     out[...] = (weighted * cot[...].astype(F32)).astype(BF16)
     width = here.shape[1]
+    rows = attn.shape[1]
     count = out.shape[1] // width
-    for hop, ref in ((0, here), (1, ahead), (count - 1, behind), (2, across)):
+
+    def part(hop):
         start = lax.rem(y[0, 0] + hop, count) * width
-        ref[:, ref.shape[1] - width :] = out[:, pl.ds(pl.multiple_of(start, width), width)]
-    across[:, : attn.shape[1]] = attn[...]
+        return out[:, pl.ds(pl.multiple_of(start, width), width)]
+
+    here[...] = part(0)
+    for hop, ref in ((1, ahead), (count - 1, behind), (2, across)):
+        ref[:, :rows] = attn[...]
+        ref[:, rows:] = part(hop)
 
 
 def d_image_call(cot, gate, adv, y, attn, count):
     rows, width = cot.shape
+    part = width // count
     vmem = pl.BlockSpec(memory_space=pltpu.VMEM)
     smem = pl.BlockSpec(memory_space=pltpu.SMEM)
-    part = jax.ShapeDtypeStruct((rows, width // count), BF16)
     return pl.pallas_call(
         d_image_kernel,
         in_specs=[vmem, vmem, smem, smem, vmem],
         out_specs=[vmem] * 5,
-        out_shape=[
-            jax.ShapeDtypeStruct((rows, width), BF16),
-            part,
-            part,
-            part,
-            jax.ShapeDtypeStruct((rows, width // count + attn.shape[1]), BF16),
-        ],
-        compiler_params=params(56),
+        out_shape=[jax.ShapeDtypeStruct((rows, width), BF16), jax.ShapeDtypeStruct((rows, part), BF16)]
+        + [jax.ShapeDtypeStruct((rows, attn.shape[1] + part), BF16)] * 3,
+        compiler_params=params(48),
         cost_estimate=cost(2 * rows * width, 6 * rows * width),
     )(cot, gate, adv, y, attn)
 
 
-def partial_kernel(c, a0, a1, a2, d0, d1, d2, merged, keep, low, high):
+def partial_kernel(c, attn, here, m1, m2, m3, keep, low, high):
     block, half = keep.shape
-    at = pl.program_id(0) * block
-    rows = merged.shape[1] - 2 * half
-    lhs = [a0[...], a1[...], a2[...], merged[:, pl.ds(pl.multiple_of(at, block), block)]]
-    rhs = [d0[...], d1[...], d2[...], merged[:, rows:]]
+    rows = m1.shape[1] - 2 * half
+    at = pl.ds(pl.multiple_of(pl.program_id(0) * block, block), block)
+    merged = (m1, m2, m3)
     value = lax.dot_general(
-        jnp.concatenate(lhs, axis=0),
-        jnp.concatenate(rhs, axis=0),
+        jnp.concatenate([attn[...]] + [ref[:, at] for ref in merged], axis=0),
+        jnp.concatenate([here[...]] + [ref[:, rows:] for ref in merged], axis=0),
         (((0,), (0,)), ((), ())),
         preferred_element_type=F32,
     )
@@ -122,23 +125,25 @@
         high[...] = send
 
 
-def partial_call(c, attns, parts, merged):
-    tokens, rows = attns[0].shape
-    cols = parts[0].shape[1]
+def partial_call(c, attn, here, merged):
+    tokens, rows = attn.shape
+    cols = here.shape[1]
     block = 512
-    a_spec = pl.BlockSpec((tokens, block), lambda i: (0, i))
-    d_spec = pl.BlockSpec((tokens, cols), lambda i: (0, 0))
-    m_spec = pl.BlockSpec((tokens, rows + cols), lambda i: (0, 0))
     half = rows // block // 2
-    out = pl.BlockSpec((block, cols // 2), lambda i: (i, 0))
+    out = (block, cols // 2)
     return pl.pallas_call(
         partial_kernel,
         grid=(rows // block,),
-        in_specs=[pl.BlockSpec(memory_space=pltpu.SMEM)] + [a_spec] * 3 + [d_spec] * 3 + [m_spec],
+        in_specs=[
+            pl.BlockSpec(memory_space=pltpu.SMEM),
+            pl.BlockSpec((tokens, block), lambda i: (0, i)),
+            pl.BlockSpec((tokens, cols), lambda i: (0, 0)),
+        ]
+        + [pl.BlockSpec((tokens, rows + cols), lambda i: (0, 0))] * 3,
         out_specs=[
-            out,
-            pl.BlockSpec((block, cols // 2), lambda i: (jnp.minimum(i, half - 1), 0)),
-            pl.BlockSpec((block, cols // 2), lambda i: (jnp.maximum(i - half, 0), 0)),
+            pl.BlockSpec(out, lambda i: (i, 0)),
+            pl.BlockSpec(out, lambda i: (jnp.minimum(i, half - 1), 0)),
+            pl.BlockSpec(out, lambda i: (jnp.maximum(i - half, 0), 0)),
         ],
         out_shape=[
             jax.ShapeDtypeStruct((rows, cols // 2), BF16),
@@ -146,8 +151,8 @@
             jax.ShapeDtypeStruct((rows // 2, cols // 2), BF16),
         ],
         compiler_params=params(40),
-        cost_estimate=cost(8 * tokens * rows * cols, 8 * tokens * (rows + cols) + 2 * rows * cols),
-    )(c, *attns, *parts, merged)
+        cost_estimate=cost(8 * tokens * rows * cols, 8 * tokens * (rows + cols) + 2 * rows * cols, SMALL),
+    )(c, attn, here, *merged)
 
 
 def place_kernel(ring, keep, low, high, out):
@@ -170,9 +175,31 @@
         in_specs=[block] + [pl.BlockSpec((ring * places * rows, cols), lambda h: (0, 0))] * len(got),
         out_specs=pl.BlockSpec((places, ring * rows, cols), lambda h: (h, 0, 0)),
         out_shape=jax.ShapeDtypeStruct((len(got) * places, ring * rows, cols), BF16),
-        compiler_params=params(24),
-        cost_estimate=cost(0, 6 * keep.size),
+        compiler_params=params(40),
+        cost_estimate=cost(0, 6 * keep.size, SMALL),
     )(keep, *got)
+
+
+def ring_kernel(y, *refs):
+    out = refs[-1]
+    count = len(refs) - 1
+    width = refs[0].shape[1]
+    for hop in range(count):
+        start = lax.rem(y[0, 0] + count - hop, count) * width
+        out[:, pl.ds(pl.multiple_of(start, width), width)] = refs[hop][...]
+
+
+def ring_call(y, pieces):
+    rows, width = pieces[0].shape
+    vmem = pl.BlockSpec(memory_space=pltpu.VMEM)
+    return pl.pallas_call(
+        ring_kernel,
+        in_specs=[pl.BlockSpec(memory_space=pltpu.SMEM)] + [vmem] * len(pieces),
+        out_specs=vmem,
+        out_shape=jax.ShapeDtypeStruct((rows, width * len(pieces)), F32),
+        compiler_params=params(16),
+        cost_estimate=cost(0, 8 * rows * width * len(pieces), SMALL),
+    )(y, *pieces)
 
 
 def d_out_kernel(dimg, weight, cot_txt, adv, vt, vi, out):
@@ -207,7 +234,7 @@
         ],
         out_specs=pl.BlockSpec((step, t + rows, 2 * HEAD_SIZE), lambda g: (g, 0, 0)),
         out_shape=jax.ShapeDtypeStruct((heads, t + rows, 2 * HEAD_SIZE), BF16),
-        compiler_params=params(56),
+        compiler_params=params(51),
         cost_estimate=cost(
             2 * rows * weight.size, 2 * (weight.size + dimg.size + 3 * (t + rows) * heads * HEAD_SIZE)
         ),
@@ -256,7 +283,7 @@
         ],
         scratch_shapes=[pltpu.VMEM((n, block), F32)],
         compiler_params=params(56),
-        cost_estimate=cost(2 * n * n * HEAD_SIZE * 2, 2 * n * n, n * n),
+        cost_estimate=cost(2 * n * n * HEAD_SIZE * 2, 2 * n * n, SMALL),
     )(qk, qk)
 
 
@@ -304,7 +331,7 @@
         out_shape=jax.ShapeDtypeStruct((n, 3 * HEAD_SIZE), BF16),
         scratch_shapes=[pltpu.VMEM((n, HEAD_SIZE), F32)] * 2 + [pltpu.VMEM((n, BLOCK), F32)],
         compiler_params=params(56),
-        cost_estimate=cost(2 * n * n * HEAD_SIZE * 8, 2 * n * n),
+        cost_estimate=cost(2 * n * n * HEAD_SIZE * 8, 2 * n * n, SMALL),
     )(exps, inverse, qk, qk, vd, vd)
 
 
@@ -333,30 +360,8 @@
             jax.ShapeDtypeStruct((i, 3 * width), BF16),
         ],
         compiler_params=params(24),
-        cost_estimate=cost(0, 12 * tokens * width),
+        cost_estimate=cost(0, 12 * tokens * width, SMALL),
     )(back)
-
-
-def ring_kernel(y, *refs):
-    out = refs[-1]
-    count = len(refs) - 1
-    width = refs[0].shape[1]
-    for hop in range(count):
-        start = lax.rem(y[0, 0] + count - hop, count) * width
-        out[:, pl.ds(pl.multiple_of(start, width), width)] = refs[hop][...]
-
-
-def ring_call(y, pieces):
-    rows, width = pieces[0].shape
-    vmem = pl.BlockSpec(memory_space=pltpu.VMEM)
-    return pl.pallas_call(
-        ring_kernel,
-        in_specs=[pl.BlockSpec(memory_space=pltpu.SMEM)] + [vmem] * len(pieces),
-        out_specs=vmem,
-        out_shape=jax.ShapeDtypeStruct((rows, width * len(pieces)), F32),
-        compiler_params=params(16),
-        cost_estimate=cost(0, 8 * rows * width * len(pieces)),
-    )(y, *pieces)
 
 
 def per_device(qkv_txt, qkv_img, attn_img, cot_txt, cot_img, gate, advantage, proj_weight):
@@ -366,13 +371,12 @@
     heads = width // HEAD_SIZE
     model = cot_img.shape[2]
     adv = advantage[:, None]
-    count = lax.axis_size("y")
-    y = lax.axis_index("y").astype(jnp.int32)
-    c = lax.axis_index("c").astype(jnp.int32)
-    hops = (1, count - 1, 2)
-
-    def shift(array, hop):
-        return lax.ppermute(array, "y", [(i, (i + hop) % count) for i in range(count)])
+    index = lambda axes: lax.axis_index(axes).astype(jnp.int32).reshape(1, 1)
+    y, core = index("y"), index("c")
+
+    def shift(arrays, axes):
+        perms = [[(i, (i + hop) % RING) for i in range(RING)] for hop in HOPS]
+        return [lax.ppermute(array, axes, perm) for array, perm in zip(arrays, perms)]
 
     def swap(array):
         return lax.ppermute(array, "c", [(0, 1), (1, 0)])
@@ -381,9 +385,8 @@
     packed = pack_heads(txt, img, 0, 2, heads)
     qk = exchange(packed, SEQ)
     cot, attn, packed = lax.optimization_barrier((cot_img[0], attn, packed))
-    attns = [shift(attn, hop) for hop in hops[:2]]
-    d_image, here, *parts = d_image_call(cot, gate, adv, y.reshape(1, 1), attn, count)
-    *parts, merged = [shift(part, hop) for hop, part in zip(hops, parts)]
+    d_image, here, *merged = d_image_call(cot, gate, adv, y, attn, RING)
+    merged = shift(merged, "y")
     vd = d_out_call(d_image, proj_weight, cot_txt[0], adv, txt, img, heads)
     vd, qk = lax.optimization_barrier((vd, qk))
     vd = exchange(vd, SEQ)
@@ -391,16 +394,14 @@
     n = heads * tokens
     qk = qk.reshape(n, 2 * HEAD_SIZE)
     exps, inverse = exps_call(qk)
-    attn, attns, here, parts, merged, inverse = lax.optimization_barrier(
-        (attn, attns, here, parts, merged, inverse)
-    )
-    keep, *send = partial_call(c.reshape(1, 1), [attn, *attns], [here, *parts], merged)
-    got = [swap(part) for part in send]
+    attn, here, merged, inverse = lax.optimization_barrier((attn, here, merged, inverse))
+    keep, low, high = partial_call(core, attn, here, merged)
+    low, high = swap(low), swap(high)
 
     devices = lax.axis_size(ALL)
     rows = width // devices
     cols = keep.shape[1]
-    product = place_call(keep, got, count, lax.axis_size(PLANE) // 2, 2 * rows)
+    product = place_call(keep, [low, high], RING, lax.axis_size(PLANE) // 2, 2 * rows)
     product = exchange(product, PLANE)
 
     vd = vd.reshape(n, 2 * HEAD_SIZE)
@@ -409,14 +410,14 @@
     back = exchange(grads, SEQ)
 
     total = jnp.sum(product.astype(F32), axis=0) * (1.0 / (img.shape[0] * devices))
-    total = total.reshape(count, 2, rows, cols)
+    total = total.reshape(RING, 2, rows, cols)
+    c, y = core[0, 0], y[0, 0]
     own = lax.dynamic_index_in_dim(total, c, 1, keepdims=False)
     other = swap(lax.dynamic_index_in_dim(total, 1 - c, 1, keepdims=False))
     wide = jnp.where(c == 0, jnp.concatenate([own, other], -1), jnp.concatenate([other, own], -1))
-    pick = lambda hop: lax.dynamic_index_in_dim(wide, (y + hop) % count, 0, keepdims=False)
-    placed = [pick(0)] + [shift(pick(hop), hop) for hop in hops]
-    order = [placed[0], placed[1], placed[3], placed[2]]
-    grad_proj = ring_call(y.reshape(1, 1), order)
+    pick = lambda hop: lax.dynamic_index_in_dim(wide, (y + hop) % RING, 0, keepdims=False)
+    behind, ahead, across = shift([pick(hop) for hop in HOPS], "y")
+    grad_proj = ring_call(y.reshape(1, 1), [pick(0), behind, across, ahead])
     back, grad_proj = lax.optimization_barrier((back, grad_proj))
 
     dqkv_txt, dqkv_img = unpack_call(back, txt.shape[0])

time: 126 us -> 122 us (0.968)
  starting transfers between devices: 41.1 us -> 38.1 us
  Pallas kernels: 57.3 us -> 54.4 us
  waiting for transfers between devices: 25.8 us -> 27.3 us
    ppermute x8 -> x6, starting transfers between devices: 13.4 us -> 9.84 us  [shift(): lax.ppermute(array, axes, perm)]
    pallas_call x1, Pallas kernels: 3.64 us -> 2.3 us  [pack_heads(): pl.pallas_call(functools.partial(pack_kernel, slots), grid=(per,), in_spe...]
    ppermute x8 -> x6, waiting for transfers between devices: 3.12 us -> 4.2 us  [shift(): lax.ppermute(array, axes, perm)]
  transfers between devices with their start and end apart: 15 -> 13, of which waited for: 7 -> 10; matrix products, arithmetic and copies ran while one was open for 0% -> 0% of each run, Pallas kernels for 41% -> 41%
where the time goes in v3:
time: 122 us; the launch traced here: 121 us
  Pallas kernels  54.4 us (45%)
  starting transfers between devices  38.1 us (31%)
  waiting for transfers between devices  27.3 us (22%)
  between operations  1.39 us (1%)
    all_to_all x4, starting transfers between devices, exchange(): return lax.all_to_all(array, axes, split_axis=0, concat_axis=0, tiled=True)  27.4 us
    pallas_call x1, Pallas kernels, grads_call(): pl.pallas_call(grads_kernel, grid=(n // BLOCK,), in_specs=[pl.BlockSpec((...  21 us
    all_to_all x4, waiting for transfers between devices, exchange(): return lax.all_to_all(array, axes, split_axis=0, concat_axis=0, tiled=True)  19 us
    pallas_call x1, Pallas kernels, exps_call(): pl.pallas_call(exps_kernel, grid=(n // block,), in_specs=[pl.BlockSpec((b...  13.7 us
    ppermute x6, starting transfers between devices, shift(): lax.ppermute(array, axes, perm)  9.84 us
    pallas_call x1, Pallas kernels, d_out_call(): pl.pallas_call(d_out_kernel, grid=(per,), in_specs=[pl.BlockSpec((rows, m...  8.43 us
    ppermute x6, waiting for transfers between devices, shift(): lax.ppermute(array, axes, perm)  4.2 us
    ppermute x3, waiting for transfers between devices, swap(): return lax.ppermute(array, 'c', [(0, 1), (1, 0)])  4.05 us
  transfers between devices with their start and end apart: 13, of which 10 were waited for; matrix products, arithmetic and copies ran while one was open for 0% of the time, Pallas kernels for 41%

profile of v3, /device:TPU:2, one launch (start us, length us, event | category | flops | bytes accessed | tf_op | source)
XLA Modules:
  0.0 121.4 jit_solution(14518511056695015102)
XLA Ops:
  0.6 2.3 %shard_map.103 = bf16[16,160,256]{2,1,0:T(8,128)(2,1)} custom-call(bf16[32,6144]{1,0:T(8,128)(2,1)} %bitcast.28, bf16[32,6144]{1,0:T(8,128)(2,1)} %bitcast.29, bf16[128,6144]{1,0:T(8,128)(2,1)} %bitcast.35, bf16[128,6144]{1,0:T(8,128)(2,1)} %bitcast.36), custom_call_target="tpu_custom_call" | custom-call | bytes 2621440 | tf_op jit(solution)/shard_map/pallas_call | solution.py:58
  2.9 0.0 copy-start.1
  2.9 0.0 copy-start.2
  2.9 0.0 copy-start.4
  2.9 0.0 copy-start
  3.0 0.0 copy-start.3
  3.0 6.3 %all-to-all-start = ((bf16[16,160,256]{2,1,0:T(8,128)(2,1)}), bf16[16,160,256]{2,1,0:T(8,128)(2,1)}, u32[]{:S(2)}, u32[]{:S(2)}) async-start(bf16[16,160,256]{2,1,0:T(8,128)(2,1)} %shard_map.103), calls=%async_computation | async-start | bytes 2621440 | tf_op jit(solution)/shard_map/all_to_all | solution.py:26
  10.0 0.0 copy-done.1
  10.0 0.0 copy-done.2
  10.0 0.0 copy-done.4
  10.0 1.8 %shard_map.104 = (bf16[128,3072]{1,0:T(8,128)(2,1)S(1)}, bf16[128,768]{1,0:T(8,128)(2,1)S(1)}, bf16[128,2816]{1,0:T(8,128)(2,1)}, bf16[128,2816]{1,0:T(8,128)(2,1)}, bf16[128,2816]{1,0:T(8,128)(2,1)}) custom-call(bf16[128,3072]{1,0:T(8,128)(2,1)S(1)} %bitcast.33, f32[1,3072]{1,0:T(1,128)S(1)} %copy-done.4, f32[1,1]{1,0:T(1,128)} %bitcast.26.adv, ...), custom_call_target="tpu_custom_call" | custom-call | flops 786432 | bytes 2359296 | tf_op jit(solution)/shard_map/pallas_call | solution.py:91
  11.8 1.6 %collective-permute-start = (bf16[128,2816]{1,0:T(8,128)(2,1)}, bf16[128,2816]{1,0:T(8,128)(2,1)S(1)}, u32[]{:S(2)}, u32[]{:S(2)}) collective-permute-start(bf16[128,2816]{1,0:T(8,128)(2,1)} %get-tuple-element.35), channel_id=1, source_target_pairs={{0,16},{16,32},{32,48},{48,0},{1,17},{17,33},{33,49},{49,1},{2,18}... | collective-permute-start | bytes 2162696 | tf_op jit(solution)/shard_map/ppermute | solution.py:379
  13.4 1.7 %collective-permute-start.1 = (bf16[128,2816]{1,0:T(8,128)(2,1)}, bf16[128,2816]{1,0:T(8,128)(2,1)S(1)}, u32[]{:S(2)}, u32[]{:S(2)}) collective-permute-start(bf16[128,2816]{1,0:T(8,128)(2,1)} %get-tuple-element.36), channel_id=1, source_target_pairs={{0,48},{16,0},{32,16},{48,32},{1,49},{17,1},{33,17},{49,33},{2,50}... | collective-permute-start | bytes 2162696 | tf_op jit(solution)/shard_map/ppermute | solution.py:379
  15.0 2.0 %collective-permute-start.2 = (bf16[128,2816]{1,0:T(8,128)(2,1)}, bf16[128,2816]{1,0:T(8,128)(2,1)S(1)}, u32[]{:S(2)}, u32[]{:S(2)}) collective-permute-start(bf16[128,2816]{1,0:T(8,128)(2,1)} %get-tuple-element.37), channel_id=1, source_target_pairs={{0,32},{16,48},{32,0},{48,16},{1,33},{17,49},{33,1},{49,17},{2,34}... | collective-permute-start | bytes 2162696 | tf_op jit(solution)/shard_map/ppermute | solution.py:379
  17.0 0.0 copy-done
  17.0 0.0 copy-done.3
  17.0 8.4 %shard_map.105 = bf16[16,160,256]{2,1,0:T(8,128)(2,1)} custom-call(bf16[128,3072]{1,0:T(8,128)(2,1)S(1)} %get-tuple-element.31.dimg, bf16[2048,3072]{1,0:T(8,128)(2,1)} %weight.1, bf16[32,2048]{1,0:T(8,128)(2,1)S(1)} %bitcast.34, f32[1,1]{1,0:T(1,128)} %bitcast.27.adv, bf16[32,6144]{1,0:T(8,128)(2,1)S(1)} %bitcast.30, bf16[128,6144]{1,0:T(8,128)(2,1)} %bitcast.37), custom_call_target="tpu_custom_call" | custom-call | flops 1610612736 | bytes 15335424 | tf_op jit(solution)/shard_map/pallas_call | solution.py:224
  25.5 1.1 all-to-all-done
  26.6 6.4 %all-to-all-start.1 = ((bf16[16,160,256]{2,1,0:T(8,128)(2,1)}), bf16[16,160,256]{2,1,0:T(8,128)(2,1)}, u32[]{:S(2)}, u32[]{:S(2)}) async-start(bf16[16,160,256]{2,1,0:T(8,128)(2,1)} %shard_map.105), calls=%async_computation.1 | async-start | bytes 2621440 | tf_op jit(solution)/shard_map/all_to_all | solution.py:26
  32.9 13.7 %shard_map.106 = (bf16[2560,2560]{1,0:T(8,128)(2,1)}, f32[2560,128]{1,0:T(8,128)}) custom-call(bf16[2560,256]{1,0:T(8,128)(2,1)} %bitcast.7.q.k, bf16[2560,256]{1,0:T(8,128)(2,1)} %bitcast.7.q.k), custom_call_target="tpu_custom_call" | custom-call | flops 3355443 | bytes 13107 | tf_op jit(solution)/shard_map/pallas_call | solution.py:269
  46.7 0.0 collective-permute-done.m1
  46.7 0.0 collective-permute-done.1.m2
  46.7 1.4 %collective-permute-done.2.m3 = bf16[128,2816]{1,0:T(8,128)(2,1)S(1)} collective-permute-done((bf16[128,2816]{1,0:T(8,128)(2,1)}, bf16[128,2816]{1,0:T(8,128)(2,1)S(1)}, u32[]{:S(2)}, u32[]{:S(2)}) %collective-permute-start.2) | collective-permute-done | bytes 720928 | tf_op jit(solution)/shard_map/ppermute | solution.py:379
  48.1 2.8 %shard_map.108 = (bf16[2048,384]{1,0:T(8,128)(2,1)S(1)}, bf16[1024,384]{1,0:T(8,128)(2,1)S(1)}, bf16[1024,384]{1,0:T(8,128)(2,1)S(1)}) custom-call(s32[1,1]{1,0:T(1,128)} %bitcast.10.c, bf16[128,2048]{1,0:T(8,128)(2,1)S(1)} %bitcast.32, bf16[128,768]{1,0:T(8,128)(2,1)S(1)} %get-tuple-element.42.here, bf16[128,2816]{1,0:T(8,128)(2,1)S(1)} %collective-permute-done.m1, ...), custom_call_target="tpu_custom_call" | custom-call | flops 1610612 | bytes 6029 | tf_op jit(solution)/shard_map/pallas_call | solution.py:134
  50.9 0.1 collective-permute-start.3
  51.0 0.5 collective-permute-start.4
  51.5 1.8 %collective-permute-done.3.low = bf16[1024,384]{1,0:T(8,128)(2,1)S(1)} collective-permute-done((bf16[1024,384]{1,0:T(8,128)(2,1)S(1)}, bf16[1024,384]{1,0:T(8,128)(2,1)S(1)}, u32[]{:S(2)}, u32[]{:S(2)}) %collective-permute-start.3) | collective-permute-done | bytes 786464 | tf_op jit(solution)/shard_map/ppermute | solution.py:382
  53.2 1.1 collective-permute-done.4.high
  54.4 1.4 %shard_map.109 = bf16[16,128,384]{2,1,0:T(8,128)(2,1)} custom-call(bf16[2048,384]{1,0:T(8,128)(2,1)S(1)} %get-tuple-element.46.keep, bf16[1024,384]{1,0:T(8,128)(2,1)S(1)} %collective-permute-done.3.low, bf16[1024,384]{1,0:T(8,128)(2,1)S(1)} %collective-permute-done.4.high), custom_call_target="tpu_custom_call" | custom-call | bytes 4718 | tf_op jit(solution)/shard_map/pallas_call | solution.py:172
  55.7 0.0 all-to-all-done.1
  55.7 7.8 %all-to-all-start.2 = ((bf16[16,128,384]{2,1,0:T(8,128)(2,1)}), bf16[16,128,384]{2,1,0:T(8,128)(2,1)S(1)}, u32[]{:S(2)}, u32[]{:S(2)}) async-start(bf16[16,128,384]{2,1,0:T(8,128)(2,1)} %shard_map.109), calls=%async_computation.2 | async-start | bytes 3145728 | tf_op jit(solution)/shard_map/all_to_all | solution.py:26
  63.6 21.0 %shard_map.107 = bf16[2560,384]{1,0:T(8,128)(2,1)} custom-call(bf16[2560,2560]{1,0:T(8,128)(2,1)} %get-tuple-element.33.e, f32[2560,128]{1,0:T(8,128)} %get-tuple-element.39.inv, bf16[2560,256]{1,0:T(8,128)(2,1)} %bitcast.7.q.k, bf16[2560,256]{1,0:T(8,128)(2,1)} %bitcast.7.q.k, bf16[2560,256]{1,0:T(8,128)(2,1)} %bitcast.8.v.d, bf16[2560,256]{1,0:T(8,128)(2,1)} %bitcast.8.v.d), custom_call_target="tpu_custom_call" | custom-call | flops 13421772 | bytes 13107 | tf_op jit(solution)/shard_map/pallas_call | solution.py:326
  84.6 0.8 all-to-all-done.2
  85.4 6.9 %all-to-all-start.3 = ((bf16[16,160,384]{2,1,0:T(8,128)(2,1)}), bf16[16,160,384]{2,1,0:T(8,128)(2,1)S(1)}, u32[]{:S(2)}, u32[]{:S(2)}) async-start(bf16[16,160,384]{2,1,0:T(8,128)(2,1)} %bitcast.38), calls=%async_computation.3 | async-start | bytes 3932160 | tf_op jit(solution)/shard_map/all_to_all | solution.py:26
  92.2 0.2 convert_reduce_fusion
  92.5 0.2 collective-permute-start.5
  92.7 1.2 collective-permute-done.5
  93.9 1.2 collective-permute-start.6
  95.2 2.1 %collective-permute-start.7 = (f32[16,768]{1,0:T(8,128)S(1)}, f32[16,768]{1,0:T(8,128)S(1)}, u32[]{:S(2)}, u32[]{:S(2)}) collective-permute-start(f32[16,768]{1,0:T(8,128)S(1)} %get-tuple-element.56), channel_id=1, source_target_pairs={{0,32},{16,48},{32,0},{48,16},{1,33},{17,49},{33,1},{49,17},{2,34}... | collective-permute-start | bytes 147464 | tf_op jit(solution)/shard_map/ppermute | solution.py:379
  97.3 1.3 %collective-permute-start.8 = (f32[16,768]{1,0:T(8,128)S(1)}, f32[16,768]{1,0:T(8,128)S(1)}, u32[]{:S(2)}, u32[]{:S(2)}) collective-permute-start(f32[16,768]{1,0:T(8,128)S(1)} %get-tuple-element.55), channel_id=1, source_target_pairs={{0,48},{16,0},{32,16},{48,32},{1,49},{17,1},{33,17},{49,33},{2,50}... | collective-permute-start | bytes 147464 | tf_op jit(solution)/shard_map/ppermute | solution.py:379
  98.6 0.9 collective-permute-done.6.refs_1_
  99.5 1.2 %collective-permute-done.7.refs_2_ = f32[16,768]{1,0:T(8,128)S(1)} collective-permute-done((f32[16,768]{1,0:T(8,128)S(1)}, f32[16,768]{1,0:T(8,128)S(1)}, u32[]{:S(2)}, u32[]{:S(2)}) %collective-permute-start.7) | collective-permute-done | bytes 49184 | tf_op jit(solution)/shard_map/ppermute | solution.py:379
  100.8 0.6 collective-permute-done.8.refs_3_
  101.3 0.7 shard_map.110
  102.0 17.1 %all-to-all-done.3.back = bf16[16,160,384]{2,1,0:T(8,128)(2,1)S(1)} async-done(((bf16[16,160,384]{2,1,0:T(8,128)(2,1)}), bf16[16,160,384]{2,1,0:T(8,128)(2,1)S(1)}, u32[]{:S(2)}, u32[]{:S(2)}) %all-to-all-start.3) | async-done | bytes 1966112 | tf_op jit(solution)/shard_map/all_to_all | solution.py:26
  119.2 2.3 %shard_map.111 = (bf16[32,6144]{1,0:T(8,128)(2,1)}, bf16[128,6144]{1,0:T(8,128)(2,1)}) custom-call(bf16[16,160,384]{2,1,0:T(8,128)(2,1)S(1)} %all-to-all-done.3.back), custom_call_target="tpu_custom_call" | custom-call | bytes 3932 | tf_op jit(solution)/shard_map/pallas_call | solution.py:350
  (4 shorter events, 0.1 us)
Async XLA Ops:
  2.9 7.0 %copy-start.1 = (bf16[1,128,2048]{2,1,0:T(8,128)(2,1)S(1)}, bf16[1,128,2048]{2,1,0:T(8,128)(2,1)}, u32[]{:S(2)}) copy-start(bf16[1,128,2048]{2,1,0:T(8,128)(2,1)} %param.10) | copy-start | bytes 1572868
  2.9 7.0 %copy-start.2 = (bf16[1,128,3072]{2,1,0:T(8,128)(2,1)S(1)}, bf16[1,128,3072]{2,1,0:T(8,128)(2,1)}, u32[]{:S(2)}) copy-start(bf16[1,128,3072]{2,1,0:T(8,128)(2,1)} %param.12) | copy-start | bytes 2359300
  2.9 7.1 %copy-start.4 = (f32[1,3072]{1,0:T(1,128)S(1)}, f32[1,3072]{1,0:T(1,128)}, u32[]{:S(2)}) copy-start(f32[1,3072]{1,0:T(1,128)} %gate.1) | copy-start | bytes 36868
  2.9 14.1 %copy-start = (bf16[1,32,6144]{2,1,0:T(8,128)(2,1)S(1)}, bf16[1,32,6144]{2,1,0:T(8,128)(2,1)}, u32[]{:S(2)}) copy-start(bf16[1,32,6144]{2,1,0:T(8,128)(2,1)} %param.8) | copy-start | bytes 1179652
  3.0 14.1 %copy-start.3 = (bf16[1,32,2048]{2,1,0:T(8,128)(2,1)S(1)}, bf16[1,32,2048]{2,1,0:T(8,128)(2,1)}, u32[]{:S(2)}) copy-start(bf16[1,32,2048]{2,1,0:T(8,128)(2,1)} %param.11) | copy-start | bytes 393220
  3.0 23.6 %all-to-all-start = ((bf16[16,160,256]{2,1,0:T(8,128)(2,1)}), bf16[16,160,256]{2,1,0:T(8,128)(2,1)}, u32[]{:S(2)}, u32[]{:S(2)}) async-start(bf16[16,160,256]{2,1,0:T(8,128)(2,1)} %shard_map.103), calls=%async_computation | async-start | bytes 2621440 | tf_op jit(solution)/shard_map/all_to_all | solution.py:26
  11.8 34.9 %collective-permute-start = (bf16[128,2816]{1,0:T(8,128)(2,1)}, bf16[128,2816]{1,0:T(8,128)(2,1)S(1)}, u32[]{:S(2)}, u32[]{:S(2)}) collective-permute-start(bf16[128,2816]{1,0:T(8,128)(2,1)} %get-tuple-element.35), channel_id=1, source_target_pairs={{0,16},{16,32},{32,48},{48,0},{1,17},{17,33},{33,49},{49,1},{2,18}... | collective-permute-start | bytes 2162696 | tf_op jit(solution)/shard_map/ppermute | solution.py:379
  13.4 33.3 %collective-permute-start.1 = (bf16[128,2816]{1,0:T(8,128)(2,1)}, bf16[128,2816]{1,0:T(8,128)(2,1)S(1)}, u32[]{:S(2)}, u32[]{:S(2)}) collective-permute-start(bf16[128,2816]{1,0:T(8,128)(2,1)} %get-tuple-element.36), channel_id=1, source_target_pairs={{0,48},{16,0},{32,16},{48,32},{1,49},{17,1},{33,17},{49,33},{2,50}... | collective-permute-start | bytes 2162696 | tf_op jit(solution)/shard_map/ppermute | solution.py:379
  15.0 33.1 %collective-permute-start.2 = (bf16[128,2816]{1,0:T(8,128)(2,1)}, bf16[128,2816]{1,0:T(8,128)(2,1)S(1)}, u32[]{:S(2)}, u32[]{:S(2)}) collective-permute-start(bf16[128,2816]{1,0:T(8,128)(2,1)} %get-tuple-element.37), channel_id=1, source_target_pairs={{0,32},{16,48},{32,0},{48,16},{1,33},{17,49},{33,1},{49,17},{2,34}... | collective-permute-start | bytes 2162696 | tf_op jit(solution)/shard_map/ppermute | solution.py:379
  26.6 29.2 %all-to-all-start.1 = ((bf16[16,160,256]{2,1,0:T(8,128)(2,1)}), bf16[16,160,256]{2,1,0:T(8,128)(2,1)}, u32[]{:S(2)}, u32[]{:S(2)}) async-start(bf16[16,160,256]{2,1,0:T(8,128)(2,1)} %shard_map.105), calls=%async_computation.1 | async-start | bytes 2621440 | tf_op jit(solution)/shard_map/all_to_all | solution.py:26
  50.9 2.4 %collective-permute-start.3 = (bf16[1024,384]{1,0:T(8,128)(2,1)S(1)}, bf16[1024,384]{1,0:T(8,128)(2,1)S(1)}, u32[]{:S(2)}, u32[]{:S(2)}) collective-permute-start(bf16[1024,384]{1,0:T(8,128)(2,1)S(1)} %get-tuple-element.47), channel_id=1, source_target_pairs={{0,1},{1,0},{2,3},{3,2},{4,5},{5,4},{6,7},{7,6},{8,9},{9,8},{10,11... | collective-permute-start | bytes 2359304 | tf_op jit(solution)/shard_map/ppermute | solution.py:382
  51.0 3.4 %collective-permute-start.4 = (bf16[1024,384]{1,0:T(8,128)(2,1)S(1)}, bf16[1024,384]{1,0:T(8,128)(2,1)S(1)}, u32[]{:S(2)}, u32[]{:S(2)}) collective-permute-start(bf16[1024,384]{1,0:T(8,128)(2,1)S(1)} %get-tuple-element.48), channel_id=1, source_target_pairs={{0,1},{1,0},{2,3},{3,2},{4,5},{5,4},{6,7},{7,6},{8,9},{9,8},{10,11... | collective-permute-start | bytes 2359304 | tf_op jit(solution)/shard_map/ppermute | solution.py:382
  55.7 29.7 %all-to-all-start.2 = ((bf16[16,128,384]{2,1,0:T(8,128)(2,1)}), bf16[16,128,384]{2,1,0:T(8,128)(2,1)S(1)}, u32[]{:S(2)}, u32[]{:S(2)}) async-start(bf16[16,128,384]{2,1,0:T(8,128)(2,1)} %shard_map.109), calls=%async_computation.2 | async-start | bytes 3145728 | tf_op jit(solution)/shard_map/all_to_all | solution.py:26
  85.4 33.8 %all-to-all-start.3 = ((bf16[16,160,384]{2,1,0:T(8,128)(2,1)}), bf16[16,160,384]{2,1,0:T(8,128)(2,1)S(1)}, u32[]{:S(2)}, u32[]{:S(2)}) async-start(bf16[16,160,384]{2,1,0:T(8,128)(2,1)} %bitcast.38), calls=%async_computation.3 | async-start | bytes 3932160 | tf_op jit(solution)/shard_map/all_to_all | solution.py:26
  92.5 1.4 %collective-permute-start.5 = (f32[4,16,384]{2,1,0:T(8,128)S(1)}, f32[4,16,384]{2,1,0:T(8,128)S(1)}, u32[]{:S(2)}, u32[]{:S(2)}) collective-permute-start(f32[4,16,384]{2,1,0:T(8,128)S(1)} %get-tuple-element.60), channel_id=1, source_target_pairs={{0,1},{1,0},{2,3},{3,2},{4,5},{5,4},{6,7},{7,6},{8,9},{9,8},{10,11... | collective-permute-start | bytes 294920 | tf_op jit(solution)/shard_map/ppermute | solution.py:382
  93.9 5.6 %collective-permute-start.6 = (f32[16,768]{1,0:T(8,128)S(1)}, f32[16,768]{1,0:T(8,128)S(1)}, u32[]{:S(2)}, u32[]{:S(2)}) collective-permute-start(f32[16,768]{1,0:T(8,128)S(1)} %get-tuple-element.57), channel_id=1, source_target_pairs={{0,16},{16,32},{32,48},{48,0},{1,17},{17,33},{33,49},{49,1},{2,18}... | collective-permute-start | bytes 147464 | tf_op jit(solution)/shard_map/ppermute | solution.py:379
  95.2 5.6 %collective-permute-start.7 = (f32[16,768]{1,0:T(8,128)S(1)}, f32[16,768]{1,0:T(8,128)S(1)}, u32[]{:S(2)}, u32[]{:S(2)}) collective-permute-start(f32[16,768]{1,0:T(8,128)S(1)} %get-tuple-element.56), channel_id=1, source_target_pairs={{0,32},{16,48},{32,0},{48,16},{1,33},{17,49},{33,1},{49,17},{2,34}... | collective-permute-start | bytes 147464 | tf_op jit(solution)/shard_map/ppermute | solution.py:379
  97.3 4.1 %collective-permute-start.8 = (f32[16,768]{1,0:T(8,128)S(1)}, f32[16,768]{1,0:T(8,128)S(1)}, u32[]{:S(2)}, u32[]{:S(2)}) collective-permute-start(f32[16,768]{1,0:T(8,128)S(1)} %get-tuple-element.55), channel_id=1, source_target_pairs={{0,48},{16,0},{32,16},{48,32},{1,49},{17,1},{33,17},{49,33},{2,50}... | collective-permute-start | bytes 147464 | tf_op jit(solution)/shard_map/ppermute | solution.py:379

commit v4 on v3

--- a/solution.py
+++ b/solution.py
@@ -13,6 +13,7 @@
 BLOCK = 512
 CHUNK = 256
 SMALL = 1000
+SAFE = 2.0**40
 SEQ = ("zl", "x", "c")
 ALL = ("zh", "y", "zl", "x", "c")
 PLANE = ("zh", "zl", "x")
@@ -245,22 +246,32 @@
     return combine(array.reshape(-1, 8, array.shape[1]), axis=0)
 
 
-def exps_kernel(q, k, e_out, inv_out, scores):
+def exps_kernel(q, k, e_out, inv_out):
     chunks = [slice(at, at + CHUNK) for at in range(0, k.shape[0], CHUNK)]
-    top = None
-    for rows in chunks:
-        part = lax.dot_general(k[rows], q[...], (((1,), (1,)), ((), ())), preferred_element_type=F32)
-        scores[rows] = part
-        part = fold(part, jnp.max)
-        top = part if top is None else jnp.maximum(top, part)
-    top = jnp.max(top, axis=0, keepdims=True)
-    total = jnp.zeros((8, top.shape[1]), F32)
-    for rows in chunks:
-        low = jnp.exp2((scores[rows] - top) * (SCALE * LOG2E)).astype(BF16)
-        e_out[rows] = low
-        total += fold(low.astype(F32), jnp.sum)
-    inverse = 1.0 / jnp.sum(total, axis=0, keepdims=True)
-    inv_out[...] = jnp.transpose(jnp.broadcast_to(inverse, (HEAD_SIZE, inverse.shape[1])))
+
+    def scores(rows):
+        return lax.dot_general(k[rows], q[...], (((1,), (1,)), ((), ())), preferred_element_type=F32)
+
+    def fill(top):
+        total = jnp.zeros((8, top.shape[1]), F32)
+        top = top * (SCALE * LOG2E)
+        for rows in chunks:
+            low = jnp.exp2(scores(rows) * (SCALE * LOG2E) - top).astype(BF16)
+            e_out[rows] = low
+            total += fold(low.astype(F32), jnp.sum)
+        total = jnp.sum(total, axis=0, keepdims=True)
+        inv_out[...] = jnp.transpose(jnp.broadcast_to(1.0 / total, (HEAD_SIZE, total.shape[1])))
+        return total
+
+    total = fill(jnp.max(scores(chunks[0]), axis=0, keepdims=True))
+
+    @pl.when(jnp.logical_not(jnp.max(total) < SAFE))
+    def _():
+        top = None
+        for rows in chunks:
+            part = fold(scores(rows), jnp.max)
+            top = part if top is None else jnp.maximum(top, part)
+        fill(jnp.max(top, axis=0, keepdims=True))
 
 
 def exps_call(qk):
@@ -281,7 +292,6 @@
             jax.ShapeDtypeStruct((n, n), BF16),
             jax.ShapeDtypeStruct((n, HEAD_SIZE), F32),
         ],
-        scratch_shapes=[pltpu.VMEM((n, block), F32)],
         compiler_params=params(56),
         cost_estimate=cost(2 * n * n * HEAD_SIZE * 2, 2 * n * n, SMALL),
     )(qk, qk)

time: 122 us -> 125 us (1.025)
  Pallas kernels: 54.4 us -> 58.4 us
  waiting for transfers between devices: 27.3 us -> 24.6 us
  starting transfers between devices: 38.1 us -> 39.5 us
    pallas_call x1, Pallas kernels: 13.7 us -> 17.7 us  [exps_call(): pl.pallas_call(exps_kernel, grid=(n // block,), in_specs=[pl.BlockSpec((b...]
    ppermute x6, waiting for transfers between devices: 4.2 us -> 2.75 us  [shift(): lax.ppermute(array, axes, perm)]
    ppermute x6, starting transfers between devices: 9.84 us -> 11.1 us  [shift(): lax.ppermute(array, axes, perm)]
  transfers between devices with their start and end apart: 13 -> 13, of which waited for: 10 -> 8; matrix products, arithmetic and copies ran while one was open for 0% -> 0% of each run, Pallas kernels for 41% -> 43%
where the time goes in v4:
time: 125 us; the launch traced here: 124 us
  Pallas kernels  58.4 us (47%)
  starting transfers between devices  39.5 us (32%)
  waiting for transfers between devices  24.6 us (20%)
  between operations  1.39 us (1%)
    all_to_all x4, starting transfers between devices, exchange(): return lax.all_to_all(array, axes, split_axis=0, concat_axis=0, tiled=True)  27.5 us
    pallas_call x1, Pallas kernels, grads_call(): pl.pallas_call(grads_kernel, grid=(n // BLOCK,), in_specs=[pl.BlockSpec((...  21 us
    all_to_all x4, waiting for transfers between devices, exchange(): return lax.all_to_all(array, axes, split_axis=0, concat_axis=0, tiled=True)  17.8 us
    pallas_call x1, Pallas kernels, exps_call(): pl.pallas_call(exps_kernel, grid=(n // block,), in_specs=[pl.BlockSpec((b...  17.7 us
    ppermute x6, starting transfers between devices, shift(): lax.ppermute(array, axes, perm)  11.1 us
    pallas_call x1, Pallas kernels, d_out_call(): pl.pallas_call(d_out_kernel, grid=(per,), in_specs=[pl.BlockSpec((rows, m...  8.43 us
    ppermute x3, waiting for transfers between devices, swap(): return lax.ppermute(array, 'c', [(0, 1), (1, 0)])  4.05 us
    pallas_call x1, Pallas kernels, partial_call(): pl.pallas_call(partial_kernel, grid=(rows // block,), in_specs=[pl.BlockS...  2.78 us
  transfers between devices with their start and end apart: 13, of which 8 were waited for; matrix products, arithmetic and copies ran while one was open for 0% of the time, Pallas kernels for 43%

profile of v4, /device:TPU:2, one launch (start us, length us, event | category | flops | bytes accessed | tf_op | source)
XLA Modules:
  0.0 124.1 jit_solution(6719217962961835744)
XLA Ops:
  0.6 2.3 %shard_map.103 = bf16[16,160,256]{2,1,0:T(8,128)(2,1)} custom-call(bf16[32,6144]{1,0:T(8,128)(2,1)} %bitcast.28, bf16[32,6144]{1,0:T(8,128)(2,1)} %bitcast.29, bf16[128,6144]{1,0:T(8,128)(2,1)} %bitcast.35, bf16[128,6144]{1,0:T(8,128)(2,1)} %bitcast.36), custom_call_target="tpu_custom_call" | custom-call | bytes 2621440 | tf_op jit(solution)/shard_map/pallas_call | solution.py:59
  2.9 0.0 copy-start.1
  2.9 0.0 copy-start.2
  2.9 0.0 copy-start.4
  2.9 0.0 copy-start
  3.0 0.0 copy-start.3
  3.0 6.3 %all-to-all-start = ((bf16[16,160,256]{2,1,0:T(8,128)(2,1)}), bf16[16,160,256]{2,1,0:T(8,128)(2,1)}, u32[]{:S(2)}, u32[]{:S(2)}) async-start(bf16[16,160,256]{2,1,0:T(8,128)(2,1)} %shard_map.103), calls=%async_computation | async-start | bytes 2621440 | tf_op jit(solution)/shard_map/all_to_all | solution.py:27
  10.0 0.0 copy-done.1
  10.0 0.0 copy-done.2
  10.0 0.0 copy-done.4
  10.0 1.8 %shard_map.104 = (bf16[128,3072]{1,0:T(8,128)(2,1)S(1)}, bf16[128,768]{1,0:T(8,128)(2,1)S(1)}, bf16[128,2816]{1,0:T(8,128)(2,1)}, bf16[128,2816]{1,0:T(8,128)(2,1)}, bf16[128,2816]{1,0:T(8,128)(2,1)}) custom-call(bf16[128,3072]{1,0:T(8,128)(2,1)S(1)} %bitcast.33, f32[1,3072]{1,0:T(1,128)S(1)} %copy-done.4, f32[1,1]{1,0:T(1,128)} %bitcast.26.adv, ...), custom_call_target="tpu_custom_call" | custom-call | flops 786432 | bytes 2359296 | tf_op jit(solution)/shard_map/pallas_call | solution.py:92
  11.8 1.6 %collective-permute-start = (bf16[128,2816]{1,0:T(8,128)(2,1)}, bf16[128,2816]{1,0:T(8,128)(2,1)S(1)}, u32[]{:S(2)}, u32[]{:S(2)}) collective-permute-start(bf16[128,2816]{1,0:T(8,128)(2,1)} %get-tuple-element.35), channel_id=1, source_target_pairs={{0,16},{16,32},{32,48},{48,0},{1,17},{17,33},{33,49},{49,1},{2,18}... | collective-permute-start | bytes 2162696 | tf_op jit(solution)/shard_map/ppermute | solution.py:389
  13.4 1.7 %collective-permute-start.1 = (bf16[128,2816]{1,0:T(8,128)(2,1)}, bf16[128,2816]{1,0:T(8,128)(2,1)S(1)}, u32[]{:S(2)}, u32[]{:S(2)}) collective-permute-start(bf16[128,2816]{1,0:T(8,128)(2,1)} %get-tuple-element.36), channel_id=1, source_target_pairs={{0,48},{16,0},{32,16},{48,32},{1,49},{17,1},{33,17},{49,33},{2,50}... | collective-permute-start | bytes 2162696 | tf_op jit(solution)/shard_map/ppermute | solution.py:389
  15.0 2.0 %collective-permute-start.2 = (bf16[128,2816]{1,0:T(8,128)(2,1)}, bf16[128,2816]{1,0:T(8,128)(2,1)S(1)}, u32[]{:S(2)}, u32[]{:S(2)}) collective-permute-start(bf16[128,2816]{1,0:T(8,128)(2,1)} %get-tuple-element.37), channel_id=1, source_target_pairs={{0,32},{16,48},{32,0},{48,16},{1,33},{17,49},{33,1},{49,17},{2,34}... | collective-permute-start | bytes 2162696 | tf_op jit(solution)/shard_map/ppermute | solution.py:389
  17.0 0.0 copy-done
  17.0 0.0 copy-done.3
  17.0 8.4 %shard_map.105 = bf16[16,160,256]{2,1,0:T(8,128)(2,1)} custom-call(bf16[128,3072]{1,0:T(8,128)(2,1)S(1)} %get-tuple-element.31.dimg, bf16[2048,3072]{1,0:T(8,128)(2,1)} %weight.1, bf16[32,2048]{1,0:T(8,128)(2,1)S(1)} %bitcast.34, f32[1,1]{1,0:T(1,128)} %bitcast.27.adv, bf16[32,6144]{1,0:T(8,128)(2,1)S(1)} %bitcast.30, bf16[128,6144]{1,0:T(8,128)(2,1)} %bitcast.37), custom_call_target="tpu_custom_call" | custom-call | flops 1610612736 | bytes 15335424 | tf_op jit(solution)/shard_map/pallas_call | solution.py:225
  25.5 1.1 all-to-all-done
  26.6 6.4 %all-to-all-start.1 = ((bf16[16,160,256]{2,1,0:T(8,128)(2,1)}), bf16[16,160,256]{2,1,0:T(8,128)(2,1)}, u32[]{:S(2)}, u32[]{:S(2)}) async-start(bf16[16,160,256]{2,1,0:T(8,128)(2,1)} %shard_map.105), calls=%async_computation.1 | async-start | bytes 2621440 | tf_op jit(solution)/shard_map/all_to_all | solution.py:27
  32.9 17.7 %shard_map.106 = (bf16[2560,2560]{1,0:T(8,128)(2,1)}, f32[2560,128]{1,0:T(8,128)}) custom-call(bf16[2560,256]{1,0:T(8,128)(2,1)} %bitcast.7.q.k, bf16[2560,256]{1,0:T(8,128)(2,1)} %bitcast.7.q.k), custom_call_target="tpu_custom_call" | custom-call | flops 3355443 | bytes 13107 | tf_op jit(solution)/shard_map/pallas_call | solution.py:280
  50.6 0.0 collective-permute-done.m1
  50.6 0.0 collective-permute-done.1.m2
  50.6 0.0 collective-permute-done.2.m3
  50.7 2.8 %shard_map.108 = (bf16[2048,384]{1,0:T(8,128)(2,1)S(1)}, bf16[1024,384]{1,0:T(8,128)(2,1)S(1)}, bf16[1024,384]{1,0:T(8,128)(2,1)S(1)}) custom-call(s32[1,1]{1,0:T(1,128)} %bitcast.10.c, bf16[128,2048]{1,0:T(8,128)(2,1)S(1)} %bitcast.32, bf16[128,768]{1,0:T(8,128)(2,1)S(1)} %get-tuple-element.42.here, bf16[128,2816]{1,0:T(8,128)(2,1)S(1)} %collective-permute-done.m1, ...), custom_call_target="tpu_custom_call" | custom-call | flops 1610612 | bytes 6029 | tf_op jit(solution)/shard_map/pallas_call | solution.py:135
  53.4 0.2 collective-permute-start.3
  53.7 0.4 collective-permute-start.4
  54.0 1.8 %collective-permute-done.3.low = bf16[1024,384]{1,0:T(8,128)(2,1)S(1)} collective-permute-done((bf16[1024,384]{1,0:T(8,128)(2,1)S(1)}, bf16[1024,384]{1,0:T(8,128)(2,1)S(1)}, u32[]{:S(2)}, u32[]{:S(2)}) %collective-permute-start.3) | collective-permute-done | bytes 786464 | tf_op jit(solution)/shard_map/ppermute | solution.py:392
  55.8 1.1 collective-permute-done.4.high
  56.9 1.4 %shard_map.109 = bf16[16,128,384]{2,1,0:T(8,128)(2,1)} custom-call(bf16[2048,384]{1,0:T(8,128)(2,1)S(1)} %get-tuple-element.46.keep, bf16[1024,384]{1,0:T(8,128)(2,1)S(1)} %collective-permute-done.3.low, bf16[1024,384]{1,0:T(8,128)(2,1)S(1)} %collective-permute-done.4.high), custom_call_target="tpu_custom_call" | custom-call | bytes 4718 | tf_op jit(solution)/shard_map/pallas_call | solution.py:173
  58.3 0.0 all-to-all-done.1
  58.3 7.9 %all-to-all-start.2 = ((bf16[16,128,384]{2,1,0:T(8,128)(2,1)}), bf16[16,128,384]{2,1,0:T(8,128)(2,1)S(1)}, u32[]{:S(2)}, u32[]{:S(2)}) async-start(bf16[16,128,384]{2,1,0:T(8,128)(2,1)} %shard_map.109), calls=%async_computation.2 | async-start | bytes 3145728 | tf_op jit(solution)/shard_map/all_to_all | solution.py:27
  66.2 21.0 %shard_map.107 = bf16[2560,384]{1,0:T(8,128)(2,1)} custom-call(bf16[2560,2560]{1,0:T(8,128)(2,1)} %get-tuple-element.33.e, f32[2560,128]{1,0:T(8,128)} %get-tuple-element.39.inv, bf16[2560,256]{1,0:T(8,128)(2,1)} %bitcast.7.q.k, bf16[2560,256]{1,0:T(8,128)(2,1)} %bitcast.7.q.k, bf16[2560,256]{1,0:T(8,128)(2,1)} %bitcast.8.v.d, bf16[2560,256]{1,0:T(8,128)(2,1)} %bitcast.8.v.d), custom_call_target="tpu_custom_call" | custom-call | flops 13421772 | bytes 13107 | tf_op jit(solution)/shard_map/pallas_call | solution.py:336
  87.2 0.8 all-to-all-done.2
  88.0 6.9 %all-to-all-start.3 = ((bf16[16,160,384]{2,1,0:T(8,128)(2,1)}), bf16[16,160,384]{2,1,0:T(8,128)(2,1)S(1)}, u32[]{:S(2)}, u32[]{:S(2)}) async-start(bf16[16,160,384]{2,1,0:T(8,128)(2,1)} %bitcast.38), calls=%async_computation.3 | async-start | bytes 3932160 | tf_op jit(solution)/shard_map/all_to_all | solution.py:27
  94.9 0.2 convert_reduce_fusion
  95.2 0.2 collective-permute-start.5
  95.4 1.2 collective-permute-done.5
  96.6 1.6 %collective-permute-start.6 = (f32[16,768]{1,0:T(8,128)S(1)}, f32[16,768]{1,0:T(8,128)S(1)}, u32[]{:S(2)}, u32[]{:S(2)}) collective-permute-start(f32[16,768]{1,0:T(8,128)S(1)} %get-tuple-element.57), channel_id=1, source_target_pairs={{0,16},{16,32},{32,48},{48,0},{1,17},{17,33},{33,49},{49,1},{2,18}... | collective-permute-start | bytes 147464 | tf_op jit(solution)/shard_map/ppermute | solution.py:389
  98.3 2.9 %collective-permute-start.7 = (f32[16,768]{1,0:T(8,128)S(1)}, f32[16,768]{1,0:T(8,128)S(1)}, u32[]{:S(2)}, u32[]{:S(2)}) collective-permute-start(f32[16,768]{1,0:T(8,128)S(1)} %get-tuple-element.56), channel_id=1, source_target_pairs={{0,32},{16,48},{32,0},{48,16},{1,33},{17,49},{33,1},{49,17},{2,34}... | collective-permute-start | bytes 147464 | tf_op jit(solution)/shard_map/ppermute | solution.py:389
  101.2 1.3 %collective-permute-start.8 = (f32[16,768]{1,0:T(8,128)S(1)}, f32[16,768]{1,0:T(8,128)S(1)}, u32[]{:S(2)}, u32[]{:S(2)}) collective-permute-start(f32[16,768]{1,0:T(8,128)S(1)} %get-tuple-element.55), channel_id=1, source_target_pairs={{0,48},{16,0},{32,16},{48,32},{1,49},{17,1},{33,17},{49,33},{2,50}... | collective-permute-start | bytes 147464 | tf_op jit(solution)/shard_map/ppermute | solution.py:389
  102.5 0.0 collective-permute-done.6.refs_1_
  102.5 1.5 %collective-permute-done.7.refs_2_ = f32[16,768]{1,0:T(8,128)S(1)} collective-permute-done((f32[16,768]{1,0:T(8,128)S(1)}, f32[16,768]{1,0:T(8,128)S(1)}, u32[]{:S(2)}, u32[]{:S(2)}) %collective-permute-start.7) | collective-permute-done | bytes 49184 | tf_op jit(solution)/shard_map/ppermute | solution.py:389
  104.0 1.3 %collective-permute-done.8.refs_3_ = f32[16,768]{1,0:T(8,128)S(1)} collective-permute-done((f32[16,768]{1,0:T(8,128)S(1)}, f32[16,768]{1,0:T(8,128)S(1)}, u32[]{:S(2)}, u32[]{:S(2)}) %collective-permute-start.8) | collective-permute-done | bytes 49184 | tf_op jit(solution)/shard_map/ppermute | solution.py:389
  105.3 0.7 shard_map.110
  106.0 15.9 %all-to-all-done.3.back = bf16[16,160,384]{2,1,0:T(8,128)(2,1)S(1)} async-done(((bf16[16,160,384]{2,1,0:T(8,128)(2,1)}), bf16[16,160,384]{2,1,0:T(8,128)(2,1)S(1)}, u32[]{:S(2)}, u32[]{:S(2)}) %all-to-all-start.3) | async-done | bytes 1966112 | tf_op jit(solution)/shard_map/all_to_all | solution.py:27
  121.9 2.3 %shard_map.111 = (bf16[32,6144]{1,0:T(8,128)(2,1)}, bf16[128,6144]{1,0:T(8,128)(2,1)}) custom-call(bf16[16,160,384]{2,1,0:T(8,128)(2,1)S(1)} %all-to-all-done.3.back), custom_call_target="tpu_custom_call" | custom-call | bytes 3932 | tf_op jit(solution)/shard_map/pallas_call | solution.py:360
  (4 shorter events, 0.1 us)
Async XLA Ops:
  2.9 7.0 %copy-start.1 = (bf16[1,128,2048]{2,1,0:T(8,128)(2,1)S(1)}, bf16[1,128,2048]{2,1,0:T(8,128)(2,1)}, u32[]{:S(2)}) copy-start(bf16[1,128,2048]{2,1,0:T(8,128)(2,1)} %param.10) | copy-start | bytes 1572868
  2.9 7.0 %copy-start.2 = (bf16[1,128,3072]{2,1,0:T(8,128)(2,1)S(1)}, bf16[1,128,3072]{2,1,0:T(8,128)(2,1)}, u32[]{:S(2)}) copy-start(bf16[1,128,3072]{2,1,0:T(8,128)(2,1)} %param.12) | copy-start | bytes 2359300
  2.9 7.1 %copy-start.4 = (f32[1,3072]{1,0:T(1,128)S(1)}, f32[1,3072]{1,0:T(1,128)}, u32[]{:S(2)}) copy-start(f32[1,3072]{1,0:T(1,128)} %gate.1) | copy-start | bytes 36868
  2.9 14.1 %copy-start = (bf16[1,32,6144]{2,1,0:T(8,128)(2,1)S(1)}, bf16[1,32,6144]{2,1,0:T(8,128)(2,1)}, u32[]{:S(2)}) copy-start(bf16[1,32,6144]{2,1,0:T(8,128)(2,1)} %param.8) | copy-start | bytes 1179652
  3.0 14.1 %copy-start.3 = (bf16[1,32,2048]{2,1,0:T(8,128)(2,1)S(1)}, bf16[1,32,2048]{2,1,0:T(8,128)(2,1)}, u32[]{:S(2)}) copy-start(bf16[1,32,2048]{2,1,0:T(8,128)(2,1)} %param.11) | copy-start | bytes 393220
  3.0 23.6 %all-to-all-start = ((bf16[16,160,256]{2,1,0:T(8,128)(2,1)}), bf16[16,160,256]{2,1,0:T(8,128)(2,1)}, u32[]{:S(2)}, u32[]{:S(2)}) async-start(bf16[16,160,256]{2,1,0:T(8,128)(2,1)} %shard_map.103), calls=%async_computation | async-start | bytes 2621440 | tf_op jit(solution)/shard_map/all_to_all | solution.py:27
  11.8 38.8 %collective-permute-start = (bf16[128,2816]{1,0:T(8,128)(2,1)}, bf16[128,2816]{1,0:T(8,128)(2,1)S(1)}, u32[]{:S(2)}, u32[]{:S(2)}) collective-permute-start(bf16[128,2816]{1,0:T(8,128)(2,1)} %get-tuple-element.35), channel_id=1, source_target_pairs={{0,16},{16,32},{32,48},{48,0},{1,17},{17,33},{33,49},{49,1},{2,18}... | collective-permute-start | bytes 2162696 | tf_op jit(solution)/shard_map/ppermute | solution.py:389
  13.4 37.3 %collective-permute-start.1 = (bf16[128,2816]{1,0:T(8,128)(2,1)}, bf16[128,2816]{1,0:T(8,128)(2,1)S(1)}, u32[]{:S(2)}, u32[]{:S(2)}) collective-permute-start(bf16[128,2816]{1,0:T(8,128)(2,1)} %get-tuple-element.36), channel_id=1, source_target_pairs={{0,48},{16,0},{32,16},{48,32},{1,49},{17,1},{33,17},{49,33},{2,50}... | collective-permute-start | bytes 2162696 | tf_op jit(solution)/shard_map/ppermute | solution.py:389
  15.0 35.6 %collective-permute-start.2 = (bf16[128,2816]{1,0:T(8,128)(2,1)}, bf16[128,2816]{1,0:T(8,128)(2,1)S(1)}, u32[]{:S(2)}, u32[]{:S(2)}) collective-permute-start(bf16[128,2816]{1,0:T(8,128)(2,1)} %get-tuple-element.37), channel_id=1, source_target_pairs={{0,32},{16,48},{32,0},{48,16},{1,33},{17,49},{33,1},{49,17},{2,34}... | collective-permute-start | bytes 2162696 | tf_op jit(solution)/shard_map/ppermute | solution.py:389
  26.6 31.7 %all-to-all-start.1 = ((bf16[16,160,256]{2,1,0:T(8,128)(2,1)}), bf16[16,160,256]{2,1,0:T(8,128)(2,1)}, u32[]{:S(2)}, u32[]{:S(2)}) async-start(bf16[16,160,256]{2,1,0:T(8,128)(2,1)} %shard_map.105), calls=%async_computation.1 | async-start | bytes 2621440 | tf_op jit(solution)/shard_map/all_to_all | solution.py:27
  53.4 2.4 %collective-permute-start.3 = (bf16[1024,384]{1,0:T(8,128)(2,1)S(1)}, bf16[1024,384]{1,0:T(8,128)(2,1)S(1)}, u32[]{:S(2)}, u32[]{:S(2)}) collective-permute-start(bf16[1024,384]{1,0:T(8,128)(2,1)S(1)} %get-tuple-element.47), channel_id=1, source_target_pairs={{0,1},{1,0},{2,3},{3,2},{4,5},{5,4},{6,7},{7,6},{8,9},{9,8},{10,11... | collective-permute-start | bytes 2359304 | tf_op jit(solution)/shard_map/ppermute | solution.py:392
  53.7 3.3 %collective-permute-start.4 = (bf16[1024,384]{1,0:T(8,128)(2,1)S(1)}, bf16[1024,384]{1,0:T(8,128)(2,1)S(1)}, u32[]{:S(2)}, u32[]{:S(2)}) collective-permute-start(bf16[1024,384]{1,0:T(8,128)(2,1)S(1)} %get-tuple-element.48), channel_id=1, source_target_pairs={{0,1},{1,0},{2,3},{3,2},{4,5},{5,4},{6,7},{7,6},{8,9},{9,8},{10,11... | collective-permute-start | bytes 2359304 | tf_op jit(solution)/shard_map/ppermute | solution.py:392
  58.3 29.7 %all-to-all-start.2 = ((bf16[16,128,384]{2,1,0:T(8,128)(2,1)}), bf16[16,128,384]{2,1,0:T(8,128)(2,1)S(1)}, u32[]{:S(2)}, u32[]{:S(2)}) async-start(bf16[16,128,384]{2,1,0:T(8,128)(2,1)} %shard_map.109), calls=%async_computation.2 | async-start | bytes 3145728 | tf_op jit(solution)/shard_map/all_to_all | solution.py:27
  88.0 33.8 %all-to-all-start.3 = ((bf16[16,160,384]{2,1,0:T(8,128)(2,1)}), bf16[16,160,384]{2,1,0:T(8,128)(2,1)S(1)}, u32[]{:S(2)}, u32[]{:S(2)}) async-start(bf16[16,160,384]{2,1,0:T(8,128)(2,1)} %bitcast.38), calls=%async_computation.3 | async-start | bytes 3932160 | tf_op jit(solution)/shard_map/all_to_all | solution.py:27
  95.2 1.4 %collective-permute-start.5 = (f32[4,16,384]{2,1,0:T(8,128)S(1)}, f32[4,16,384]{2,1,0:T(8,128)S(1)}, u32[]{:S(2)}, u32[]{:S(2)}) collective-permute-start(f32[4,16,384]{2,1,0:T(8,128)S(1)} %get-tuple-element.60), channel_id=1, source_target_pairs={{0,1},{1,0},{2,3},{3,2},{4,5},{5,4},{6,7},{7,6},{8,9},{9,8},{10,11... | collective-permute-start | bytes 294920 | tf_op jit(solution)/shard_map/ppermute | solution.py:392
  96.6 5.9 %collective-permute-start.6 = (f32[16,768]{1,0:T(8,128)S(1)}, f32[16,768]{1,0:T(8,128)S(1)}, u32[]{:S(2)}, u32[]{:S(2)}) collective-permute-start(f32[16,768]{1,0:T(8,128)S(1)} %get-tuple-element.57), channel_id=1, source_target_pairs={{0,16},{16,32},{32,48},{48,0},{1,17},{17,33},{33,49},{49,1},{2,18}... | collective-permute-start | bytes 147464 | tf_op jit(solution)/shard_map/ppermute | solution.py:389
  98.3 5.7 %collective-permute-start.7 = (f32[16,768]{1,0:T(8,128)S(1)}, f32[16,768]{1,0:T(8,128)S(1)}, u32[]{:S(2)}, u32[]{:S(2)}) collective-permute-start(f32[16,768]{1,0:T(8,128)S(1)} %get-tuple-element.56), channel_id=1, source_target_pairs={{0,32},{16,48},{32,0},{48,16},{1,33},{17,49},{33,1},{49,17},{2,34}... | collective-permute-start | bytes 147464 | tf_op jit(solution)/shard_map/ppermute | solution.py:389
  101.2 4.1 %collective-permute-start.8 = (f32[16,768]{1,0:T(8,128)S(1)}, f32[16,768]{1,0:T(8,128)S(1)}, u32[]{:S(2)}, u32[]{:S(2)}) collective-permute-start(f32[16,768]{1,0:T(8,128)S(1)} %get-tuple-element.55), channel_id=1, source_target_pairs={{0,48},{16,0},{32,16},{48,32},{1,49},{17,1},{33,17},{49,33},{2,50}... | collective-permute-start | bytes 147464 | tf_op jit(solution)/shard_map/ppermute | solution.py:389

commit v5 on v4

--- a/solution.py
+++ b/solution.py
@@ -19,6 +19,7 @@
 PLANE = ("zh", "zl", "x")
 RING = 4
 HOPS = (1, RING - 1, 2)
+SPAN = 256
 BF16 = jnp.bfloat16
 F32 = jnp.float32
 
@@ -70,44 +71,39 @@
 def d_image_kernel(cot, gate, adv, y, attn, out, here, ahead, behind, across):
     weighted = adv[0, 0] * gate[...]
     out[...] = (weighted * cot[...].astype(F32)).astype(BF16)
-    width = here.shape[1]
-    rows = attn.shape[1]
-    count = out.shape[1] // width
-
-    def part(hop):
-        start = lax.rem(y[0, 0] + hop, count) * width
-        return out[:, pl.ds(pl.multiple_of(start, width), width)]
-
-    here[...] = part(0)
-    for hop, ref in ((1, ahead), (count - 1, behind), (2, across)):
-        ref[:, :rows] = attn[...]
-        ref[:, rows:] = part(hop)
-
-
-def d_image_call(cot, gate, adv, y, attn, count):
+    rows, cols = attn.shape[1] // 2, out.shape[1] // 2
+    for hop, ref in zip((0,) + HOPS, (here, ahead, behind, across)):
+        place = lax.rem(y[0, 0] + hop, RING)
+        odd, upper = lax.rem(place, 2), lax.div(place, 2)
+        for block in range(rows // SPAN):
+            start = (2 * block + odd) * SPAN
+            ref[:, block * SPAN : (block + 1) * SPAN] = attn[:, pl.ds(pl.multiple_of(start, SPAN), SPAN)]
+        ref[:, rows:] = out[:, pl.ds(pl.multiple_of(upper * cols, cols), cols)]
+
+
+def d_image_call(cot, gate, adv, y, attn):
     rows, width = cot.shape
-    part = width // count
     vmem = pl.BlockSpec(memory_space=pltpu.VMEM)
     smem = pl.BlockSpec(memory_space=pltpu.SMEM)
+    payload = jax.ShapeDtypeStruct((rows, attn.shape[1] // 2 + width // 2), BF16)
     return pl.pallas_call(
         d_image_kernel,
         in_specs=[vmem, vmem, smem, smem, vmem],
         out_specs=[vmem] * 5,
-        out_shape=[jax.ShapeDtypeStruct((rows, width), BF16), jax.ShapeDtypeStruct((rows, part), BF16)]
-        + [jax.ShapeDtypeStruct((rows, attn.shape[1] + part), BF16)] * 3,
+        out_shape=[jax.ShapeDtypeStruct((rows, width), BF16)] + [payload] * 4,
         compiler_params=params(48),
         cost_estimate=cost(2 * rows * width, 6 * rows * width),
     )(cot, gate, adv, y, attn)
 
 
-def partial_kernel(c, attn, here, m1, m2, m3, keep, low, high):
+def partial_kernel(c, m0, m1, m2, m3, keep, low, high):
     block, half = keep.shape
-    rows = m1.shape[1] - 2 * half
+    rows = m0.shape[1] - 2 * half
     at = pl.ds(pl.multiple_of(pl.program_id(0) * block, block), block)
-    merged = (m1, m2, m3)
+    merged = (m0, m1, m2, m3)
     value = lax.dot_general(
-        jnp.concatenate([attn[...]] + [ref[:, at] for ref in merged], axis=0),
-        jnp.concatenate([here[...]] + [ref[:, rows:] for ref in merged], axis=0),
+        jnp.concatenate([ref[:, at] for ref in merged], axis=0),
+        jnp.concatenate([ref[:, rows:] for ref in merged], axis=0),
         (((0,), (0,)), ((), ())),
         preferred_element_type=F32,
     )
@@ -126,21 +122,16 @@
         high[...] = send
 
 
-def partial_call(c, attn, here, merged):
-    tokens, rows = attn.shape
-    cols = here.shape[1]
-    block = 512
+def partial_call(c, merged, rows, cols):
+    tokens = merged[0].shape[0]
+    block = SPAN
     half = rows // block // 2
     out = (block, cols // 2)
     return pl.pallas_call(
         partial_kernel,
         grid=(rows // block,),
-        in_specs=[
-            pl.BlockSpec(memory_space=pltpu.SMEM),
-            pl.BlockSpec((tokens, block), lambda i: (0, i)),
-            pl.BlockSpec((tokens, cols), lambda i: (0, 0)),
-        ]
-        + [pl.BlockSpec((tokens, rows + cols), lambda i: (0, 0))] * 3,
+        in_specs=[pl.BlockSpec(memory_space=pltpu.SMEM)]
+        + [pl.BlockSpec((tokens, rows + cols), lambda i: (0, 0))] * len(merged),
         out_specs=[
             pl.BlockSpec(out, lambda i: (i, 0)),
             pl.BlockSpec(out, lambda i: (jnp.minimum(i, half - 1), 0)),
@@ -153,7 +144,7 @@
         ],
         compiler_params=params(40),
         cost_estimate=cost(8 * tokens * rows * cols, 8 * tokens * (rows + cols) + 2 * rows * cols, SMALL),
-    )(c, attn, here, *merged)
+    )(c, *merged)
 
 
 def place_kernel(ring, keep, low, high, out):
@@ -179,28 +170,6 @@
         compiler_params=params(40),
         cost_estimate=cost(0, 6 * keep.size, SMALL),
     )(keep, *got)
-
-
-def ring_kernel(y, *refs):
-    out = refs[-1]
-    count = len(refs) - 1
-    width = refs[0].shape[1]
-    for hop in range(count):
-        start = lax.rem(y[0, 0] + count - hop, count) * width
-        out[:, pl.ds(pl.multiple_of(start, width), width)] = refs[hop][...]
-
-
-def ring_call(y, pieces):
-    rows, width = pieces[0].shape
-    vmem = pl.BlockSpec(memory_space=pltpu.VMEM)
-    return pl.pallas_call(
-        ring_kernel,
-        in_specs=[pl.BlockSpec(memory_space=pltpu.SMEM)] + [vmem] * len(pieces),
-        out_specs=vmem,
-        out_shape=jax.ShapeDtypeStruct((rows, width * len(pieces)), F32),
-        compiler_params=params(16),
-        cost_estimate=cost(0, 8 * rows * width * len(pieces), SMALL),
-    )(y, *pieces)
 
 
 def d_out_kernel(dimg, weight, cot_txt, adv, vt, vi, out):
@@ -395,8 +364,8 @@
     packed = pack_heads(txt, img, 0, 2, heads)
     qk = exchange(packed, SEQ)
     cot, attn, packed = lax.optimization_barrier((cot_img[0], attn, packed))
-    d_image, here, *merged = d_image_call(cot, gate, adv, y, attn, RING)
-    merged = shift(merged, "y")
+    d_image, here, *merged = d_image_call(cot, gate, adv, y, attn)
+    merged = [here, *shift(merged, "y")]
     vd = d_out_call(d_image, proj_weight, cot_txt[0], adv, txt, img, heads)
     vd, qk = lax.optimization_barrier((vd, qk))
     vd = exchange(vd, SEQ)
@@ -404,14 +373,14 @@
     n = heads * tokens
     qk = qk.reshape(n, 2 * HEAD_SIZE)
     exps, inverse = exps_call(qk)
-    attn, here, merged, inverse = lax.optimization_barrier((attn, here, merged, inverse))
-    keep, low, high = partial_call(core, attn, here, merged)
+    merged, inverse = lax.optimization_barrier((merged, inverse))
+    keep, low, high = partial_call(core, merged, width // 2, model // 2)
     low, high = swap(low), swap(high)
 
     devices = lax.axis_size(ALL)
     rows = width // devices
     cols = keep.shape[1]
-    product = place_call(keep, [low, high], RING, lax.axis_size(PLANE) // 2, 2 * rows)
+    product = place_call(keep, [low, high], RING // 2, lax.axis_size(PLANE) // 2, 2 * rows)
     product = exchange(product, PLANE)
 
     vd = vd.reshape(n, 2 * HEAD_SIZE)
@@ -420,14 +389,19 @@
     back = exchange(grads, SEQ)
 
     total = jnp.sum(product.astype(F32), axis=0) * (1.0 / (img.shape[0] * devices))
-    total = total.reshape(RING, 2, rows, cols)
-    c, y = core[0, 0], y[0, 0]
+    total = total.reshape(2, 2, rows, cols)
+    c, upper = core[0, 0], y[0, 0] // 2
+
+    def joined(first, own, other):
+        return jnp.where(first, jnp.concatenate([own, other], -1), jnp.concatenate([other, own], -1))
+
     own = lax.dynamic_index_in_dim(total, c, 1, keepdims=False)
     other = swap(lax.dynamic_index_in_dim(total, 1 - c, 1, keepdims=False))
-    wide = jnp.where(c == 0, jnp.concatenate([own, other], -1), jnp.concatenate([other, own], -1))
-    pick = lambda hop: lax.dynamic_index_in_dim(wide, (y + hop) % RING, 0, keepdims=False)
-    behind, ahead, across = shift([pick(hop) for hop in HOPS], "y")
-    grad_proj = ring_call(y.reshape(1, 1), [pick(0), behind, across, ahead])
+    wide = joined(c == 0, own, other)
+    own = lax.dynamic_index_in_dim(wide, upper, 0, keepdims=False)
+    other = lax.dynamic_index_in_dim(wide, 1 - upper, 0, keepdims=False)
+    other = lax.ppermute(other, "y", [(i, (i + 2) % RING) for i in range(RING)])
+    grad_proj = joined(upper == 0, own, other)
     back, grad_proj = lax.optimization_barrier((back, grad_proj))
 
     dqkv_txt, dqkv_img = unpack_call(back, txt.shape[0])

time: 125 us -> 126 us (level)
  waiting for transfers between devices: 24.6 us -> 27.4 us
  starting transfers between devices: 39.5 us -> 36.8 us
    ppermute x6 -> x3, starting transfers between devices: 11.1 us -> 5.22 us  [shift(): lax.ppermute(array, axes, perm)]
    ppermute x0 -> x1, starting transfers between devices: none -> 3.26 us  [per_device(): other = lax.ppermute(other, 'y', [(i, (i + 2) % RING) for i in range(RING)])]
    ppermute x0 -> x1, waiting for transfers between devices: none -> 3.17 us  [per_device(): other = lax.ppermute(other, 'y', [(i, (i + 2) % RING) for i in range(RING)])]
    ppermute x6 -> x3, waiting for transfers between devices: 2.75 us -> 0.01 us  [shift(): lax.ppermute(array, axes, perm)]
    all_to_all x4, waiting for transfers between devices: 17.8 us -> 20.2 us  [exchange(): return lax.all_to_all(array, axes, split_axis=0, concat_axis=0, tiled=True)]
  transfers between devices with their start and end apart: 13 -> 11, of which waited for: 8 -> 7; matrix products, arithmetic and copies ran while one was open for 0% -> 1% of each run, Pallas kernels for 43% -> 43%
where the time goes in v5:
time: 126 us; the launch traced here: 124 us
  Pallas kernels  57.4 us (46%)
  starting transfers between devices  36.8 us (29%)
  waiting for transfers between devices  27.4 us (22%)
  between operations  1.39 us (1%)
    all_to_all x4, starting transfers between devices, exchange(): return lax.all_to_all(array, axes, split_axis=0, concat_axis=0, tiled=True)  27.5 us
    pallas_call x1, Pallas kernels, grads_call(): pl.pallas_call(grads_kernel, grid=(n // BLOCK,), in_specs=[pl.BlockSpec((...  21 us
    all_to_all x4, waiting for transfers between devices, exchange(): return lax.all_to_all(array, axes, split_axis=0, concat_axis=0, tiled=True)  20.2 us
    pallas_call x1, Pallas kernels, exps_call(): pl.pallas_call(exps_kernel, grid=(n // block,), in_specs=[pl.BlockSpec((b...  17.7 us
    pallas_call x1, Pallas kernels, d_out_call(): pl.pallas_call(d_out_kernel, grid=(per,), in_specs=[pl.BlockSpec((rows, m...  8.42 us
    ppermute x3, starting transfers between devices, shift(): lax.ppermute(array, axes, perm)  5.22 us
    ppermute x3, waiting for transfers between devices, swap(): return lax.ppermute(array, 'c', [(0, 1), (1, 0)])  4.05 us
    ppermute x1, starting transfers between devices, per_device(): other = lax.ppermute(other, 'y', [(i, (i + 2) % RING) for i in range(RING)])  3.26 us
  transfers between devices with their start and end apart: 11, of which 7 were waited for; matrix products, arithmetic and copies ran while one was open for 1% of the time, Pallas kernels for 43%

profile of v5, /device:TPU:2, one launch (start us, length us, event | category | flops | bytes accessed | tf_op | source)
XLA Modules:
  0.0 124.0 jit_solution(14167815333231719465)
XLA Ops:
  0.6 2.3 %shard_map.103 = bf16[16,160,256]{2,1,0:T(8,128)(2,1)} custom-call(bf16[32,6144]{1,0:T(8,128)(2,1)} %bitcast.24, bf16[32,6144]{1,0:T(8,128)(2,1)} %bitcast.25, bf16[128,6144]{1,0:T(8,128)(2,1)} %bitcast.30, bf16[128,6144]{1,0:T(8,128)(2,1)} %bitcast.31), custom_call_target="tpu_custom_call" | custom-call | bytes 2621440 | tf_op jit(solution)/shard_map/pallas_call | solution.py:60
  2.9 0.0 copy-start.1
  2.9 0.0 copy-start.2
  2.9 0.0 copy-start.4
  2.9 0.0 copy-start
  3.0 0.0 copy-start.3
  3.0 6.3 %all-to-all-start = ((bf16[16,160,256]{2,1,0:T(8,128)(2,1)}), bf16[16,160,256]{2,1,0:T(8,128)(2,1)}, u32[]{:S(2)}, u32[]{:S(2)}) async-start(bf16[16,160,256]{2,1,0:T(8,128)(2,1)} %shard_map.103), calls=%async_computation | async-start | bytes 2621440 | tf_op jit(solution)/shard_map/all_to_all | solution.py:28
  10.0 0.0 copy-done.1
  10.0 0.0 copy-done.2
  10.0 0.0 copy-done.4
  10.0 1.7 %shard_map.104 = (bf16[128,3072]{1,0:T(8,128)(2,1)S(1)}, bf16[128,2560]{1,0:T(8,128)(2,1)S(1)}, bf16[128,2560]{1,0:T(8,128)(2,1)}, bf16[128,2560]{1,0:T(8,128)(2,1)}, bf16[128,2560]{1,0:T(8,128)(2,1)}) custom-call(bf16[128,3072]{1,0:T(8,128)(2,1)S(1)} %bitcast.27, f32[1,3072]{1,0:T(1,128)S(1)} %copy-done.4, f32[1,1]{1,0:T(1,128)} %bitcast.22.adv, ...), custom_call_target="tpu_custom_call" | custom-call | flops 786432 | bytes 2359296 | tf_op jit(solution)/shard_map/pallas_call | solution.py:89
  11.7 1.6 %collective-permute-start = (bf16[128,2560]{1,0:T(8,128)(2,1)}, bf16[128,2560]{1,0:T(8,128)(2,1)S(1)}, u32[]{:S(2)}, u32[]{:S(2)}) collective-permute-start(bf16[128,2560]{1,0:T(8,128)(2,1)} %get-tuple-element.34), channel_id=1, source_target_pairs={{0,16},{16,32},{32,48},{48,0},{1,17},{17,33},{33,49},{49,1},{2,18}... | collective-permute-start | bytes 1966088 | tf_op jit(solution)/shard_map/ppermute | solution.py:358
  13.3 1.7 %collective-permute-start.1 = (bf16[128,2560]{1,0:T(8,128)(2,1)}, bf16[128,2560]{1,0:T(8,128)(2,1)S(1)}, u32[]{:S(2)}, u32[]{:S(2)}) collective-permute-start(bf16[128,2560]{1,0:T(8,128)(2,1)} %get-tuple-element.35), channel_id=1, source_target_pairs={{0,48},{16,0},{32,16},{48,32},{1,49},{17,1},{33,17},{49,33},{2,50}... | collective-permute-start | bytes 1966088 | tf_op jit(solution)/shard_map/ppermute | solution.py:358
  14.9 2.0 %collective-permute-start.2 = (bf16[128,2560]{1,0:T(8,128)(2,1)}, bf16[128,2560]{1,0:T(8,128)(2,1)S(1)}, u32[]{:S(2)}, u32[]{:S(2)}) collective-permute-start(bf16[128,2560]{1,0:T(8,128)(2,1)} %get-tuple-element.36), channel_id=1, source_target_pairs={{0,32},{16,48},{32,0},{48,16},{1,33},{17,49},{33,1},{49,17},{2,34}... | collective-permute-start | bytes 1966088 | tf_op jit(solution)/shard_map/ppermute | solution.py:358
  16.9 0.0 copy-done
  16.9 0.0 copy-done.3
  16.9 8.4 %shard_map.105 = bf16[16,160,256]{2,1,0:T(8,128)(2,1)} custom-call(bf16[128,3072]{1,0:T(8,128)(2,1)S(1)} %get-tuple-element.30.dimg, bf16[2048,3072]{1,0:T(8,128)(2,1)} %weight.1, bf16[32,2048]{1,0:T(8,128)(2,1)S(1)} %bitcast.29, f32[1,1]{1,0:T(1,128)} %bitcast.23.adv, bf16[32,6144]{1,0:T(8,128)(2,1)S(1)} %bitcast.26, bf16[128,6144]{1,0:T(8,128)(2,1)} %bitcast.32), custom_call_target="tpu_custom_call" | custom-call | flops 1610612736 | bytes 15335424 | tf_op jit(solution)/shard_map/pallas_call | solution.py:194
  25.3 1.2 all-to-all-done
  26.6 6.4 %all-to-all-start.1 = ((bf16[16,160,256]{2,1,0:T(8,128)(2,1)}), bf16[16,160,256]{2,1,0:T(8,128)(2,1)}, u32[]{:S(2)}, u32[]{:S(2)}) async-start(bf16[16,160,256]{2,1,0:T(8,128)(2,1)} %shard_map.105), calls=%async_computation.1 | async-start | bytes 2621440 | tf_op jit(solution)/shard_map/all_to_all | solution.py:28
  32.9 17.7 %shard_map.106 = (bf16[2560,2560]{1,0:T(8,128)(2,1)}, f32[2560,128]{1,0:T(8,128)}) custom-call(bf16[2560,256]{1,0:T(8,128)(2,1)} %bitcast.7.q.k, bf16[2560,256]{1,0:T(8,128)(2,1)} %bitcast.7.q.k), custom_call_target="tpu_custom_call" | custom-call | flops 3355443 | bytes 13107 | tf_op jit(solution)/shard_map/pallas_call | solution.py:249
  50.7 0.0 collective-permute-done.m1
  50.7 0.0 collective-permute-done.1.m2
  50.7 0.0 collective-permute-done.2.m3
  50.7 2.6 %shard_map.108 = (bf16[1024,768]{1,0:T(8,128)(2,1)S(1)}, bf16[512,768]{1,0:T(8,128)(2,1)S(1)}, bf16[512,768]{1,0:T(8,128)(2,1)S(1)}) custom-call(s32[1,1]{1,0:T(1,128)} %bitcast.10.c, bf16[128,2560]{1,0:T(8,128)(2,1)S(1)} %get-tuple-element.40.m0, bf16[128,2560]{1,0:T(8,128)(2,1)S(1)} %collective-permute-done.m1, ...), custom_call_target="tpu_custom_call" | custom-call | flops 1610612 | bytes 5767 | tf_op jit(solution)/shard_map/pallas_call | solution.py:130
  53.3 0.2 collective-permute-start.3
  53.5 0.4 collective-permute-start.4
  53.9 1.8 %collective-permute-done.3.low = bf16[512,768]{1,0:T(8,128)(2,1)S(1)} collective-permute-done((bf16[512,768]{1,0:T(8,128)(2,1)S(1)}, bf16[512,768]{1,0:T(8,128)(2,1)S(1)}, u32[]{:S(2)}, u32[]{:S(2)}) %collective-permute-start.3) | collective-permute-done | bytes 786464 | tf_op jit(solution)/shard_map/ppermute | solution.py:361
  55.7 1.1 collective-permute-done.4.high
  56.8 1.3 %shard_map.109 = bf16[16,64,768]{2,1,0:T(8,128)(2,1)} custom-call(bf16[1024,768]{1,0:T(8,128)(2,1)S(1)} %get-tuple-element.44.keep, bf16[512,768]{1,0:T(8,128)(2,1)S(1)} %collective-permute-done.3.low, bf16[512,768]{1,0:T(8,128)(2,1)S(1)} %collective-permute-done.4.high), custom_call_target="tpu_custom_call" | custom-call | bytes 4718 | tf_op jit(solution)/shard_map/pallas_call | solution.py:164
  58.1 0.0 all-to-all-done.1
  58.1 7.9 %all-to-all-start.2 = ((bf16[16,64,768]{2,1,0:T(8,128)(2,1)}), bf16[16,64,768]{2,1,0:T(8,128)(2,1)S(1)}, u32[]{:S(2)}, u32[]{:S(2)}) async-start(bf16[16,64,768]{2,1,0:T(8,128)(2,1)} %shard_map.109), calls=%async_computation.2 | async-start | bytes 3145728 | tf_op jit(solution)/shard_map/all_to_all | solution.py:28
  66.1 21.0 %shard_map.107 = bf16[2560,384]{1,0:T(8,128)(2,1)} custom-call(bf16[2560,2560]{1,0:T(8,128)(2,1)} %get-tuple-element.32.e, f32[2560,128]{1,0:T(8,128)} %get-tuple-element.38.inv, bf16[2560,256]{1,0:T(8,128)(2,1)} %bitcast.7.q.k, bf16[2560,256]{1,0:T(8,128)(2,1)} %bitcast.7.q.k, bf16[2560,256]{1,0:T(8,128)(2,1)} %bitcast.8.v.d, bf16[2560,256]{1,0:T(8,128)(2,1)} %bitcast.8.v.d), custom_call_target="tpu_custom_call" | custom-call | flops 13421772 | bytes 13107 | tf_op jit(solution)/shard_map/pallas_call | solution.py:305
  87.0 0.8 all-to-all-done.2
  87.9 6.9 %all-to-all-start.3 = ((bf16[16,160,384]{2,1,0:T(8,128)(2,1)}), bf16[16,160,384]{2,1,0:T(8,128)(2,1)S(1)}, u32[]{:S(2)}, u32[]{:S(2)}) async-start(bf16[16,160,384]{2,1,0:T(8,128)(2,1)} %bitcast.33), calls=%async_computation.3 | async-start | bytes 3932160 | tf_op jit(solution)/shard_map/all_to_all | solution.py:28
  94.8 0.2 convert_reduce_fusion
  95.0 0.2 collective-permute-start.5
  95.3 1.2 collective-permute-done.5
  96.5 3.3 %collective-permute-start.6 = (f32[16,1536]{1,0:T(8,128)S(1)}, f32[16,1536]{1,0:T(8,128)S(1)}, u32[]{:S(2)}, u32[]{:S(2)}) collective-permute-start(f32[16,1536]{1,0:T(8,128)S(1)} %get-tuple-element.54), channel_id=1, source_target_pairs={{0,32},{16,48},{32,0},{48,16},{1,33},{17,49},{33,1},{49,17},{2,34}... | collective-permute-start | bytes 294920 | tf_op jit(solution)/shard_map/ppermute | solution.py:403
  99.7 3.2 %collective-permute-done.6 = f32[16,1536]{1,0:T(8,128)S(1)} collective-permute-done((f32[16,1536]{1,0:T(8,128)S(1)}, f32[16,1536]{1,0:T(8,128)S(1)}, u32[]{:S(2)}, u32[]{:S(2)}) %collective-permute-start.6) | collective-permute-done | bytes 98336 | tf_op jit(solution)/shard_map/ppermute | solution.py:403
  102.9 0.7 maximum_select_fusion.1
  103.6 18.1 %all-to-all-done.3.back = bf16[16,160,384]{2,1,0:T(8,128)(2,1)S(1)} async-done(((bf16[16,160,384]{2,1,0:T(8,128)(2,1)}), bf16[16,160,384]{2,1,0:T(8,128)(2,1)S(1)}, u32[]{:S(2)}, u32[]{:S(2)}) %all-to-all-start.3) | async-done | bytes 1966112 | tf_op jit(solution)/shard_map/all_to_all | solution.py:28
  121.7 2.3 %shard_map.110 = (bf16[32,6144]{1,0:T(8,128)(2,1)}, bf16[128,6144]{1,0:T(8,128)(2,1)}) custom-call(bf16[16,160,384]{2,1,0:T(8,128)(2,1)S(1)} %all-to-all-done.3.back), custom_call_target="tpu_custom_call" | custom-call | bytes 3932 | tf_op jit(solution)/shard_map/pallas_call | solution.py:329
  (4 shorter events, 0.1 us)
Async XLA Ops:
  2.9 7.0 %copy-start.1 = (bf16[1,128,3072]{2,1,0:T(8,128)(2,1)S(1)}, bf16[1,128,3072]{2,1,0:T(8,128)(2,1)}, u32[]{:S(2)}) copy-start(bf16[1,128,3072]{2,1,0:T(8,128)(2,1)} %param.12) | copy-start | bytes 2359300
  2.9 7.0 %copy-start.2 = (bf16[1,128,2048]{2,1,0:T(8,128)(2,1)S(1)}, bf16[1,128,2048]{2,1,0:T(8,128)(2,1)}, u32[]{:S(2)}) copy-start(bf16[1,128,2048]{2,1,0:T(8,128)(2,1)} %param.10) | copy-start | bytes 1572868
  2.9 7.1 %copy-start.4 = (f32[1,3072]{1,0:T(1,128)S(1)}, f32[1,3072]{1,0:T(1,128)}, u32[]{:S(2)}) copy-start(f32[1,3072]{1,0:T(1,128)} %gate.1) | copy-start | bytes 36868
  2.9 14.0 %copy-start = (bf16[1,32,6144]{2,1,0:T(8,128)(2,1)S(1)}, bf16[1,32,6144]{2,1,0:T(8,128)(2,1)}, u32[]{:S(2)}) copy-start(bf16[1,32,6144]{2,1,0:T(8,128)(2,1)} %param.8) | copy-start | bytes 1179652
  3.0 14.0 %copy-start.3 = (bf16[1,32,2048]{2,1,0:T(8,128)(2,1)S(1)}, bf16[1,32,2048]{2,1,0:T(8,128)(2,1)}, u32[]{:S(2)}) copy-start(bf16[1,32,2048]{2,1,0:T(8,128)(2,1)} %param.11) | copy-start | bytes 393220
  3.0 23.6 %all-to-all-start = ((bf16[16,160,256]{2,1,0:T(8,128)(2,1)}), bf16[16,160,256]{2,1,0:T(8,128)(2,1)}, u32[]{:S(2)}, u32[]{:S(2)}) async-start(bf16[16,160,256]{2,1,0:T(8,128)(2,1)} %shard_map.103), calls=%async_computation | async-start | bytes 2621440 | tf_op jit(solution)/shard_map/all_to_all | solution.py:28
  11.7 39.0 %collective-permute-start = (bf16[128,2560]{1,0:T(8,128)(2,1)}, bf16[128,2560]{1,0:T(8,128)(2,1)S(1)}, u32[]{:S(2)}, u32[]{:S(2)}) collective-permute-start(bf16[128,2560]{1,0:T(8,128)(2,1)} %get-tuple-element.34), channel_id=1, source_target_pairs={{0,16},{16,32},{32,48},{48,0},{1,17},{17,33},{33,49},{49,1},{2,18}... | collective-permute-start | bytes 1966088 | tf_op jit(solution)/shard_map/ppermute | solution.py:358
  13.3 37.4 %collective-permute-start.1 = (bf16[128,2560]{1,0:T(8,128)(2,1)}, bf16[128,2560]{1,0:T(8,128)(2,1)S(1)}, u32[]{:S(2)}, u32[]{:S(2)}) collective-permute-start(bf16[128,2560]{1,0:T(8,128)(2,1)} %get-tuple-element.35), channel_id=1, source_target_pairs={{0,48},{16,0},{32,16},{48,32},{1,49},{17,1},{33,17},{49,33},{2,50}... | collective-permute-start | bytes 1966088 | tf_op jit(solution)/shard_map/ppermute | solution.py:358
  14.9 35.8 %collective-permute-start.2 = (bf16[128,2560]{1,0:T(8,128)(2,1)}, bf16[128,2560]{1,0:T(8,128)(2,1)S(1)}, u32[]{:S(2)}, u32[]{:S(2)}) collective-permute-start(bf16[128,2560]{1,0:T(8,128)(2,1)} %get-tuple-element.36), channel_id=1, source_target_pairs={{0,32},{16,48},{32,0},{48,16},{1,33},{17,49},{33,1},{49,17},{2,34}... | collective-permute-start | bytes 1966088 | tf_op jit(solution)/shard_map/ppermute | solution.py:358
  26.6 31.6 %all-to-all-start.1 = ((bf16[16,160,256]{2,1,0:T(8,128)(2,1)}), bf16[16,160,256]{2,1,0:T(8,128)(2,1)}, u32[]{:S(2)}, u32[]{:S(2)}) async-start(bf16[16,160,256]{2,1,0:T(8,128)(2,1)} %shard_map.105), calls=%async_computation.1 | async-start | bytes 2621440 | tf_op jit(solution)/shard_map/all_to_all | solution.py:28
  53.3 2.4 %collective-permute-start.3 = (bf16[512,768]{1,0:T(8,128)(2,1)S(1)}, bf16[512,768]{1,0:T(8,128)(2,1)S(1)}, u32[]{:S(2)}, u32[]{:S(2)}) collective-permute-start(bf16[512,768]{1,0:T(8,128)(2,1)S(1)} %get-tuple-element.45), channel_id=1, source_target_pairs={{0,1},{1,0},{2,3},{3,2},{4,5},{5,4},{6,7},{7,6},{8,9},{9,8},{10,11... | collective-permute-start | bytes 2359304 | tf_op jit(solution)/shard_map/ppermute | solution.py:361
  53.5 3.3 %collective-permute-start.4 = (bf16[512,768]{1,0:T(8,128)(2,1)S(1)}, bf16[512,768]{1,0:T(8,128)(2,1)S(1)}, u32[]{:S(2)}, u32[]{:S(2)}) collective-permute-start(bf16[512,768]{1,0:T(8,128)(2,1)S(1)} %get-tuple-element.46), channel_id=1, source_target_pairs={{0,1},{1,0},{2,3},{3,2},{4,5},{5,4},{6,7},{7,6},{8,9},{9,8},{10,11... | collective-permute-start | bytes 2359304 | tf_op jit(solution)/shard_map/ppermute | solution.py:361
  58.1 29.7 %all-to-all-start.2 = ((bf16[16,64,768]{2,1,0:T(8,128)(2,1)}), bf16[16,64,768]{2,1,0:T(8,128)(2,1)S(1)}, u32[]{:S(2)}, u32[]{:S(2)}) async-start(bf16[16,64,768]{2,1,0:T(8,128)(2,1)} %shard_map.109), calls=%async_computation.2 | async-start | bytes 3145728 | tf_op jit(solution)/shard_map/all_to_all | solution.py:28
  87.9 33.8 %all-to-all-start.3 = ((bf16[16,160,384]{2,1,0:T(8,128)(2,1)}), bf16[16,160,384]{2,1,0:T(8,128)(2,1)S(1)}, u32[]{:S(2)}, u32[]{:S(2)}) async-start(bf16[16,160,384]{2,1,0:T(8,128)(2,1)} %bitcast.33), calls=%async_computation.3 | async-start | bytes 3932160 | tf_op jit(solution)/shard_map/all_to_all | solution.py:28
  95.0 1.4 %collective-permute-start.5 = (f32[2,16,768]{2,1,0:T(8,128)S(1)}, f32[2,16,768]{2,1,0:T(8,128)S(1)}, u32[]{:S(2)}, u32[]{:S(2)}) collective-permute-start(f32[2,16,768]{2,1,0:T(8,128)S(1)} %get-tuple-element.56), channel_id=1, source_target_pairs={{0,1},{1,0},{2,3},{3,2},{4,5},{5,4},{6,7},{7,6},{8,9},{9,8},{10,11... | collective-permute-start | bytes 294920 | tf_op jit(solution)/shard_map/ppermute | solution.py:361
  96.5 6.4 %collective-permute-start.6 = (f32[16,1536]{1,0:T(8,128)S(1)}, f32[16,1536]{1,0:T(8,128)S(1)}, u32[]{:S(2)}, u32[]{:S(2)}) collective-permute-start(f32[16,1536]{1,0:T(8,128)S(1)} %get-tuple-element.54), channel_id=1, source_target_pairs={{0,32},{16,48},{32,0},{48,16},{1,33},{17,49},{33,1},{49,17},{2,34}... | collective-permute-start | bytes 294920 | tf_op jit(solution)/shard_map/ppermute | solution.py:403

commit v6 on v5

--- a/solution.py
+++ b/solution.py
@@ -97,46 +97,26 @@
 
 
 def partial_kernel(c, m0, m1, m2, m3, keep, low, high):
-    block, half = keep.shape
-    rows = m0.shape[1] - 2 * half
-    at = pl.ds(pl.multiple_of(pl.program_id(0) * block, block), block)
+    rows, half = keep.shape
     merged = (m0, m1, m2, m3)
-    value = lax.dot_general(
-        jnp.concatenate([ref[:, at] for ref in merged], axis=0),
-        jnp.concatenate([ref[:, rows:] for ref in merged], axis=0),
-        (((0,), (0,)), ((), ())),
-        preferred_element_type=F32,
-    )
-    left, right = value[:, :half], value[:, half:]
+    rhs = jnp.concatenate([ref[:, rows:] for ref in merged], axis=0)
     first = c[0, 0] == 0
-    keep[...] = jnp.where(first, left, right).astype(BF16)
-    send = jnp.where(first, right, left).astype(BF16)
-    early = pl.program_id(0) < pl.num_programs(0) // 2
-
-    @pl.when(early)
-    def _():
-        low[...] = send
-
-    @pl.when(jnp.logical_not(early))
-    def _():
-        high[...] = send
+    for start in range(0, rows, SPAN):
+        lhs = jnp.concatenate([ref[:, start : start + SPAN] for ref in merged], axis=0)
+        value = lax.dot_general(lhs, rhs, (((0,), (0,)), ((), ())), preferred_element_type=F32)
+        left, right = value[:, :half], value[:, half:]
+        keep[start : start + SPAN] = jnp.where(first, left, right).astype(BF16)
+        out, skip = (low, 0) if start < rows // 2 else (high, rows // 2)
+        out[start - skip : start - skip + SPAN] = jnp.where(first, right, left).astype(BF16)
 
 
 def partial_call(c, merged, rows, cols):
     tokens = merged[0].shape[0]
-    block = SPAN
-    half = rows // block // 2
-    out = (block, cols // 2)
+    vmem = pl.BlockSpec(memory_space=pltpu.VMEM)
     return pl.pallas_call(
         partial_kernel,
-        grid=(rows // block,),
-        in_specs=[pl.BlockSpec(memory_space=pltpu.SMEM)]
-        + [pl.BlockSpec((tokens, rows + cols), lambda i: (0, 0))] * len(merged),
-        out_specs=[
-            pl.BlockSpec(out, lambda i: (i, 0)),
-            pl.BlockSpec(out, lambda i: (jnp.minimum(i, half - 1), 0)),
-            pl.BlockSpec(out, lambda i: (jnp.maximum(i - half, 0), 0)),
-        ],
+        in_specs=[pl.BlockSpec(memory_space=pltpu.SMEM)] + [vmem] * len(merged),
+        out_specs=[vmem] * 3,
         out_shape=[
             jax.ShapeDtypeStruct((rows, cols // 2), BF16),
             jax.ShapeDtypeStruct((rows // 2, cols // 2), BF16),
@@ -147,26 +127,35 @@
     )(c, *merged)
 
 
-def place_kernel(ring, keep, low, high, out):
+def place_kernel(ring, keep, low, high, out, staged, sems):
     places, rows, _ = out.shape
-    got = jnp.where(pl.program_id(0) == 0, low[...], high[...])
-    value = (keep[...].astype(F32) + got.astype(F32)).astype(BF16)
-    rows //= ring
-    for y in range(ring):
-        for place in range(places):
-            at = (y * places + place) * rows
-            out[place, y * rows : (y + 1) * rows] = value[at : at + rows]
+    half = places // 2
+    unit = rows // ring
+    copies = []
+    for part, got in enumerate((low, high)):
+        for y in range(ring):
+            for place in range(half):
+                at = (y * half + place) * unit
+                mine = keep[part * got.shape[0] + at : part * got.shape[0] + at + unit]
+                value = mine.astype(F32) + got[at : at + unit].astype(F32)
+                staged[part * half + place, y * unit : (y + 1) * unit] = value.astype(BF16)
+        span = pl.ds(part * half, half)
+        copies.append(pltpu.make_async_copy(staged.at[span], out.at[span], sems.at[part]))
+        copies[-1].start()
+    for copy in copies:
+        copy.wait()
 
 
 def place_call(keep, got, ring, places, rows):
     cols = keep.shape[1]
-    block = pl.BlockSpec((ring * places * rows, cols), lambda h: (h, 0))
+    shape = (len(got) * places, ring * rows, cols)
+    vmem = pl.BlockSpec(memory_space=pltpu.VMEM)
     return pl.pallas_call(
         functools.partial(place_kernel, ring),
-        grid=(len(got),),
-        in_specs=[block] + [pl.BlockSpec((ring * places * rows, cols), lambda h: (0, 0))] * len(got),
-        out_specs=pl.BlockSpec((places, ring * rows, cols), lambda h: (h, 0, 0)),
-        out_shape=jax.ShapeDtypeStruct((len(got) * places, ring * rows, cols), BF16),
+        in_specs=[vmem] * 3,
+        out_specs=pl.BlockSpec(memory_space=pl.ANY),
+        out_shape=jax.ShapeDtypeStruct(shape, BF16),
+        scratch_shapes=[pltpu.VMEM(shape, BF16), pltpu.SemaphoreType.DMA((len(got),))],
         compiler_params=params(40),
         cost_estimate=cost(0, 6 * keep.size, SMALL),
     )(keep, *got)
@@ -186,7 +175,7 @@
         out[h, t:, HEAD_SIZE:] = total[:, cols]
 
 
-def d_out_call(dimg, weight, cot_txt, adv, txt, img, heads, step=4):
+def d_out_call(dimg, weight, cot_txt, adv, txt, img, heads, step=8):
     rows, model = dimg.shape
     t = cot_txt.shape[0]
     width = step * HEAD_SIZE
@@ -314,32 +303,38 @@
     )(exps, inverse, qk, qk, vd, vd)
 
 
-def unpack_kernel(back, txt, img):
+def unpack_kernel(back, txt, img, txt_rows, img_rows, sems):
+    heads, _, lanes = back.shape
     t = txt.shape[0]
-    for h in range(back.shape[0]):
-        cols = slice(h * HEAD_SIZE, (h + 1) * HEAD_SIZE)
-        txt[:, cols] = back[h, :t]
-        img[:, cols] = back[h, t:]
+    width = heads * HEAD_SIZE
+    copies = []
+    for slot in range(lanes // HEAD_SIZE):
+        source = slice(slot * HEAD_SIZE, (slot + 1) * HEAD_SIZE)
+        for h in range(heads):
+            target = slice(slot * width + h * HEAD_SIZE, slot * width + (h + 1) * HEAD_SIZE)
+            txt_rows[:, target] = back[h, :t, source]
+            img_rows[:, target] = back[h, t:, source]
+        whole = pl.ds(slot * width, width)
+        for near, far in ((txt_rows, txt), (img_rows, img)):
+            copy = pltpu.make_async_copy(near.at[:, whole], far.at[:, whole], sems.at[len(copies)])
+            copy.start()
+            copies.append(copy)
+    for copy in copies:
+        copy.wait()
 
 
 def unpack_call(back, t):
-    heads, tokens, _ = back.shape
-    width = heads * HEAD_SIZE
-    i = tokens - t
+    heads, tokens, lanes = back.shape
+    shapes = [(t, heads * lanes), (tokens - t, heads * lanes)]
     return pl.pallas_call(
         unpack_kernel,
-        grid=(3,),
-        in_specs=[pl.BlockSpec((heads, tokens, HEAD_SIZE), lambda j: (0, 0, j))],
-        out_specs=[
-            pl.BlockSpec((t, width), lambda j: (0, j)),
-            pl.BlockSpec((i, width), lambda j: (0, j)),
-        ],
-        out_shape=[
-            jax.ShapeDtypeStruct((t, 3 * width), BF16),
-            jax.ShapeDtypeStruct((i, 3 * width), BF16),
-        ],
+        in_specs=[pl.BlockSpec(memory_space=pltpu.VMEM)],
+        out_specs=[pl.BlockSpec(memory_space=pl.ANY)] * 2,
+        out_shape=[jax.ShapeDtypeStruct(shape, BF16) for shape in shapes],
+        scratch_shapes=[pltpu.VMEM(shape, BF16) for shape in shapes]
+        + [pltpu.SemaphoreType.DMA((2 * lanes // HEAD_SIZE,))],
         compiler_params=params(24),
-        cost_estimate=cost(0, 12 * tokens * width, SMALL),
+        cost_estimate=cost(0, 2 * back.size, SMALL),
     )(back)
 
 

time: 126 us -> 124 us (0.984)
  Pallas kernels: 57.4 us -> 55.4 us
    pallas_call x3, Pallas kernels: 6.22 us -> 4.64 us  [the longest x1 1.83 us: partial_call(): pl.pallas_call(partial_kernel, in_specs=[pl.BlockSpec(memory_space=pltpu....]
  transfers between devices with their start and end apart: 11 -> 11, of which waited for: 7 -> 7; matrix products, arithmetic and copies ran while one was open for 1% -> 1% of each run, Pallas kernels for 43% -> 42%
where the time goes in v6:
time: 124 us; the launch traced here: 123 us
  Pallas kernels  55.4 us (45%)
  starting transfers between devices  36.8 us (30%)
  waiting for transfers between devices  27.8 us (22%)
  between operations  1.57 us (1%)
    all_to_all x4, starting transfers between devices, exchange(): return lax.all_to_all(array, axes, split_axis=0, concat_axis=0, tiled=True)  27.5 us
    pallas_call x1, Pallas kernels, grads_call(): pl.pallas_call(grads_kernel, grid=(n // BLOCK,), in_specs=[pl.BlockSpec((...  21 us
    all_to_all x4, waiting for transfers between devices, exchange(): return lax.all_to_all(array, axes, split_axis=0, concat_axis=0, tiled=True)  20.5 us
    pallas_call x1, Pallas kernels, exps_call(): pl.pallas_call(exps_kernel, grid=(n // block,), in_specs=[pl.BlockSpec((b...  17.7 us
    pallas_call x1, Pallas kernels, d_out_call(): pl.pallas_call(d_out_kernel, grid=(per,), in_specs=[pl.BlockSpec((rows, m...  8.04 us
    ppermute x3, starting transfers between devices, shift(): lax.ppermute(array, axes, perm)  5.22 us
    ppermute x3, waiting for transfers between devices, swap(): return lax.ppermute(array, 'c', [(0, 1), (1, 0)])  4.05 us
    ppermute x1, starting transfers between devices, per_device(): other = lax.ppermute(other, 'y', [(i, (i + 2) % RING) for i in range(RING)])  3.26 us
  transfers between devices with their start and end apart: 11, of which 7 were waited for; matrix products, arithmetic and copies ran while one was open for 1% of the time, Pallas kernels for 42%

profile of v6, /device:TPU:2, one launch (start us, length us, event | category | flops | bytes accessed | tf_op | source)
XLA Modules:
  0.0 122.6 jit_solution(3690435251847442191)
XLA Ops:
  0.6 2.3 %shard_map.103 = bf16[16,160,256]{2,1,0:T(8,128)(2,1)} custom-call(bf16[32,6144]{1,0:T(8,128)(2,1)} %bitcast.24, bf16[32,6144]{1,0:T(8,128)(2,1)} %bitcast.25, bf16[128,6144]{1,0:T(8,128)(2,1)} %bitcast.30, bf16[128,6144]{1,0:T(8,128)(2,1)} %bitcast.31), custom_call_target="tpu_custom_call" | custom-call | bytes 2621440 | tf_op jit(solution)/shard_map/pallas_call | solution.py:60
  2.9 0.0 copy-start.1
  2.9 0.0 copy-start.2
  2.9 0.0 copy-start.4
  2.9 0.0 copy-start
  3.0 0.0 copy-start.3
  3.0 6.3 %all-to-all-start = ((bf16[16,160,256]{2,1,0:T(8,128)(2,1)}), bf16[16,160,256]{2,1,0:T(8,128)(2,1)}, u32[]{:S(2)}, u32[]{:S(2)}) async-start(bf16[16,160,256]{2,1,0:T(8,128)(2,1)} %shard_map.103), calls=%async_computation | async-start | bytes 2621440 | tf_op jit(solution)/shard_map/all_to_all | solution.py:28
  10.0 0.0 copy-done.1
  10.0 0.0 copy-done.2
  10.0 0.0 copy-done.4
  10.0 1.7 %shard_map.104 = (bf16[128,3072]{1,0:T(8,128)(2,1)S(1)}, bf16[128,2560]{1,0:T(8,128)(2,1)S(1)}, bf16[128,2560]{1,0:T(8,128)(2,1)}, bf16[128,2560]{1,0:T(8,128)(2,1)}, bf16[128,2560]{1,0:T(8,128)(2,1)}) custom-call(bf16[128,3072]{1,0:T(8,128)(2,1)S(1)} %bitcast.27, f32[1,3072]{1,0:T(1,128)S(1)} %copy-done.4, f32[1,1]{1,0:T(1,128)} %bitcast.22.adv, ...), custom_call_target="tpu_custom_call" | custom-call | flops 786432 | bytes 2359296 | tf_op jit(solution)/shard_map/pallas_call | solution.py:89
  11.7 1.6 %collective-permute-start = (bf16[128,2560]{1,0:T(8,128)(2,1)}, bf16[128,2560]{1,0:T(8,128)(2,1)S(1)}, u32[]{:S(2)}, u32[]{:S(2)}) collective-permute-start(bf16[128,2560]{1,0:T(8,128)(2,1)} %get-tuple-element.34), channel_id=1, source_target_pairs={{0,16},{16,32},{32,48},{48,0},{1,17},{17,33},{33,49},{49,1},{2,18}... | collective-permute-start | bytes 1966088 | tf_op jit(solution)/shard_map/ppermute | solution.py:353
  13.3 1.7 %collective-permute-start.1 = (bf16[128,2560]{1,0:T(8,128)(2,1)}, bf16[128,2560]{1,0:T(8,128)(2,1)S(1)}, u32[]{:S(2)}, u32[]{:S(2)}) collective-permute-start(bf16[128,2560]{1,0:T(8,128)(2,1)} %get-tuple-element.35), channel_id=1, source_target_pairs={{0,48},{16,0},{32,16},{48,32},{1,49},{17,1},{33,17},{49,33},{2,50}... | collective-permute-start | bytes 1966088 | tf_op jit(solution)/shard_map/ppermute | solution.py:353
  14.9 2.0 %collective-permute-start.2 = (bf16[128,2560]{1,0:T(8,128)(2,1)}, bf16[128,2560]{1,0:T(8,128)(2,1)S(1)}, u32[]{:S(2)}, u32[]{:S(2)}) collective-permute-start(bf16[128,2560]{1,0:T(8,128)(2,1)} %get-tuple-element.36), channel_id=1, source_target_pairs={{0,32},{16,48},{32,0},{48,16},{1,33},{17,49},{33,1},{49,17},{2,34}... | collective-permute-start | bytes 1966088 | tf_op jit(solution)/shard_map/ppermute | solution.py:353
  16.9 0.0 copy-done
  16.9 0.0 copy-done.3
  16.9 8.0 %shard_map.105 = bf16[16,160,256]{2,1,0:T(8,128)(2,1)} custom-call(bf16[128,3072]{1,0:T(8,128)(2,1)S(1)} %get-tuple-element.30.dimg, bf16[2048,3072]{1,0:T(8,128)(2,1)} %weight.1, bf16[32,2048]{1,0:T(8,128)(2,1)S(1)} %bitcast.29, f32[1,1]{1,0:T(1,128)} %bitcast.23.adv, bf16[32,6144]{1,0:T(8,128)(2,1)S(1)} %bitcast.26, bf16[128,6144]{1,0:T(8,128)(2,1)} %bitcast.32), custom_call_target="tpu_custom_call" | custom-call | flops 1610612736 | bytes 15335424 | tf_op jit(solution)/shard_map/pallas_call | solution.py:183
  24.9 1.6 %all-to-all-done = bf16[16,160,256]{2,1,0:T(8,128)(2,1)} async-done(((bf16[16,160,256]{2,1,0:T(8,128)(2,1)}), bf16[16,160,256]{2,1,0:T(8,128)(2,1)}, u32[]{:S(2)}, u32[]{:S(2)}) %all-to-all-start) | async-done | bytes 1310752 | tf_op jit(solution)/shard_map/all_to_all | solution.py:28
  26.6 6.4 %all-to-all-start.1 = ((bf16[16,160,256]{2,1,0:T(8,128)(2,1)}), bf16[16,160,256]{2,1,0:T(8,128)(2,1)}, u32[]{:S(2)}, u32[]{:S(2)}) async-start(bf16[16,160,256]{2,1,0:T(8,128)(2,1)} %shard_map.105), calls=%async_computation.1 | async-start | bytes 2621440 | tf_op jit(solution)/shard_map/all_to_all | solution.py:28
  32.9 17.7 %shard_map.106 = (bf16[2560,2560]{1,0:T(8,128)(2,1)}, f32[2560,128]{1,0:T(8,128)}) custom-call(bf16[2560,256]{1,0:T(8,128)(2,1)} %bitcast.7.q.k, bf16[2560,256]{1,0:T(8,128)(2,1)} %bitcast.7.q.k), custom_call_target="tpu_custom_call" | custom-call | flops 3355443 | bytes 13107 | tf_op jit(solution)/shard_map/pallas_call | solution.py:238
  50.7 0.0 collective-permute-done.m1
  50.7 0.0 collective-permute-done.1.m2
  50.7 0.0 collective-permute-done.2.m3
  50.7 1.8 %shard_map.108 = (bf16[1024,768]{1,0:T(8,128)(2,1)S(1)}, bf16[512,768]{1,0:T(8,128)(2,1)S(1)}, bf16[512,768]{1,0:T(8,128)(2,1)S(1)}) custom-call(s32[1,1]{1,0:T(1,128)} %bitcast.10.c, bf16[128,2560]{1,0:T(8,128)(2,1)S(1)} %get-tuple-element.40.m0, bf16[128,2560]{1,0:T(8,128)(2,1)S(1)} %collective-permute-done.m1, ...), custom_call_target="tpu_custom_call" | custom-call | flops 1610612 | bytes 5767 | tf_op jit(solution)/shard_map/pallas_call | solution.py:116
  52.5 0.2 collective-permute-start.3
  52.8 0.4 collective-permute-start.4
  53.1 1.8 %collective-permute-done.3.low = bf16[512,768]{1,0:T(8,128)(2,1)S(1)} collective-permute-done((bf16[512,768]{1,0:T(8,128)(2,1)S(1)}, bf16[512,768]{1,0:T(8,128)(2,1)S(1)}, u32[]{:S(2)}, u32[]{:S(2)}) %collective-permute-start.3) | collective-permute-done | bytes 786464 | tf_op jit(solution)/shard_map/ppermute | solution.py:356
  54.9 1.1 collective-permute-done.4.high
  56.0 1.3 %shard_map.109 = bf16[16,64,768]{2,1,0:T(8,128)(2,1)} custom-call(bf16[1024,768]{1,0:T(8,128)(2,1)S(1)} %get-tuple-element.44.keep, bf16[512,768]{1,0:T(8,128)(2,1)S(1)} %collective-permute-done.3.low, bf16[512,768]{1,0:T(8,128)(2,1)S(1)} %collective-permute-done.4.high), custom_call_target="tpu_custom_call" | custom-call | bytes 4718 | tf_op jit(solution)/shard_map/pallas_call | solution.py:153
  57.4 0.0 all-to-all-done.1
  57.4 7.9 %all-to-all-start.2 = ((bf16[16,64,768]{2,1,0:T(8,128)(2,1)}), bf16[16,64,768]{2,1,0:T(8,128)(2,1)S(1)}, u32[]{:S(2)}, u32[]{:S(2)}) async-start(bf16[16,64,768]{2,1,0:T(8,128)(2,1)} %shard_map.109), calls=%async_computation.2 | async-start | bytes 3145728 | tf_op jit(solution)/shard_map/all_to_all | solution.py:28
  65.3 21.0 %shard_map.107 = bf16[2560,384]{1,0:T(8,128)(2,1)} custom-call(bf16[2560,2560]{1,0:T(8,128)(2,1)} %get-tuple-element.32.e, f32[2560,128]{1,0:T(8,128)} %get-tuple-element.38.inv, bf16[2560,256]{1,0:T(8,128)(2,1)} %bitcast.7.q.k, bf16[2560,256]{1,0:T(8,128)(2,1)} %bitcast.7.q.k, bf16[2560,256]{1,0:T(8,128)(2,1)} %bitcast.8.v.d, bf16[2560,256]{1,0:T(8,128)(2,1)} %bitcast.8.v.d), custom_call_target="tpu_custom_call" | custom-call | flops 13421772 | bytes 13107 | tf_op jit(solution)/shard_map/pallas_call | solution.py:294
  86.3 0.8 all-to-all-done.2
  87.1 6.9 %all-to-all-start.3 = ((bf16[16,160,384]{2,1,0:T(8,128)(2,1)}), bf16[16,160,384]{2,1,0:T(8,128)(2,1)S(1)}, u32[]{:S(2)}, u32[]{:S(2)}) async-start(bf16[16,160,384]{2,1,0:T(8,128)(2,1)} %bitcast.33), calls=%async_computation.3 | async-start | bytes 3932160 | tf_op jit(solution)/shard_map/all_to_all | solution.py:28
  94.0 0.2 convert_reduce_fusion
  94.3 0.2 collective-permute-start.5
  94.5 1.2 collective-permute-done.5
  95.7 3.3 %collective-permute-start.6 = (f32[16,1536]{1,0:T(8,128)S(1)}, f32[16,1536]{1,0:T(8,128)S(1)}, u32[]{:S(2)}, u32[]{:S(2)}) collective-permute-start(f32[16,1536]{1,0:T(8,128)S(1)} %get-tuple-element.54), channel_id=1, source_target_pairs={{0,32},{16,48},{32,0},{48,16},{1,33},{17,49},{33,1},{49,17},{2,34}... | collective-permute-start | bytes 294920 | tf_op jit(solution)/shard_map/ppermute | solution.py:398
  99.0 3.2 %collective-permute-done.6 = f32[16,1536]{1,0:T(8,128)S(1)} collective-permute-done((f32[16,1536]{1,0:T(8,128)S(1)}, f32[16,1536]{1,0:T(8,128)S(1)}, u32[]{:S(2)}, u32[]{:S(2)}) %collective-permute-start.6) | collective-permute-done | bytes 98336 | tf_op jit(solution)/shard_map/ppermute | solution.py:398
  102.2 0.7 maximum_select_fusion.1
  102.8 18.1 %all-to-all-done.3.back = bf16[16,160,384]{2,1,0:T(8,128)(2,1)S(1)} async-done(((bf16[16,160,384]{2,1,0:T(8,128)(2,1)}), bf16[16,160,384]{2,1,0:T(8,128)(2,1)S(1)}, u32[]{:S(2)}, u32[]{:S(2)}) %all-to-all-start.3) | async-done | bytes 1966112 | tf_op jit(solution)/shard_map/all_to_all | solution.py:28
  120.9 1.5 %shard_map.110 = (bf16[32,6144]{1,0:T(8,128)(2,1)}, bf16[128,6144]{1,0:T(8,128)(2,1)}) custom-call(bf16[16,160,384]{2,1,0:T(8,128)(2,1)S(1)} %all-to-all-done.3.back), custom_call_target="tpu_custom_call" | custom-call | bytes 1966 | tf_op jit(solution)/shard_map/pallas_call | solution.py:329
  (4 shorter events, 0.1 us)
Async XLA Ops:
  2.9 7.0 %copy-start.1 = (bf16[1,128,3072]{2,1,0:T(8,128)(2,1)S(1)}, bf16[1,128,3072]{2,1,0:T(8,128)(2,1)}, u32[]{:S(2)}) copy-start(bf16[1,128,3072]{2,1,0:T(8,128)(2,1)} %param.12) | copy-start | bytes 2359300
  2.9 7.0 %copy-start.2 = (bf16[1,128,2048]{2,1,0:T(8,128)(2,1)S(1)}, bf16[1,128,2048]{2,1,0:T(8,128)(2,1)}, u32[]{:S(2)}) copy-start(bf16[1,128,2048]{2,1,0:T(8,128)(2,1)} %param.10) | copy-start | bytes 1572868
  2.9 7.1 %copy-start.4 = (f32[1,3072]{1,0:T(1,128)S(1)}, f32[1,3072]{1,0:T(1,128)}, u32[]{:S(2)}) copy-start(f32[1,3072]{1,0:T(1,128)} %gate.1) | copy-start | bytes 36868
  2.9 14.0 %copy-start = (bf16[1,32,6144]{2,1,0:T(8,128)(2,1)S(1)}, bf16[1,32,6144]{2,1,0:T(8,128)(2,1)}, u32[]{:S(2)}) copy-start(bf16[1,32,6144]{2,1,0:T(8,128)(2,1)} %param.8) | copy-start | bytes 1179652
  3.0 14.0 %copy-start.3 = (bf16[1,32,2048]{2,1,0:T(8,128)(2,1)S(1)}, bf16[1,32,2048]{2,1,0:T(8,128)(2,1)}, u32[]{:S(2)}) copy-start(bf16[1,32,2048]{2,1,0:T(8,128)(2,1)} %param.11) | copy-start | bytes 393220
  3.0 23.6 %all-to-all-start = ((bf16[16,160,256]{2,1,0:T(8,128)(2,1)}), bf16[16,160,256]{2,1,0:T(8,128)(2,1)}, u32[]{:S(2)}, u32[]{:S(2)}) async-start(bf16[16,160,256]{2,1,0:T(8,128)(2,1)} %shard_map.103), calls=%async_computation | async-start | bytes 2621440 | tf_op jit(solution)/shard_map/all_to_all | solution.py:28
  11.7 39.0 %collective-permute-start = (bf16[128,2560]{1,0:T(8,128)(2,1)}, bf16[128,2560]{1,0:T(8,128)(2,1)S(1)}, u32[]{:S(2)}, u32[]{:S(2)}) collective-permute-start(bf16[128,2560]{1,0:T(8,128)(2,1)} %get-tuple-element.34), channel_id=1, source_target_pairs={{0,16},{16,32},{32,48},{48,0},{1,17},{17,33},{33,49},{49,1},{2,18}... | collective-permute-start | bytes 1966088 | tf_op jit(solution)/shard_map/ppermute | solution.py:353
  13.3 37.4 %collective-permute-start.1 = (bf16[128,2560]{1,0:T(8,128)(2,1)}, bf16[128,2560]{1,0:T(8,128)(2,1)S(1)}, u32[]{:S(2)}, u32[]{:S(2)}) collective-permute-start(bf16[128,2560]{1,0:T(8,128)(2,1)} %get-tuple-element.35), channel_id=1, source_target_pairs={{0,48},{16,0},{32,16},{48,32},{1,49},{17,1},{33,17},{49,33},{2,50}... | collective-permute-start | bytes 1966088 | tf_op jit(solution)/shard_map/ppermute | solution.py:353
  14.9 35.8 %collective-permute-start.2 = (bf16[128,2560]{1,0:T(8,128)(2,1)}, bf16[128,2560]{1,0:T(8,128)(2,1)S(1)}, u32[]{:S(2)}, u32[]{:S(2)}) collective-permute-start(bf16[128,2560]{1,0:T(8,128)(2,1)} %get-tuple-element.36), channel_id=1, source_target_pairs={{0,32},{16,48},{32,0},{48,16},{1,33},{17,49},{33,1},{49,17},{2,34}... | collective-permute-start | bytes 1966088 | tf_op jit(solution)/shard_map/ppermute | solution.py:353
  26.6 30.8 %all-to-all-start.1 = ((bf16[16,160,256]{2,1,0:T(8,128)(2,1)}), bf16[16,160,256]{2,1,0:T(8,128)(2,1)}, u32[]{:S(2)}, u32[]{:S(2)}) async-start(bf16[16,160,256]{2,1,0:T(8,128)(2,1)} %shard_map.105), calls=%async_computation.1 | async-start | bytes 2621440 | tf_op jit(solution)/shard_map/all_to_all | solution.py:28
  52.5 2.4 %collective-permute-start.3 = (bf16[512,768]{1,0:T(8,128)(2,1)S(1)}, bf16[512,768]{1,0:T(8,128)(2,1)S(1)}, u32[]{:S(2)}, u32[]{:S(2)}) collective-permute-start(bf16[512,768]{1,0:T(8,128)(2,1)S(1)} %get-tuple-element.45), channel_id=1, source_target_pairs={{0,1},{1,0},{2,3},{3,2},{4,5},{5,4},{6,7},{7,6},{8,9},{9,8},{10,11... | collective-permute-start | bytes 2359304 | tf_op jit(solution)/shard_map/ppermute | solution.py:356
  52.8 3.3 %collective-permute-start.4 = (bf16[512,768]{1,0:T(8,128)(2,1)S(1)}, bf16[512,768]{1,0:T(8,128)(2,1)S(1)}, u32[]{:S(2)}, u32[]{:S(2)}) collective-permute-start(bf16[512,768]{1,0:T(8,128)(2,1)S(1)} %get-tuple-element.46), channel_id=1, source_target_pairs={{0,1},{1,0},{2,3},{3,2},{4,5},{5,4},{6,7},{7,6},{8,9},{9,8},{10,11... | collective-permute-start | bytes 2359304 | tf_op jit(solution)/shard_map/ppermute | solution.py:356
  57.4 29.7 %all-to-all-start.2 = ((bf16[16,64,768]{2,1,0:T(8,128)(2,1)}), bf16[16,64,768]{2,1,0:T(8,128)(2,1)S(1)}, u32[]{:S(2)}, u32[]{:S(2)}) async-start(bf16[16,64,768]{2,1,0:T(8,128)(2,1)} %shard_map.109), calls=%async_computation.2 | async-start | bytes 3145728 | tf_op jit(solution)/shard_map/all_to_all | solution.py:28
  87.1 33.8 %all-to-all-start.3 = ((bf16[16,160,384]{2,1,0:T(8,128)(2,1)}), bf16[16,160,384]{2,1,0:T(8,128)(2,1)S(1)}, u32[]{:S(2)}, u32[]{:S(2)}) async-start(bf16[16,160,384]{2,1,0:T(8,128)(2,1)} %bitcast.33), calls=%async_computation.3 | async-start | bytes 3932160 | tf_op jit(solution)/shard_map/all_to_all | solution.py:28
  94.3 1.4 %collective-permute-start.5 = (f32[2,16,768]{2,1,0:T(8,128)S(1)}, f32[2,16,768]{2,1,0:T(8,128)S(1)}, u32[]{:S(2)}, u32[]{:S(2)}) collective-permute-start(f32[2,16,768]{2,1,0:T(8,128)S(1)} %get-tuple-element.56), channel_id=1, source_target_pairs={{0,1},{1,0},{2,3},{3,2},{4,5},{5,4},{6,7},{7,6},{8,9},{9,8},{10,11... | collective-permute-start | bytes 294920 | tf_op jit(solution)/shard_map/ppermute | solution.py:356
  95.7 6.4 %collective-permute-start.6 = (f32[16,1536]{1,0:T(8,128)S(1)}, f32[16,1536]{1,0:T(8,128)S(1)}, u32[]{:S(2)}, u32[]{:S(2)}) collective-permute-start(f32[16,1536]{1,0:T(8,128)S(1)} %get-tuple-element.54), channel_id=1, source_target_pairs={{0,32},{16,48},{32,0},{48,16},{1,33},{17,49},{33,1},{49,17},{2,34}... | collective-permute-start | bytes 294920 | tf_op jit(solution)/shard_map/ppermute | solution.py:398

commit v7 on v6

--- a/solution.py
+++ b/solution.py
@@ -218,7 +218,7 @@
             e_out[rows] = low
             total += fold(low.astype(F32), jnp.sum)
         total = jnp.sum(total, axis=0, keepdims=True)
-        inv_out[...] = jnp.transpose(jnp.broadcast_to(1.0 / total, (HEAD_SIZE, total.shape[1])))
+        inv_out[...] = jnp.broadcast_to(1.0 / total, inv_out.shape)
         return total
 
     total = fill(jnp.max(scores(chunks[0]), axis=0, keepdims=True))
@@ -244,11 +244,11 @@
         ],
         out_specs=[
             pl.BlockSpec((n, block), lambda i: (0, i)),
-            pl.BlockSpec((block, HEAD_SIZE), lambda i: (i, 0)),
+            pl.BlockSpec((8, block), lambda i: (0, i)),
         ],
         out_shape=[
             jax.ShapeDtypeStruct((n, n), BF16),
-            jax.ShapeDtypeStruct((n, HEAD_SIZE), F32),
+            jax.ShapeDtypeStruct((8, n), F32),
         ],
         compiler_params=params(56),
         cost_estimate=cost(2 * n * n * HEAD_SIZE * 2, 2 * n * n, SMALL),
@@ -264,7 +264,7 @@
         dk[...] = jnp.zeros_like(dk)
         dv[...] = jnp.zeros_like(dv)
 
-    inverse = inv[...]
+    inverse = jnp.transpose(jnp.broadcast_to(inv[:1], (HEAD_SIZE, BLOCK)))
     d_low = (d[...].astype(F32) * inverse).astype(BF16)
     centre = jnp.zeros((8, BLOCK), F32)
     for rows in chunks:
@@ -273,7 +273,7 @@
         prob_grads[rows] = part
         centre += fold(probs.astype(F32) * part, jnp.sum)
         dv[rows] += jnp.dot(probs, d_low, preferred_element_type=F32)
-    centre = jnp.sum(centre, axis=0, keepdims=True) * jnp.transpose(inverse)[:1]
+    centre = jnp.sum(centre, axis=0, keepdims=True) * inv[:1]
     dq = jnp.zeros((BLOCK, HEAD_SIZE), F32)
     for rows in chunks:
         score_grad = (e[rows].astype(F32) * (prob_grads[rows] - centre)).astype(BF16)
@@ -294,7 +294,14 @@
     return pl.pallas_call(
         grads_kernel,
         grid=(n // BLOCK,),
-        in_specs=[pl.BlockSpec((n, BLOCK), lambda i: (0, i)), block(0), block(0), whole(1), whole(0), block(1)],
+        in_specs=[
+            pl.BlockSpec((n, BLOCK), lambda i: (0, i)),
+            pl.BlockSpec((8, BLOCK), lambda i: (0, i)),
+            block(0),
+            whole(1),
+            whole(0),
+            block(1),
+        ],
         out_specs=pl.BlockSpec((n, 3 * HEAD_SIZE), lambda i: (0, 0)),
         out_shape=jax.ShapeDtypeStruct((n, 3 * HEAD_SIZE), BF16),
         scratch_shapes=[pltpu.VMEM((n, HEAD_SIZE), F32)] * 2 + [pltpu.VMEM((n, BLOCK), F32)],

time: 124 us -> 122 us (0.984); the launches traced: 123 us -> 122 us
  no operation moved by 1% of the time
where the time goes in v7:
time: 122 us
  Pallas kernels  54.9 us (45%)
  starting transfers between devices  36.8 us (30%)
  waiting for transfers between devices  27.6 us (23%)
  between operations  1.57 us (1%)
    all_to_all x4, starting transfers between devices, exchange(): return lax.all_to_all(array, axes, split_axis=0, concat_axis=0, tiled=True)  27.5 us
    pallas_call x1, Pallas kernels, grads_call(): pl.pallas_call(grads_kernel, grid=(n // BLOCK,), in_specs=[pl.BlockSpec((...  21.2 us
    all_to_all x4, waiting for transfers between devices, exchange(): return lax.all_to_all(array, axes, split_axis=0, concat_axis=0, tiled=True)  20.4 us
    pallas_call x1, Pallas kernels, exps_call(): pl.pallas_call(exps_kernel, grid=(n // block,), in_specs=[pl.BlockSpec((b...  17 us
    pallas_call x1, Pallas kernels, d_out_call(): pl.pallas_call(d_out_kernel, grid=(per,), in_specs=[pl.BlockSpec((rows, m...  8.04 us
    ppermute x3, starting transfers between devices, shift(): lax.ppermute(array, axes, perm)  5.22 us
    ppermute x3, waiting for transfers between devices, swap(): return lax.ppermute(array, 'c', [(0, 1), (1, 0)])  4.05 us
    ppermute x1, starting transfers between devices, per_device(): other = lax.ppermute(other, 'y', [(i, (i + 2) % RING) for i in range(RING)])  3.28 us
  transfers between devices with their start and end apart: 11, of which 7 were waited for; matrix products, arithmetic and copies ran while one was open for 1% of the time, Pallas kernels for 42%

profile of v7, /device:TPU:2, one launch (start us, length us, event | category | flops | bytes accessed | tf_op | source)
XLA Modules:
  0.0 121.9 jit_solution(2493225516931270264)
XLA Ops:
  0.6 2.3 %shard_map.103 = bf16[16,160,256]{2,1,0:T(8,128)(2,1)} custom-call(bf16[32,6144]{1,0:T(8,128)(2,1)} %bitcast.24, bf16[32,6144]{1,0:T(8,128)(2,1)} %bitcast.25, bf16[128,6144]{1,0:T(8,128)(2,1)} %bitcast.30, bf16[128,6144]{1,0:T(8,128)(2,1)} %bitcast.31), custom_call_target="tpu_custom_call" | custom-call | bytes 2621440 | tf_op jit(solution)/shard_map/pallas_call | solution.py:60
  2.9 0.0 copy-start.1
  2.9 0.0 copy-start.2
  2.9 0.0 copy-start.4
  2.9 0.0 copy-start
  3.0 0.0 copy-start.3
  3.0 6.3 %all-to-all-start = ((bf16[16,160,256]{2,1,0:T(8,128)(2,1)}), bf16[16,160,256]{2,1,0:T(8,128)(2,1)}, u32[]{:S(2)}, u32[]{:S(2)}) async-start(bf16[16,160,256]{2,1,0:T(8,128)(2,1)} %shard_map.103), calls=%async_computation | async-start | bytes 2621440 | tf_op jit(solution)/shard_map/all_to_all | solution.py:28
  10.0 0.0 copy-done.1
  10.0 0.0 copy-done.2
  10.0 0.0 copy-done.4
  10.0 1.7 %shard_map.104 = (bf16[128,3072]{1,0:T(8,128)(2,1)S(1)}, bf16[128,2560]{1,0:T(8,128)(2,1)S(1)}, bf16[128,2560]{1,0:T(8,128)(2,1)}, bf16[128,2560]{1,0:T(8,128)(2,1)}, bf16[128,2560]{1,0:T(8,128)(2,1)}) custom-call(bf16[128,3072]{1,0:T(8,128)(2,1)S(1)} %bitcast.27, f32[1,3072]{1,0:T(1,128)S(1)} %copy-done.4, f32[1,1]{1,0:T(1,128)} %bitcast.22.adv, ...), custom_call_target="tpu_custom_call" | custom-call | flops 786432 | bytes 2359296 | tf_op jit(solution)/shard_map/pallas_call | solution.py:89
  11.7 1.6 %collective-permute-start = (bf16[128,2560]{1,0:T(8,128)(2,1)}, bf16[128,2560]{1,0:T(8,128)(2,1)S(1)}, u32[]{:S(2)}, u32[]{:S(2)}) collective-permute-start(bf16[128,2560]{1,0:T(8,128)(2,1)} %get-tuple-element.34), channel_id=1, source_target_pairs={{0,16},{16,32},{32,48},{48,0},{1,17},{17,33},{33,49},{49,1},{2,18}... | collective-permute-start | bytes 1966088 | tf_op jit(solution)/shard_map/ppermute | solution.py:360
  13.3 1.7 %collective-permute-start.1 = (bf16[128,2560]{1,0:T(8,128)(2,1)}, bf16[128,2560]{1,0:T(8,128)(2,1)S(1)}, u32[]{:S(2)}, u32[]{:S(2)}) collective-permute-start(bf16[128,2560]{1,0:T(8,128)(2,1)} %get-tuple-element.35), channel_id=1, source_target_pairs={{0,48},{16,0},{32,16},{48,32},{1,49},{17,1},{33,17},{49,33},{2,50}... | collective-permute-start | bytes 1966088 | tf_op jit(solution)/shard_map/ppermute | solution.py:360
  14.9 2.0 %collective-permute-start.2 = (bf16[128,2560]{1,0:T(8,128)(2,1)}, bf16[128,2560]{1,0:T(8,128)(2,1)S(1)}, u32[]{:S(2)}, u32[]{:S(2)}) collective-permute-start(bf16[128,2560]{1,0:T(8,128)(2,1)} %get-tuple-element.36), channel_id=1, source_target_pairs={{0,32},{16,48},{32,0},{48,16},{1,33},{17,49},{33,1},{49,17},{2,34}... | collective-permute-start | bytes 1966088 | tf_op jit(solution)/shard_map/ppermute | solution.py:360
  16.9 0.0 copy-done
  16.9 0.0 copy-done.3
  16.9 8.0 %shard_map.105 = bf16[16,160,256]{2,1,0:T(8,128)(2,1)} custom-call(bf16[128,3072]{1,0:T(8,128)(2,1)S(1)} %get-tuple-element.30.dimg, bf16[2048,3072]{1,0:T(8,128)(2,1)} %weight.1, bf16[32,2048]{1,0:T(8,128)(2,1)S(1)} %bitcast.29, f32[1,1]{1,0:T(1,128)} %bitcast.23.adv, bf16[32,6144]{1,0:T(8,128)(2,1)S(1)} %bitcast.26, bf16[128,6144]{1,0:T(8,128)(2,1)} %bitcast.32), custom_call_target="tpu_custom_call" | custom-call | flops 1610612736 | bytes 15335424 | tf_op jit(solution)/shard_map/pallas_call | solution.py:183
  24.9 1.6 %all-to-all-done = bf16[16,160,256]{2,1,0:T(8,128)(2,1)} async-done(((bf16[16,160,256]{2,1,0:T(8,128)(2,1)}), bf16[16,160,256]{2,1,0:T(8,128)(2,1)}, u32[]{:S(2)}, u32[]{:S(2)}) %all-to-all-start) | async-done | bytes 1310752 | tf_op jit(solution)/shard_map/all_to_all | solution.py:28
  26.6 6.4 %all-to-all-start.1 = ((bf16[16,160,256]{2,1,0:T(8,128)(2,1)}), bf16[16,160,256]{2,1,0:T(8,128)(2,1)}, u32[]{:S(2)}, u32[]{:S(2)}) async-start(bf16[16,160,256]{2,1,0:T(8,128)(2,1)} %shard_map.105), calls=%async_computation.1 | async-start | bytes 2621440 | tf_op jit(solution)/shard_map/all_to_all | solution.py:28
  32.9 17.0 %shard_map.106 = (bf16[2560,2560]{1,0:T(8,128)(2,1)}, f32[8,2560]{1,0:T(8,128)}) custom-call(bf16[2560,256]{1,0:T(8,128)(2,1)} %bitcast.7.q.k, bf16[2560,256]{1,0:T(8,128)(2,1)} %bitcast.7.q.k), custom_call_target="tpu_custom_call" | custom-call | flops 3355443 | bytes 13107 | tf_op jit(solution)/shard_map/pallas_call | solution.py:238
  50.0 0.0 collective-permute-done.m1
  50.0 0.0 collective-permute-done.1.m2
  50.0 0.0 collective-permute-done.2.m3
  50.0 1.8 %shard_map.108 = (bf16[1024,768]{1,0:T(8,128)(2,1)S(1)}, bf16[512,768]{1,0:T(8,128)(2,1)S(1)}, bf16[512,768]{1,0:T(8,128)(2,1)S(1)}) custom-call(s32[1,1]{1,0:T(1,128)} %bitcast.10.c, bf16[128,2560]{1,0:T(8,128)(2,1)S(1)} %get-tuple-element.40.m0, bf16[128,2560]{1,0:T(8,128)(2,1)S(1)} %collective-permute-done.m1, ...), custom_call_target="tpu_custom_call" | custom-call | flops 1610612 | bytes 5767 | tf_op jit(solution)/shard_map/pallas_call | solution.py:116
  51.8 0.2 collective-permute-start.3
  52.0 0.4 collective-permute-start.4
  52.4 1.8 %collective-permute-done.3.low = bf16[512,768]{1,0:T(8,128)(2,1)S(1)} collective-permute-done((bf16[512,768]{1,0:T(8,128)(2,1)S(1)}, bf16[512,768]{1,0:T(8,128)(2,1)S(1)}, u32[]{:S(2)}, u32[]{:S(2)}) %collective-permute-start.3) | collective-permute-done | bytes 786464 | tf_op jit(solution)/shard_map/ppermute | solution.py:363
  54.2 1.1 collective-permute-done.4.high
  55.3 1.3 %shard_map.109 = bf16[16,64,768]{2,1,0:T(8,128)(2,1)} custom-call(bf16[1024,768]{1,0:T(8,128)(2,1)S(1)} %get-tuple-element.44.keep, bf16[512,768]{1,0:T(8,128)(2,1)S(1)} %collective-permute-done.3.low, bf16[512,768]{1,0:T(8,128)(2,1)S(1)} %collective-permute-done.4.high), custom_call_target="tpu_custom_call" | custom-call | bytes 4718 | tf_op jit(solution)/shard_map/pallas_call | solution.py:153
  56.6 0.0 all-to-all-done.1
  56.7 7.9 %all-to-all-start.2 = ((bf16[16,64,768]{2,1,0:T(8,128)(2,1)}), bf16[16,64,768]{2,1,0:T(8,128)(2,1)S(1)}, u32[]{:S(2)}, u32[]{:S(2)}) async-start(bf16[16,64,768]{2,1,0:T(8,128)(2,1)} %shard_map.109), calls=%async_computation.2 | async-start | bytes 3145728 | tf_op jit(solution)/shard_map/all_to_all | solution.py:28
  64.6 21.2 %shard_map.107 = bf16[2560,384]{1,0:T(8,128)(2,1)} custom-call(bf16[2560,2560]{1,0:T(8,128)(2,1)} %get-tuple-element.32.e, f32[8,2560]{1,0:T(8,128)} %get-tuple-element.38.inv, bf16[2560,256]{1,0:T(8,128)(2,1)} %bitcast.7.q.k, bf16[2560,256]{1,0:T(8,128)(2,1)} %bitcast.7.q.k, bf16[2560,256]{1,0:T(8,128)(2,1)} %bitcast.8.v.d, bf16[2560,256]{1,0:T(8,128)(2,1)} %bitcast.8.v.d), custom_call_target="tpu_custom_call" | custom-call | flops 13421772 | bytes 13107 | tf_op jit(solution)/shard_map/pallas_call | solution.py:294
  85.8 0.6 all-to-all-done.2
  86.4 6.9 %all-to-all-start.3 = ((bf16[16,160,384]{2,1,0:T(8,128)(2,1)}), bf16[16,160,384]{2,1,0:T(8,128)(2,1)S(1)}, u32[]{:S(2)}, u32[]{:S(2)}) async-start(bf16[16,160,384]{2,1,0:T(8,128)(2,1)} %bitcast.33), calls=%async_computation.3 | async-start | bytes 3932160 | tf_op jit(solution)/shard_map/all_to_all | solution.py:28
  93.3 0.2 convert_reduce_fusion
  93.6 0.2 collective-permute-start.5
  93.8 1.2 collective-permute-done.5
  95.0 3.3 %collective-permute-start.6 = (f32[16,1536]{1,0:T(8,128)S(1)}, f32[16,1536]{1,0:T(8,128)S(1)}, u32[]{:S(2)}, u32[]{:S(2)}) collective-permute-start(f32[16,1536]{1,0:T(8,128)S(1)} %get-tuple-element.54), channel_id=1, source_target_pairs={{0,32},{16,48},{32,0},{48,16},{1,33},{17,49},{33,1},{49,17},{2,34}... | collective-permute-start | bytes 294920 | tf_op jit(solution)/shard_map/ppermute | solution.py:405
  98.3 3.2 %collective-permute-done.6 = f32[16,1536]{1,0:T(8,128)S(1)} collective-permute-done((f32[16,1536]{1,0:T(8,128)S(1)}, f32[16,1536]{1,0:T(8,128)S(1)}, u32[]{:S(2)}, u32[]{:S(2)}) %collective-permute-start.6) | collective-permute-done | bytes 98336 | tf_op jit(solution)/shard_map/ppermute | solution.py:405
  101.4 0.7 maximum_select_fusion.1
  102.1 18.1 %all-to-all-done.3.back = bf16[16,160,384]{2,1,0:T(8,128)(2,1)S(1)} async-done(((bf16[16,160,384]{2,1,0:T(8,128)(2,1)}), bf16[16,160,384]{2,1,0:T(8,128)(2,1)S(1)}, u32[]{:S(2)}, u32[]{:S(2)}) %all-to-all-start.3) | async-done | bytes 1966112 | tf_op jit(solution)/shard_map/all_to_all | solution.py:28
  120.2 1.5 %shard_map.110 = (bf16[32,6144]{1,0:T(8,128)(2,1)}, bf16[128,6144]{1,0:T(8,128)(2,1)}) custom-call(bf16[16,160,384]{2,1,0:T(8,128)(2,1)S(1)} %all-to-all-done.3.back), custom_call_target="tpu_custom_call" | custom-call | bytes 1966 | tf_op jit(solution)/shard_map/pallas_call | solution.py:336
  (4 shorter events, 0.1 us)
Async XLA Ops:
  2.9 7.0 %copy-start.1 = (bf16[1,128,3072]{2,1,0:T(8,128)(2,1)S(1)}, bf16[1,128,3072]{2,1,0:T(8,128)(2,1)}, u32[]{:S(2)}) copy-start(bf16[1,128,3072]{2,1,0:T(8,128)(2,1)} %param.12) | copy-start | bytes 2359300
  2.9 7.0 %copy-start.2 = (bf16[1,128,2048]{2,1,0:T(8,128)(2,1)S(1)}, bf16[1,128,2048]{2,1,0:T(8,128)(2,1)}, u32[]{:S(2)}) copy-start(bf16[1,128,2048]{2,1,0:T(8,128)(2,1)} %param.10) | copy-start | bytes 1572868
  2.9 7.1 %copy-start.4 = (f32[1,3072]{1,0:T(1,128)S(1)}, f32[1,3072]{1,0:T(1,128)}, u32[]{:S(2)}) copy-start(f32[1,3072]{1,0:T(1,128)} %gate.1) | copy-start | bytes 36868
  2.9 14.0 %copy-start = (bf16[1,32,6144]{2,1,0:T(8,128)(2,1)S(1)}, bf16[1,32,6144]{2,1,0:T(8,128)(2,1)}, u32[]{:S(2)}) copy-start(bf16[1,32,6144]{2,1,0:T(8,128)(2,1)} %param.8) | copy-start | bytes 1179652
  3.0 13.9 %copy-start.3 = (bf16[1,32,2048]{2,1,0:T(8,128)(2,1)S(1)}, bf16[1,32,2048]{2,1,0:T(8,128)(2,1)}, u32[]{:S(2)}) copy-start(bf16[1,32,2048]{2,1,0:T(8,128)(2,1)} %param.11) | copy-start | bytes 393220
  3.0 23.6 %all-to-all-start = ((bf16[16,160,256]{2,1,0:T(8,128)(2,1)}), bf16[16,160,256]{2,1,0:T(8,128)(2,1)}, u32[]{:S(2)}, u32[]{:S(2)}) async-start(bf16[16,160,256]{2,1,0:T(8,128)(2,1)} %shard_map.103), calls=%async_computation | async-start | bytes 2621440 | tf_op jit(solution)/shard_map/all_to_all | solution.py:28
  11.7 38.3 %collective-permute-start = (bf16[128,2560]{1,0:T(8,128)(2,1)}, bf16[128,2560]{1,0:T(8,128)(2,1)S(1)}, u32[]{:S(2)}, u32[]{:S(2)}) collective-permute-start(bf16[128,2560]{1,0:T(8,128)(2,1)} %get-tuple-element.34), channel_id=1, source_target_pairs={{0,16},{16,32},{32,48},{48,0},{1,17},{17,33},{33,49},{49,1},{2,18}... | collective-permute-start | bytes 1966088 | tf_op jit(solution)/shard_map/ppermute | solution.py:360
  13.3 36.7 %collective-permute-start.1 = (bf16[128,2560]{1,0:T(8,128)(2,1)}, bf16[128,2560]{1,0:T(8,128)(2,1)S(1)}, u32[]{:S(2)}, u32[]{:S(2)}) collective-permute-start(bf16[128,2560]{1,0:T(8,128)(2,1)} %get-tuple-element.35), channel_id=1, source_target_pairs={{0,48},{16,0},{32,16},{48,32},{1,49},{17,1},{33,17},{49,33},{2,50}... | collective-permute-start | bytes 1966088 | tf_op jit(solution)/shard_map/ppermute | solution.py:360
  14.9 35.1 %collective-permute-start.2 = (bf16[128,2560]{1,0:T(8,128)(2,1)}, bf16[128,2560]{1,0:T(8,128)(2,1)S(1)}, u32[]{:S(2)}, u32[]{:S(2)}) collective-permute-start(bf16[128,2560]{1,0:T(8,128)(2,1)} %get-tuple-element.36), channel_id=1, source_target_pairs={{0,32},{16,48},{32,0},{48,16},{1,33},{17,49},{33,1},{49,17},{2,34}... | collective-permute-start | bytes 1966088 | tf_op jit(solution)/shard_map/ppermute | solution.py:360
  26.6 30.1 %all-to-all-start.1 = ((bf16[16,160,256]{2,1,0:T(8,128)(2,1)}), bf16[16,160,256]{2,1,0:T(8,128)(2,1)}, u32[]{:S(2)}, u32[]{:S(2)}) async-start(bf16[16,160,256]{2,1,0:T(8,128)(2,1)} %shard_map.105), calls=%async_computation.1 | async-start | bytes 2621440 | tf_op jit(solution)/shard_map/all_to_all | solution.py:28
  51.8 2.4 %collective-permute-start.3 = (bf16[512,768]{1,0:T(8,128)(2,1)S(1)}, bf16[512,768]{1,0:T(8,128)(2,1)S(1)}, u32[]{:S(2)}, u32[]{:S(2)}) collective-permute-start(bf16[512,768]{1,0:T(8,128)(2,1)S(1)} %get-tuple-element.45), channel_id=1, source_target_pairs={{0,1},{1,0},{2,3},{3,2},{4,5},{5,4},{6,7},{7,6},{8,9},{9,8},{10,11... | collective-permute-start | bytes 2359304 | tf_op jit(solution)/shard_map/ppermute | solution.py:363
  52.0 3.3 %collective-permute-start.4 = (bf16[512,768]{1,0:T(8,128)(2,1)S(1)}, bf16[512,768]{1,0:T(8,128)(2,1)S(1)}, u32[]{:S(2)}, u32[]{:S(2)}) collective-permute-start(bf16[512,768]{1,0:T(8,128)(2,1)S(1)} %get-tuple-element.46), channel_id=1, source_target_pairs={{0,1},{1,0},{2,3},{3,2},{4,5},{5,4},{6,7},{7,6},{8,9},{9,8},{10,11... | collective-permute-start | bytes 2359304 | tf_op jit(solution)/shard_map/ppermute | solution.py:363
  56.7 29.7 %all-to-all-start.2 = ((bf16[16,64,768]{2,1,0:T(8,128)(2,1)}), bf16[16,64,768]{2,1,0:T(8,128)(2,1)S(1)}, u32[]{:S(2)}, u32[]{:S(2)}) async-start(bf16[16,64,768]{2,1,0:T(8,128)(2,1)} %shard_map.109), calls=%async_computation.2 | async-start | bytes 3145728 | tf_op jit(solution)/shard_map/all_to_all | solution.py:28
  86.4 33.8 %all-to-all-start.3 = ((bf16[16,160,384]{2,1,0:T(8,128)(2,1)}), bf16[16,160,384]{2,1,0:T(8,128)(2,1)S(1)}, u32[]{:S(2)}, u32[]{:S(2)}) async-start(bf16[16,160,384]{2,1,0:T(8,128)(2,1)} %bitcast.33), calls=%async_computation.3 | async-start | bytes 3932160 | tf_op jit(solution)/shard_map/all_to_all | solution.py:28
  93.6 1.4 %collective-permute-start.5 = (f32[2,16,768]{2,1,0:T(8,128)S(1)}, f32[2,16,768]{2,1,0:T(8,128)S(1)}, u32[]{:S(2)}, u32[]{:S(2)}) collective-permute-start(f32[2,16,768]{2,1,0:T(8,128)S(1)} %get-tuple-element.56), channel_id=1, source_target_pairs={{0,1},{1,0},{2,3},{3,2},{4,5},{5,4},{6,7},{7,6},{8,9},{9,8},{10,11... | collective-permute-start | bytes 294920 | tf_op jit(solution)/shard_map/ppermute | solution.py:363
  95.0 6.4 %collective-permute-start.6 = (f32[16,1536]{1,0:T(8,128)S(1)}, f32[16,1536]{1,0:T(8,128)S(1)}, u32[]{:S(2)}, u32[]{:S(2)}) collective-permute-start(f32[16,1536]{1,0:T(8,128)S(1)} %get-tuple-element.54), channel_id=1, source_target_pairs={{0,32},{16,48},{32,0},{48,16},{1,33},{17,49},{33,1},{49,17},{2,34}... | collective-permute-start | bytes 294920 | tf_op jit(solution)/shard_map/ppermute | solution.py:405

commit v8 on v7

--- a/solution.py
+++ b/solution.py
@@ -12,6 +12,7 @@
 LOG2E = 1.4426950408889634
 BLOCK = 512
 CHUNK = 256
+WIDE = 1280
 SMALL = 1000
 SAFE = 2.0**40
 SEQ = ("zl", "x", "c")
@@ -204,8 +205,28 @@
     return combine(array.reshape(-1, 8, array.shape[1]), axis=0)
 
 
-def exps_kernel(q, k, e_out, inv_out):
+def block_copies(array, buffer, sems, step, back):
+    slot = lax.rem(step, 2)
+    columns = pl.ds(pl.multiple_of(step * WIDE, WIDE), WIDE)
+    copies = []
+    for chunk in range(array.shape[0] // CHUNK):
+        rows = pl.ds(chunk * CHUNK, CHUNK)
+        far, near = array.at[rows, columns], buffer.at[slot, rows]
+        source, target = (near, far) if back else (far, near)
+        copies.append(pltpu.make_async_copy(source, target, sems.at[slot, chunk]))
+    return copies
+
+
+def exps_kernel(q, k, e_out, inv_out, buffer, sems):
+    step, last = pl.program_id(0), pl.num_programs(0) - 1
+    slot = lax.rem(step, 2)
     chunks = [slice(at, at + CHUNK) for at in range(0, k.shape[0], CHUNK)]
+    copies = block_copies(e_out, buffer, sems, step, True)
+
+    @pl.when(step >= 2)
+    def _():
+        for copy in block_copies(e_out, buffer, sems, step - 2, True):
+            copy.wait()
 
     def scores(rows):
         return lax.dot_general(k[rows], q[...], (((1,), (1,)), ((), ())), preferred_element_type=F32)
@@ -213,9 +234,10 @@
     def fill(top):
         total = jnp.zeros((8, top.shape[1]), F32)
         top = top * (SCALE * LOG2E)
-        for rows in chunks:
+        for rows, copy in zip(chunks, copies):
             low = jnp.exp2(scores(rows) * (SCALE * LOG2E) - top).astype(BF16)
-            e_out[rows] = low
+            buffer[slot, rows] = low
+            copy.start()
             total += fold(low.astype(F32), jnp.sum)
         total = jnp.sum(total, axis=0, keepdims=True)
         inv_out[...] = jnp.broadcast_to(1.0 / total, inv_out.shape)
@@ -226,30 +248,36 @@
     @pl.when(jnp.logical_not(jnp.max(total) < SAFE))
     def _():
         top = None
-        for rows in chunks:
+        for rows, copy in zip(chunks, copies):
+            copy.wait()
             part = fold(scores(rows), jnp.max)
             top = part if top is None else jnp.maximum(top, part)
         fill(jnp.max(top, axis=0, keepdims=True))
 
+    @pl.when(step == last)
+    def _():
+        for copy in block_copies(e_out, buffer, sems, step - 1, True) + copies:
+            copy.wait()
+
 
 def exps_call(qk):
     n = qk.shape[0]
-    block = BLOCK
     return pl.pallas_call(
         exps_kernel,
-        grid=(n // block,),
+        grid=(n // WIDE,),
         in_specs=[
-            pl.BlockSpec((block, HEAD_SIZE), lambda i: (i, 0)),
+            pl.BlockSpec((WIDE, HEAD_SIZE), lambda i: (i, 0)),
             pl.BlockSpec((n, HEAD_SIZE), lambda i: (0, 1)),
         ],
         out_specs=[
-            pl.BlockSpec((n, block), lambda i: (0, i)),
-            pl.BlockSpec((8, block), lambda i: (0, i)),
+            pl.BlockSpec(memory_space=pl.ANY),
+            pl.BlockSpec((8, WIDE), lambda i: (0, i)),
         ],
         out_shape=[
             jax.ShapeDtypeStruct((n, n), BF16),
             jax.ShapeDtypeStruct((8, n), F32),
         ],
+        scratch_shapes=[pltpu.VMEM((2, n, WIDE), BF16), pltpu.SemaphoreType.DMA((2, n // CHUNK))],
         compiler_params=params(56),
         cost_estimate=cost(2 * n * n * HEAD_SIZE * 2, 2 * n * n, SMALL),
     )(qk, qk)

time: 122 us -> 130 us (1.066)
  Pallas kernels: 54.9 us -> 62.2 us
    pallas_call x1, Pallas kernels: 17 us -> 24.4 us  [exps_call(): pl.pallas_call(exps_kernel, grid=(n // WIDE,), in_specs=[pl.BlockSpec((WI...]
  transfers between devices with their start and end apart: 11 -> 11, of which waited for: 7 -> 7; matrix products, arithmetic and copies ran while one was open for 1% -> 1% of each run, Pallas kernels for 42% -> 45%
where the time goes in v8:
time: 130 us; the launch traced here: 129 us
  Pallas kernels  62.2 us (48%)
  starting transfers between devices  36.8 us (28%)
  waiting for transfers between devices  27.6 us (21%)
  between operations  1.61 us (1%)
    all_to_all x4, starting transfers between devices, exchange(): return lax.all_to_all(array, axes, split_axis=0, concat_axis=0, tiled=True)  27.5 us
    pallas_call x1, Pallas kernels, exps_call(): pl.pallas_call(exps_kernel, grid=(n // WIDE,), in_specs=[pl.BlockSpec((WI...  24.4 us
    pallas_call x1, Pallas kernels, grads_call(): pl.pallas_call(grads_kernel, grid=(n // BLOCK,), in_specs=[pl.BlockSpec((...  21.2 us
    all_to_all x4, waiting for transfers between devices, exchange(): return lax.all_to_all(array, axes, split_axis=0, concat_axis=0, tiled=True)  20.4 us
    pallas_call x1, Pallas kernels, d_out_call(): pl.pallas_call(d_out_kernel, grid=(per,), in_specs=[pl.BlockSpec((rows, m...  8.04 us
    ppermute x3, starting transfers between devices, shift(): lax.ppermute(array, axes, perm)  5.22 us
    ppermute x3, waiting for transfers between devices, swap(): return lax.ppermute(array, 'c', [(0, 1), (1, 0)])  4.05 us
    ppermute x1, starting transfers between devices, per_device(): other = lax.ppermute(other, 'y', [(i, (i + 2) % RING) for i in range(RING)])  3.27 us
  transfers between devices with their start and end apart: 11, of which 7 were waited for; matrix products, arithmetic and copies ran while one was open for 1% of the time, Pallas kernels for 45%

profile of v8, /device:TPU:2, one launch (start us, length us, event | category | flops | bytes accessed | tf_op | source)
XLA Modules:
  0.0 129.3 jit_solution(505138894484166730)
XLA Ops:
  0.6 2.3 %shard_map.103 = bf16[16,160,256]{2,1,0:T(8,128)(2,1)} custom-call(bf16[32,6144]{1,0:T(8,128)(2,1)} %bitcast.24, bf16[32,6144]{1,0:T(8,128)(2,1)} %bitcast.25, bf16[128,6144]{1,0:T(8,128)(2,1)} %bitcast.30, bf16[128,6144]{1,0:T(8,128)(2,1)} %bitcast.31), custom_call_target="tpu_custom_call" | custom-call | bytes 2621440 | tf_op jit(solution)/shard_map/pallas_call | solution.py:61
  2.9 0.0 copy-start.1
  2.9 0.0 copy-start.2
  2.9 0.0 copy-start.4
  2.9 0.0 copy-start
  3.0 0.0 copy-start.3
  3.0 6.3 %all-to-all-start = ((bf16[16,160,256]{2,1,0:T(8,128)(2,1)}), bf16[16,160,256]{2,1,0:T(8,128)(2,1)}, u32[]{:S(2)}, u32[]{:S(2)}) async-start(bf16[16,160,256]{2,1,0:T(8,128)(2,1)} %shard_map.103), calls=%async_computation | async-start | bytes 2621440 | tf_op jit(solution)/shard_map/all_to_all | solution.py:29
  10.0 0.0 copy-done.1
  10.0 0.0 copy-done.2
  10.0 0.0 copy-done.4
  10.0 1.7 %shard_map.104 = (bf16[128,3072]{1,0:T(8,128)(2,1)S(1)}, bf16[128,2560]{1,0:T(8,128)(2,1)S(1)}, bf16[128,2560]{1,0:T(8,128)(2,1)}, bf16[128,2560]{1,0:T(8,128)(2,1)}, bf16[128,2560]{1,0:T(8,128)(2,1)}) custom-call(bf16[128,3072]{1,0:T(8,128)(2,1)S(1)} %bitcast.27, f32[1,3072]{1,0:T(1,128)S(1)} %copy-done.4, f32[1,1]{1,0:T(1,128)} %bitcast.22.adv, ...), custom_call_target="tpu_custom_call" | custom-call | flops 786432 | bytes 2359296 | tf_op jit(solution)/shard_map/pallas_call | solution.py:90
  11.7 1.6 %collective-permute-start = (bf16[128,2560]{1,0:T(8,128)(2,1)}, bf16[128,2560]{1,0:T(8,128)(2,1)S(1)}, u32[]{:S(2)}, u32[]{:S(2)}) collective-permute-start(bf16[128,2560]{1,0:T(8,128)(2,1)} %get-tuple-element.34), channel_id=1, source_target_pairs={{0,16},{16,32},{32,48},{48,0},{1,17},{17,33},{33,49},{49,1},{2,18}... | collective-permute-start | bytes 1966088 | tf_op jit(solution)/shard_map/ppermute | solution.py:388
  13.3 1.7 %collective-permute-start.1 = (bf16[128,2560]{1,0:T(8,128)(2,1)}, bf16[128,2560]{1,0:T(8,128)(2,1)S(1)}, u32[]{:S(2)}, u32[]{:S(2)}) collective-permute-start(bf16[128,2560]{1,0:T(8,128)(2,1)} %get-tuple-element.35), channel_id=1, source_target_pairs={{0,48},{16,0},{32,16},{48,32},{1,49},{17,1},{33,17},{49,33},{2,50}... | collective-permute-start | bytes 1966088 | tf_op jit(solution)/shard_map/ppermute | solution.py:388
  14.9 2.0 %collective-permute-start.2 = (bf16[128,2560]{1,0:T(8,128)(2,1)}, bf16[128,2560]{1,0:T(8,128)(2,1)S(1)}, u32[]{:S(2)}, u32[]{:S(2)}) collective-permute-start(bf16[128,2560]{1,0:T(8,128)(2,1)} %get-tuple-element.36), channel_id=1, source_target_pairs={{0,32},{16,48},{32,0},{48,16},{1,33},{17,49},{33,1},{49,17},{2,34}... | collective-permute-start | bytes 1966088 | tf_op jit(solution)/shard_map/ppermute | solution.py:388
  16.9 0.0 copy-done
  16.9 0.0 copy-done.3
  16.9 8.0 %shard_map.105 = bf16[16,160,256]{2,1,0:T(8,128)(2,1)} custom-call(bf16[128,3072]{1,0:T(8,128)(2,1)S(1)} %get-tuple-element.30.dimg, bf16[2048,3072]{1,0:T(8,128)(2,1)} %weight.1, bf16[32,2048]{1,0:T(8,128)(2,1)S(1)} %bitcast.29, f32[1,1]{1,0:T(1,128)} %bitcast.23.adv, bf16[32,6144]{1,0:T(8,128)(2,1)S(1)} %bitcast.26, bf16[128,6144]{1,0:T(8,128)(2,1)} %bitcast.32), custom_call_target="tpu_custom_call" | custom-call | flops 1610612736 | bytes 15335424 | tf_op jit(solution)/shard_map/pallas_call | solution.py:184
  24.9 1.6 %all-to-all-done = bf16[16,160,256]{2,1,0:T(8,128)(2,1)} async-done(((bf16[16,160,256]{2,1,0:T(8,128)(2,1)}), bf16[16,160,256]{2,1,0:T(8,128)(2,1)}, u32[]{:S(2)}, u32[]{:S(2)}) %all-to-all-start) | async-done | bytes 1310752 | tf_op jit(solution)/shard_map/all_to_all | solution.py:29
  26.6 6.4 %all-to-all-start.1 = ((bf16[16,160,256]{2,1,0:T(8,128)(2,1)}), bf16[16,160,256]{2,1,0:T(8,128)(2,1)}, u32[]{:S(2)}, u32[]{:S(2)}) async-start(bf16[16,160,256]{2,1,0:T(8,128)(2,1)} %shard_map.105), calls=%async_computation.1 | async-start | bytes 2621440 | tf_op jit(solution)/shard_map/all_to_all | solution.py:29
  32.9 24.4 %shard_map.106 = (bf16[2560,2560]{1,0:T(8,128)(2,1)}, f32[8,2560]{1,0:T(8,128)}) custom-call(bf16[2560,256]{1,0:T(8,128)(2,1)} %bitcast.7.q.k, bf16[2560,256]{1,0:T(8,128)(2,1)} %bitcast.7.q.k), custom_call_target="tpu_custom_call" | custom-call | flops 3355443 | bytes 13107 | tf_op jit(solution)/shard_map/pallas_call | solution.py:265
  57.4 0.0 collective-permute-done.m1
  57.4 0.0 collective-permute-done.1.m2
  57.4 0.0 collective-permute-done.2.m3
  57.4 1.8 %shard_map.108 = (bf16[1024,768]{1,0:T(8,128)(2,1)S(1)}, bf16[512,768]{1,0:T(8,128)(2,1)S(1)}, bf16[512,768]{1,0:T(8,128)(2,1)S(1)}) custom-call(s32[1,1]{1,0:T(1,128)} %bitcast.10.c, bf16[128,2560]{1,0:T(8,128)(2,1)S(1)} %get-tuple-element.40.m0, bf16[128,2560]{1,0:T(8,128)(2,1)S(1)} %collective-permute-done.m1, ...), custom_call_target="tpu_custom_call" | custom-call | flops 1610612 | bytes 5767 | tf_op jit(solution)/shard_map/pallas_call | solution.py:117
  59.2 0.2 collective-permute-start.3
  59.4 0.4 collective-permute-start.4
  59.8 1.8 %collective-permute-done.3.low = bf16[512,768]{1,0:T(8,128)(2,1)S(1)} collective-permute-done((bf16[512,768]{1,0:T(8,128)(2,1)S(1)}, bf16[512,768]{1,0:T(8,128)(2,1)S(1)}, u32[]{:S(2)}, u32[]{:S(2)}) %collective-permute-start.3) | collective-permute-done | bytes 786464 | tf_op jit(solution)/shard_map/ppermute | solution.py:391
  61.6 1.1 collective-permute-done.4.high
  62.7 1.3 %shard_map.109 = bf16[16,64,768]{2,1,0:T(8,128)(2,1)} custom-call(bf16[1024,768]{1,0:T(8,128)(2,1)S(1)} %get-tuple-element.44.keep, bf16[512,768]{1,0:T(8,128)(2,1)S(1)} %collective-permute-done.3.low, bf16[512,768]{1,0:T(8,128)(2,1)S(1)} %collective-permute-done.4.high), custom_call_target="tpu_custom_call" | custom-call | bytes 4718 | tf_op jit(solution)/shard_map/pallas_call | solution.py:154
  64.1 0.0 all-to-all-done.1
  64.1 7.9 %all-to-all-start.2 = ((bf16[16,64,768]{2,1,0:T(8,128)(2,1)}), bf16[16,64,768]{2,1,0:T(8,128)(2,1)S(1)}, u32[]{:S(2)}, u32[]{:S(2)}) async-start(bf16[16,64,768]{2,1,0:T(8,128)(2,1)} %shard_map.109), calls=%async_computation.2 | async-start | bytes 3145728 | tf_op jit(solution)/shard_map/all_to_all | solution.py:29
  72.0 21.2 %shard_map.107 = bf16[2560,384]{1,0:T(8,128)(2,1)} custom-call(bf16[2560,2560]{1,0:T(8,128)(2,1)} %get-tuple-element.32.e, f32[8,2560]{1,0:T(8,128)} %get-tuple-element.38.inv, bf16[2560,256]{1,0:T(8,128)(2,1)} %bitcast.7.q.k, bf16[2560,256]{1,0:T(8,128)(2,1)} %bitcast.7.q.k, bf16[2560,256]{1,0:T(8,128)(2,1)} %bitcast.8.v.d, bf16[2560,256]{1,0:T(8,128)(2,1)} %bitcast.8.v.d), custom_call_target="tpu_custom_call" | custom-call | flops 13421772 | bytes 13107 | tf_op jit(solution)/shard_map/pallas_call | solution.py:322
  93.2 0.7 all-to-all-done.2
  93.8 6.9 %all-to-all-start.3 = ((bf16[16,160,384]{2,1,0:T(8,128)(2,1)}), bf16[16,160,384]{2,1,0:T(8,128)(2,1)S(1)}, u32[]{:S(2)}, u32[]{:S(2)}) async-start(bf16[16,160,384]{2,1,0:T(8,128)(2,1)} %bitcast.33), calls=%async_computation.3 | async-start | bytes 3932160 | tf_op jit(solution)/shard_map/all_to_all | solution.py:29
  100.7 0.2 convert_reduce_fusion
  101.0 0.2 collective-permute-start.5
  101.2 1.2 collective-permute-done.5
  102.4 3.3 %collective-permute-start.6 = (f32[16,1536]{1,0:T(8,128)S(1)}, f32[16,1536]{1,0:T(8,128)S(1)}, u32[]{:S(2)}, u32[]{:S(2)}) collective-permute-start(f32[16,1536]{1,0:T(8,128)S(1)} %get-tuple-element.54), channel_id=1, source_target_pairs={{0,32},{16,48},{32,0},{48,16},{1,33},{17,49},{33,1},{49,17},{2,34}... | collective-permute-start | bytes 294920 | tf_op jit(solution)/shard_map/ppermute | solution.py:433
  105.7 3.2 %collective-permute-done.6 = f32[16,1536]{1,0:T(8,128)S(1)} collective-permute-done((f32[16,1536]{1,0:T(8,128)S(1)}, f32[16,1536]{1,0:T(8,128)S(1)}, u32[]{:S(2)}, u32[]{:S(2)}) %collective-permute-start.6) | collective-permute-done | bytes 98336 | tf_op jit(solution)/shard_map/ppermute | solution.py:433
  108.8 0.7 maximum_select_fusion.1
  109.5 18.1 %all-to-all-done.3.back = bf16[16,160,384]{2,1,0:T(8,128)(2,1)S(1)} async-done(((bf16[16,160,384]{2,1,0:T(8,128)(2,1)}), bf16[16,160,384]{2,1,0:T(8,128)(2,1)S(1)}, u32[]{:S(2)}, u32[]{:S(2)}) %all-to-all-start.3) | async-done | bytes 1966112 | tf_op jit(solution)/shard_map/all_to_all | solution.py:29
  127.6 1.5 %shard_map.110 = (bf16[32,6144]{1,0:T(8,128)(2,1)}, bf16[128,6144]{1,0:T(8,128)(2,1)}) custom-call(bf16[16,160,384]{2,1,0:T(8,128)(2,1)S(1)} %all-to-all-done.3.back), custom_call_target="tpu_custom_call" | custom-call | bytes 1966 | tf_op jit(solution)/shard_map/pallas_call | solution.py:364
  (4 shorter events, 0.1 us)
Async XLA Ops:
  2.9 7.0 %copy-start.1 = (bf16[1,128,3072]{2,1,0:T(8,128)(2,1)S(1)}, bf16[1,128,3072]{2,1,0:T(8,128)(2,1)}, u32[]{:S(2)}) copy-start(bf16[1,128,3072]{2,1,0:T(8,128)(2,1)} %param.12) | copy-start | bytes 2359300
  2.9 7.0 %copy-start.2 = (bf16[1,128,2048]{2,1,0:T(8,128)(2,1)S(1)}, bf16[1,128,2048]{2,1,0:T(8,128)(2,1)}, u32[]{:S(2)}) copy-start(bf16[1,128,2048]{2,1,0:T(8,128)(2,1)} %param.10) | copy-start | bytes 1572868
  2.9 7.1 %copy-start.4 = (f32[1,3072]{1,0:T(1,128)S(1)}, f32[1,3072]{1,0:T(1,128)}, u32[]{:S(2)}) copy-start(f32[1,3072]{1,0:T(1,128)} %gate.1) | copy-start | bytes 36868
  2.9 14.0 %copy-start = (bf16[1,32,6144]{2,1,0:T(8,128)(2,1)S(1)}, bf16[1,32,6144]{2,1,0:T(8,128)(2,1)}, u32[]{:S(2)}) copy-start(bf16[1,32,6144]{2,1,0:T(8,128)(2,1)} %param.8) | copy-start | bytes 1179652
  3.0 13.9 %copy-start.3 = (bf16[1,32,2048]{2,1,0:T(8,128)(2,1)S(1)}, bf16[1,32,2048]{2,1,0:T(8,128)(2,1)}, u32[]{:S(2)}) copy-start(bf16[1,32,2048]{2,1,0:T(8,128)(2,1)} %param.11) | copy-start | bytes 393220
  3.0 23.6 %all-to-all-start = ((bf16[16,160,256]{2,1,0:T(8,128)(2,1)}), bf16[16,160,256]{2,1,0:T(8,128)(2,1)}, u32[]{:S(2)}, u32[]{:S(2)}) async-start(bf16[16,160,256]{2,1,0:T(8,128)(2,1)} %shard_map.103), calls=%async_computation | async-start | bytes 2621440 | tf_op jit(solution)/shard_map/all_to_all | solution.py:29
  11.7 45.7 %collective-permute-start = (bf16[128,2560]{1,0:T(8,128)(2,1)}, bf16[128,2560]{1,0:T(8,128)(2,1)S(1)}, u32[]{:S(2)}, u32[]{:S(2)}) collective-permute-start(bf16[128,2560]{1,0:T(8,128)(2,1)} %get-tuple-element.34), channel_id=1, source_target_pairs={{0,16},{16,32},{32,48},{48,0},{1,17},{17,33},{33,49},{49,1},{2,18}... | collective-permute-start | bytes 1966088 | tf_op jit(solution)/shard_map/ppermute | solution.py:388
  13.3 44.1 %collective-permute-start.1 = (bf16[128,2560]{1,0:T(8,128)(2,1)}, bf16[128,2560]{1,0:T(8,128)(2,1)S(1)}, u32[]{:S(2)}, u32[]{:S(2)}) collective-permute-start(bf16[128,2560]{1,0:T(8,128)(2,1)} %get-tuple-element.35), channel_id=1, source_target_pairs={{0,48},{16,0},{32,16},{48,32},{1,49},{17,1},{33,17},{49,33},{2,50}... | collective-permute-start | bytes 1966088 | tf_op jit(solution)/shard_map/ppermute | solution.py:388
  14.9 42.5 %collective-permute-start.2 = (bf16[128,2560]{1,0:T(8,128)(2,1)}, bf16[128,2560]{1,0:T(8,128)(2,1)S(1)}, u32[]{:S(2)}, u32[]{:S(2)}) collective-permute-start(bf16[128,2560]{1,0:T(8,128)(2,1)} %get-tuple-element.36), channel_id=1, source_target_pairs={{0,32},{16,48},{32,0},{48,16},{1,33},{17,49},{33,1},{49,17},{2,34}... | collective-permute-start | bytes 1966088 | tf_op jit(solution)/shard_map/ppermute | solution.py:388
  26.6 37.5 %all-to-all-start.1 = ((bf16[16,160,256]{2,1,0:T(8,128)(2,1)}), bf16[16,160,256]{2,1,0:T(8,128)(2,1)}, u32[]{:S(2)}, u32[]{:S(2)}) async-start(bf16[16,160,256]{2,1,0:T(8,128)(2,1)} %shard_map.105), calls=%async_computation.1 | async-start | bytes 2621440 | tf_op jit(solution)/shard_map/all_to_all | solution.py:29
  59.2 2.4 %collective-permute-start.3 = (bf16[512,768]{1,0:T(8,128)(2,1)S(1)}, bf16[512,768]{1,0:T(8,128)(2,1)S(1)}, u32[]{:S(2)}, u32[]{:S(2)}) collective-permute-start(bf16[512,768]{1,0:T(8,128)(2,1)S(1)} %get-tuple-element.45), channel_id=1, source_target_pairs={{0,1},{1,0},{2,3},{3,2},{4,5},{5,4},{6,7},{7,6},{8,9},{9,8},{10,11... | collective-permute-start | bytes 2359304 | tf_op jit(solution)/shard_map/ppermute | solution.py:391
  59.4 3.3 %collective-permute-start.4 = (bf16[512,768]{1,0:T(8,128)(2,1)S(1)}, bf16[512,768]{1,0:T(8,128)(2,1)S(1)}, u32[]{:S(2)}, u32[]{:S(2)}) collective-permute-start(bf16[512,768]{1,0:T(8,128)(2,1)S(1)} %get-tuple-element.46), channel_id=1, source_target_pairs={{0,1},{1,0},{2,3},{3,2},{4,5},{5,4},{6,7},{7,6},{8,9},{9,8},{10,11... | collective-permute-start | bytes 2359304 | tf_op jit(solution)/shard_map/ppermute | solution.py:391
  64.1 29.7 %all-to-all-start.2 = ((bf16[16,64,768]{2,1,0:T(8,128)(2,1)}), bf16[16,64,768]{2,1,0:T(8,128)(2,1)S(1)}, u32[]{:S(2)}, u32[]{:S(2)}) async-start(bf16[16,64,768]{2,1,0:T(8,128)(2,1)} %shard_map.109), calls=%async_computation.2 | async-start | bytes 3145728 | tf_op jit(solution)/shard_map/all_to_all | solution.py:29
  93.8 33.8 %all-to-all-start.3 = ((bf16[16,160,384]{2,1,0:T(8,128)(2,1)}), bf16[16,160,384]{2,1,0:T(8,128)(2,1)S(1)}, u32[]{:S(2)}, u32[]{:S(2)}) async-start(bf16[16,160,384]{2,1,0:T(8,128)(2,1)} %bitcast.33), calls=%async_computation.3 | async-start | bytes 3932160 | tf_op jit(solution)/shard_map/all_to_all | solution.py:29
  101.0 1.4 %collective-permute-start.5 = (f32[2,16,768]{2,1,0:T(8,128)S(1)}, f32[2,16,768]{2,1,0:T(8,128)S(1)}, u32[]{:S(2)}, u32[]{:S(2)}) collective-permute-start(f32[2,16,768]{2,1,0:T(8,128)S(1)} %get-tuple-element.56), channel_id=1, source_target_pairs={{0,1},{1,0},{2,3},{3,2},{4,5},{5,4},{6,7},{7,6},{8,9},{9,8},{10,11... | collective-permute-start | bytes 294920 | tf_op jit(solution)/shard_map/ppermute | solution.py:391
  102.4 6.4 %collective-permute-start.6 = (f32[16,1536]{1,0:T(8,128)S(1)}, f32[16,1536]{1,0:T(8,128)S(1)}, u32[]{:S(2)}, u32[]{:S(2)}) collective-permute-start(f32[16,1536]{1,0:T(8,128)S(1)} %get-tuple-element.54), channel_id=1, source_target_pairs={{0,32},{16,48},{32,0},{48,16},{1,33},{17,49},{33,1},{49,17},{2,34}... | collective-permute-start | bytes 294920 | tf_op jit(solution)/shard_map/ppermute | solution.py:433
